TPU v7x, 32 devices: a whole 2x2x4 slice. The times are simulated.
32 devices in a mesh: groups: 2 (over y), row: 4 (over x, core), col: 4 (over z).
Axes of the slice: x: 2, y: 2, z: 4, core: 2. Of those that a mesh axis runs over, the one named last changes fastest.
Arguments:
- pair: bfloat16 [1280, 640, 128], P(('groups', 'row'), 'col'), parts along dimension 0, may hold values from -6 to 6
- product: bfloat16 [1280, 640, 128], P(('groups', 'row'), 'col'), parts along dimension 0, may hold values from -6 to 6
- mask: int32 [1280, 640], P(('groups', 'row'), 'col'), parts along dimension 0, may hold values 0 or 1
- grad_out: bfloat16 [1280, 640, 128], P(('groups', 'row'), 'col'), parts along dimension 0, may hold values from -6 to 6
- weights: bfloat16 [6, 128, 128], replicated, may hold values from -0.5 to 0.5
- norms: float32 [4, 128], replicated, may hold values from 0.25 to 1.75
Outputs:
- grad_pair: bfloat16 [1280, 640, 128], P(('groups', 'row'), 'col'), parts along dimension 0
- grad_weights: float32 [12, 128, 128], P('groups'), parts along dimension 0
- norm_vector_gradients: float32 [8, 128], P('groups'), parts along dimension 0
There are 2 independent parts, one for each index of `groups`. A program takes and returns all parts, laid end to end along the dimension named above; an argument that names none is the same for every part. Nothing has to cross between parts.
Inputs may be any that keep to these rules, and one draw needn't show every extreme that they name: `mask`: 0 marks an invalid pair, 1 a valid one.
All inputs are finite; a program needn't handle non-finite values. No bound on the sum of `mask` on one device may be relied on, other than what follows from the above.
Results may differ from a plain program's by a relative error of at most 0.01.
Values may be sent and summed in bfloat16 or wider, within the bound.
No kernel may reach another device: no remote copies, remote signals or barrier semaphores. Data moves between devices by JAX's collectives and lax.ppermute only.
A program may use at most 448 MiB of HBM per device.

v0:
```python
import jax
import jax.numpy as jnp
from jax import lax
from jax.sharding import PartitionSpec as P

eps = 1e-05


def layer_normalize(v):
    mean = jnp.mean(v, axis=-1, keepdims=True)
    cent = v - mean
    inv = lax.rsqrt(jnp.mean(cent * cent, axis=-1, keepdims=True) + eps)
    return (cent * inv, inv)


def layer_norm_backward(grad, centered_scaled, inv):
    return inv * (
        grad
        - jnp.mean(grad, axis=-1, keepdims=True)
        - centered_scaled * jnp.mean(grad * centered_scaled, axis=-1, keepdims=True)
    )


def shards(pair, product, mask, grad_out, weights, norms):
    rows_here, cols_here, channel_total = pair.shape
    element_count = rows_here * cols_here
    centered_scaled, inv = layer_normalize(
        pair.astype(jnp.float32).reshape(element_count, channel_total)
    )
    zn = (centered_scaled * norms[0] + norms[1]).astype(jnp.bfloat16)
    wcat = jnp.transpose(weights[:5], (1, 0, 2)).reshape(channel_total, 5 * channel_total)
    logits = jnp.dot(zn, wcat, preferred_element_type=jnp.float32)
    ga = jax.nn.sigmoid(logits[:, 0:channel_total])
    pa = logits[:, channel_total : 2 * channel_total]
    gb = jax.nn.sigmoid(logits[:, 2 * channel_total : 3 * channel_total])
    pb = logits[:, 3 * channel_total : 4 * channel_total]
    og = jax.nn.sigmoid(logits[:, 4 * channel_total :])
    valid = mask.astype(jnp.float32).reshape(element_count, 1)
    a_proj = (valid * ga * pa).astype(jnp.bfloat16).reshape(rows_here, cols_here, channel_total)
    b_proj = (valid * gb * pb).astype(jnp.bfloat16).reshape(rows_here, cols_here, channel_total)
    standardized_input, inverse_deviation_squared = layer_normalize(
        product.astype(jnp.float32).reshape(element_count, channel_total)
    )
    normed_input = (standardized_input * norms[2] + norms[3]).astype(jnp.bfloat16)
    y_out = jnp.dot(normed_input, weights[5], preferred_element_type=jnp.float32)
    go = grad_out.astype(jnp.float32).reshape(element_count, channel_total)
    d_og = go * y_out
    d_y = (go * og).astype(jnp.bfloat16)
    normed_input_gradient = lax.dot_general(
        d_y, weights[5], (((1,), (1,)), ((), ())), preferred_element_type=jnp.float32
    )
    input_gradient = (
        layer_norm_backward(
            normed_input_gradient * norms[2], standardized_input, inverse_deviation_squared
        )
        .astype(jnp.bfloat16)
        .reshape(rows_here, cols_here, channel_total)
    )
    d_ologit = (d_og * og * (1.0 - og)).astype(jnp.bfloat16)
    gathered = lax.all_gather(input_gradient, "col", axis=1, tiled=True)
    block = gathered
    da = jnp.einsum(
        "ijc,jkc->ikc",
        block,
        lax.all_gather(b_proj, "row", axis=0, tiled=True),
        preferred_element_type=jnp.float32,
    )
    block = gathered
    db = lax.psum_scatter(
        jnp.einsum("ijc,ikc->jkc", block, a_proj, preferred_element_type=jnp.float32).astype(
            jnp.bfloat16
        ),
        "row",
        scatter_dimension=0,
        tiled=True,
    ).astype(jnp.float32)
    da = da.reshape(element_count, channel_total)
    db = db.reshape(element_count, channel_total)
    d_pa = da * valid * ga
    d_ga = da * valid * pa * ga * (1.0 - ga)
    d_pb = db * valid * gb
    d_gb = db * valid * pb * gb * (1.0 - gb)
    dcat = jnp.concatenate([d_ga, d_pa, d_gb, d_pb], axis=1).astype(jnp.bfloat16)
    dcat = jnp.concatenate([dcat, d_ologit], axis=1)
    normed_output_gradient = lax.dot_general(
        dcat, wcat, (((1,), (1,)), ((), ())), preferred_element_type=jnp.float32
    )
    grad_pair = (
        layer_norm_backward(normed_output_gradient * norms[0], centered_scaled, inv)
        .astype(jnp.bfloat16)
        .reshape(rows_here, cols_here, channel_total)
    )
    local_w = lax.dot_general(
        zn, dcat, (((0,), (0,)), ((), ())), preferred_element_type=jnp.float32
    )
    local_w = jnp.transpose(local_w.reshape(channel_total, 5, channel_total), (1, 0, 2))
    local_wo = lax.dot_general(
        normed_input, d_y, (((0,), (0,)), ((), ())), preferred_element_type=jnp.float32
    )
    local_weights = jnp.concatenate([local_w, local_wo[None]], axis=0)
    local_norms = jnp.stack(
        [
            jnp.sum(normed_output_gradient * centered_scaled, axis=0),
            jnp.sum(normed_output_gradient, axis=0),
            jnp.sum(normed_input_gradient * standardized_input, axis=0),
            jnp.sum(normed_input_gradient, axis=0),
        ]
    )
    grad_weights, norm_vector_gradients = lax.psum((local_weights, local_norms), ("row", "col"))
    return (grad_pair, grad_weights, norm_vector_gradients)


def solution(mesh):
    in_specs = (
        P(("groups", "row"), "col", None),
        P(("groups", "row"), "col", None),
        P(("groups", "row"), "col"),
        P(("groups", "row"), "col", None),
        P(),
        P(),
    )
    out_specs = (P(("groups", "row"), "col", None), P("groups", None, None), P("groups", None))
    return jax.shard_map(shards, mesh=mesh, in_specs=in_specs, out_specs=out_specs, check_vma=False)
```

profile of v0, /device:TPU:0, one launch (start us, length us, event | category | flops | bytes accessed | tf_op | source)
XLA Modules:
  0.0 1287.0 jit_solution(7433690190034810187)
XLA Ops:
  37.4 25.4 %fusion.33 = f32[25600,640]{1,0:T(8,128)} fusion(bf16[25600,128]{1,0:T(8,128)(2,1)} %bitcast.91, bf16[128,640]{0,1:T(8,128)(2,1)S(1)} %bitcast.107), kind=kOutput, calls=%fused_computation.80 | convolution fusion | flops 4194304000 | bytes 72253440 | tf_op jit(solution)/shard_map/dot_general | solution.py:32
  62.9 20.6 %fusion.4 = (bf16[25600,128]{1,0:T(8,128)(2,1)}, bf16[25600,128]{1,0:T(8,128)(2,1)}) fusion(f32[25600,640]{1,0:T(8,128)} %fusion.33, bf16[160,160,128]{2,1,0:T(8,128)(2,1)} %param.9, f32[25600]{0:T(1024)S(1)} %mul.196), kind=kLoop, calls=%fused_computation.7 | loop fusion | flops 39321600 | bytes 59084800 | tf_op jit(solution)/shard_map/convert_element_type | solution.py:48
  101.6 15.0 %fusion.21 = f32[25600,128]{1,0:T(8,128)S(1)} fusion(bf16[160,160,128]{2,1,0:T(8,128)(2,1)} %param.7, f32[25600]{0:T(1024)S(1)} %div.44, f32[25600]{0:T(1024)S(1)} %rsqrt.27), kind=kLoop, calls=%fused_computation.31 | loop fusion | flops 9830400 | bytes 19865600 | tf_op jit(solution)/shard_map/mul | solution.py:13
  116.7 24.7 %multiply_reduce_fusion = (f32[128]{0:T(128)}, f32[128]{0:T(128)}, f32[25600]{0:T(1024)S(1)}, f32[25600]{0:T(1024)S(1)}, f32[25600,128]{1,0:T(8,128)S(1)}) fusion(f32[25600]{0:T(1024)S(1)} %rsqrt.27, f32[25600]{0:T(1024)S(1)} %div.44, bf16[160,160,128]{2,1,0:T(8,128)(2,1)S(1)} %bitcast.81, f32[25600,128]{1,0:T(8,128)S(1)} %fusion.21, ...), kind=kOutput, calls=%fused_computation.32 | convolution fusion | flops 871577344 | bytes 39765504 | tf_op jit(solution)/shard_map/dot_general | solution.py:49
  141.4 20.1 %multiply_convert_fusion.4 = bf16[25600,128]{1,0:T(8,128)(2,1)} fusion(f32[25600,128]{1,0:T(8,128)S(1)} %get-tuple-element.24, f32[25600]{0:T(1024)S(1)} %get-tuple-element.26, f32[25600]{0:T(1024)S(1)} %get-tuple-element.27, f32[128]{0:T(128)S(1)} %get-tuple-element.23, f32[25600]{0:T(1024)S(1)} %rsqrt.27, f32[25600]{0:T(1024)S(1)} %div.44, ...), kind=kLoop, calls=%fused_computation.41 | loop fusion | flops 29491200 | bytes 26624512 | tf_op jit(solution)/shard_map/convert_element_type | solution.py:56
  169.9 77.0 %all-gather.3.cloned.1.call-done = bf16[640,160,128]{2,1,0:T(8,128)(2,1)} async-done(((bf16[160,160,128]{2,1,0:T(8,128)(2,1)}), bf16[640,160,128]{2,1,0:T(8,128)(2,1)}) %all-gather.3.cloned.1.call-update) | async-done | bytes 26214416 | tf_op jit(solution)/shard_map/all_gather | solution.py:65
  246.9 38.9 %copy.28 = bf16[640,160,128]{0,1,2:T(8,128)(2,1)} copy(bf16[640,160,128]{2,1,0:T(8,128)(2,1)} %all-gather.3.cloned.1.call-done) | data formatting | bytes 52428800 | tf_op jit(solution)/shard_map/all_gather | solution.py:65
  285.9 404.8 %all-gather.5.cloned.1.call-done = bf16[160,640,128]{2,0,1:T(8,128)(2,1)} async-done(((bf16[160,160,128]{2,0,1:T(8,128)(2,1)}), bf16[160,640,128]{2,0,1:T(8,128)(2,1)}) %all-gather.5.cloned.1.call-update) | async-done | bytes 26214416 | tf_op jit(solution)/shard_map/all_gather | solution.py:60
  690.7 37.9 %copy.29 = bf16[160,640,128]{1,0,2:T(8,128)(2,1)} copy(bf16[160,640,128]{2,0,1:T(8,128)(2,1)} %all-gather.5.cloned.1.call-done) | data formatting | bytes 52428800 | tf_op jit(solution)/shard_map/all_gather | solution.py:60
  728.6 25.5 %convolution_bitcast_fusion = f32[160,160,128]{0,1,2:T(8,128)} fusion(bf16[640,160,128]{0,1,2:T(8,128)(2,1)} %copy.28, bf16[160,640,128]{1,0,2:T(8,128)(2,1)} %copy.29), kind=kOutput, calls=%fused_computation.51 | convolution fusion | flops 4194304000 | bytes 65536000 | tf_op jit(solution)/shard_map/ijc,jkc->ikc/dot_general | solution.py:62
  754.1 18.7 %copy.30 = f32[160,160,128]{2,1,0:T(8,128)} copy(f32[160,160,128]{0,1,2:T(8,128)} %convolution_bitcast_fusion) | data formatting | bytes 26214400 | tf_op jit(solution)/shard_map/ijc,jkc->ikc/transpose | solution.py:62
  772.8 22.3 %multiply_convert_fusion.2 = (bf16[25600,128]{1,0:T(8,128)(2,1)}, bf16[25600,128]{1,0:T(8,128)(2,1)}, bf16[25600,128]{1,0:T(8,128)(2,1)}) fusion(f32[160,160,128]{2,1,0:T(8,128)} %copy.30, f32[25600]{0:T(1024)S(1)} %mul.196, f32[25600,640]{1,0:T(8,128)} %fusion.33), kind=kLoop, calls=%fused_computation.39 | loop fusion | flops 45875200 | bytes 59084800 | tf_op jit(solution)/shard_map/convert.3
  795.0 15.6 %copy.31 = bf16[160,160,128]{0,1,2:T(8,128)(2,1)} copy(bf16[160,160,128]{2,1,0:T(8,128)(2,1)} %bitcast.101) | data formatting | bytes 13107200 | tf_op jit(solution)/shard_map/reshape | solution.py:39
  810.6 25.2 %convert_bitcast_fusion = bf16[640,160,128]{0,1,2:T(8,128)(2,1)} fusion(bf16[160,160,128]{0,1,2:T(8,128)(2,1)} %copy.31, bf16[160,640,128]{1,0,2:T(8,128)(2,1)} %copy.29), kind=kOutput, calls=%fused_computation.5 | convolution fusion | flops 4207411200 | bytes 58982400 | tf_op jit(solution)/shard_map/ijc,ikc->jkc/dot_general | solution.py:70
  835.8 38.1 %copy.33 = bf16[640,160,128]{2,1,0:T(8,128)(2,1)} copy(bf16[640,160,128]{0,1,2:T(8,128)(2,1)} %convert_bitcast_fusion) | data formatting | bytes 52428800 | tf_op jit(solution)/shard_map/convert_element_type | solution.py:70
  898.8 15.2 %fusion.20 = f32[25600,128]{1,0:T(8,128)} fusion(bf16[160,160,128]{2,1,0:T(8,128)(2,1)S(1)} %bitcast.87, f32[25600]{0:T(1024)S(1)} %div.48, f32[25600]{0:T(1024)S(1)} %rsqrt.25), kind=kLoop, calls=%fused_computation.28 | loop fusion | flops 9830400 | bytes 19865600 | tf_op jit(solution)/shard_map/mul | solution.py:13
  922.7 136.8 %reduce-scatter.2.cloned.1.call-done = bf16[160,160,128]{2,1,0:T(8,128)(2,1)} async-done(((bf16[640,160,128]{2,1,0:T(8,128)(2,1)}), bf16[160,160,128]{2,1,0:T(8,128)(2,1)}) %reduce-scatter.2.cloned.1.call-update) | async-done | bytes 6553616 | tf_op jit(solution)/shard_map/reduce_scatter | solution.py:69
  1059.5 19.3 %fusion.24 = bf16[25600,640]{1,0:T(8,128)(2,1)} fusion(bf16[25600,640]{1,0:T(8,128)(2,1)} %constant_dynamic-update-slice_fusion, f32[25600,640]{1,0:T(8,128)} %fusion.33, bf16[25600,128]{1,0:T(8,128)(2,1)} %bitcast.99, f32[25600]{0:T(1024)S(1)} %mul.196), kind=kLoop, calls=%fused_computation.54 | loop fusion | flops 32768000 | bytes 39424000
  1103.1 26.9 %multiply_reduce_fusion.1 = (f32[128]{0:T(128)S(1)}, f32[128]{0:T(128)S(1)}, f32[25600]{0:T(1024)S(1)}, f32[25600]{0:T(1024)S(1)}, f32[25600,128]{1,0:T(8,128)}) fusion(f32[25600]{0:T(1024)S(1)} %rsqrt.25, f32[25600]{0:T(1024)S(1)} %div.48, bf16[160,160,128]{2,1,0:T(8,128)(2,1)S(1)} %bitcast.89, f32[25600,128]{1,0:T(8,128)} %fusion.20, ...), kind=kOutput, calls=%fused_computation.33 | convolution fusion | flops 4227020800 | bytes 66110976 | tf_op jit(solution)/shard_map/dot_general | solution.py:85
  1130.0 40.6 %copy.35 = bf16[640,25600]{1,0:T(8,128)(2,1)} copy(bf16[640,25600]{0,1:T(8,128)(2,1)} %bitcast.22) | data formatting | bytes 65536000 | tf_op jit(solution)/shard_map/dot_general | solution.py:93
  1170.6 16.2 %convolution_bitcast_fusion.1 = f32[5,128,128]{2,1,0:T(8,128)S(1)} fusion(bf16[25600,128,1]{1,0,2:T(8,128)(2,1)} %bitcast.92, bf16[5,128,25600]{2,1,0:T(8,128)(2,1)} %bitcast.90), kind=kOutput, calls=%fused_computation.57 | convolution fusion | flops 4194304000 | bytes 39649280 | tf_op jit(solution)/shard_map/dot_general | solution.py:93
  1187.7 21.6 %multiply_convert_fusion = bf16[25600,128]{1,0:T(8,128)(2,1)} fusion(f32[25600,128]{1,0:T(8,128)} %get-tuple-element.25, f32[25600]{0:T(1024)S(1)} %broadcast_multiply_fusion.2, f32[25600]{0:T(1024)S(1)} %broadcast_multiply_fusion.3, f32[128]{0:T(128)S(1)} %copy-done.13, f32[25600]{0:T(1024)S(1)} %rsqrt.25, f32[25600]{0:T(1024)S(1)} %div.48, ...), kind=kLoop, calls=%fused_computation.35 | loop fusion | flops 29491200 | bytes 26624512 | tf_op jit(solution)/shard_map/convert_element_type | solution.py:90
  1209.3 33.1 %psum.15 = f32[4,128]{1,0:T(4,128)} all-reduce(f32[4,128]{1,0:T(4,128)S(1)} %pad_maximum_fusion.1), channel_id=1, replica_groups=mesh['groups'=2,'row'=4,'col'=4] {'row','col'}, use_global_device_ids=true, to_apply=%region_14.0 | all-reduce | flops 512 | bytes 4096 | tf_op jit(solution)/shard_map/psum | solution.py:109
  1242.3 35.9 %all-reduce.2.cloned.1.call-done = f32[6,128,128]{2,1,0:T(8,128)} async-done(((f32[6,128,128]{2,1,0:T(8,128)}), f32[6,128,128]{2,1,0:T(8,128)}) %all-reduce.2.cloned.1.call-update) | async-done | bytes 393232 | tf_op jit(solution)/shard_map/psum | solution.py:109
  (113 shorter events, 116.9 us)
Async XLA Ops:
  7.2 21.0 %slice-start.4 = ((s8[6553600]{0:T(1024)(128)(4,1)}), s8[2359296]{0:T(1024)(128)(4,1)S(1)}, s32[]{:S(2)}) async-start(s8[6553600]{0:T(1024)(128)(4,1)} %bitcast.84), calls=%async_computation.9 | async-start | bytes 4718592
  7.2 239.8 %all-gather.3.cloned.1.call-start = ((), (), s32[]{:S(2)}) async-start(), calls=%async_computation.1 | async-start | bytes 32768000 | tf_op jit(solution)/shard_map/all_gather | solution.py:65
  8.6 28.8 %copy-start.12 = (f32[128]{0:T(128)}, f32[128]{0:T(128)S(1)}, u32[]{:S(2)}) copy-start(f32[128]{0:T(128)S(1)} %get-tuple-element.22) | copy-start | bytes 1540
  10.8 26.6 %copy-start.10 = (bf16[5,128,128]{1,2,0:T(8,128)(2,1)}, bf16[5,128,128]{1,2,0:T(8,128)(2,1)S(1)}, u32[]{:S(2)}) copy-start(bf16[5,128,128]{1,2,0:T(8,128)(2,1)S(1)} %copy.40) | copy-start | bytes 491524
  10.8 17.3 %slice-start.5 = ((s8[6553600]{0:T(1024)(128)(4,1)}), s8[4194304]{0:T(1024)(128)(4,1)S(1)}, s32[]{:S(2)}) async-start(s8[6553600]{0:T(1024)(128)(4,1)} %bitcast.84), calls=%async_computation.10 | async-start | bytes 8388608
  16.8 20.7 %copy-start.2 = (f32[160,160]{1,0:T(8,128)}, f32[160,160]{1,0:T(8,128)S(1)}, u32[]{:S(2)}) copy-start(f32[160,160]{1,0:T(8,128)S(1)} %broadcast_multiply_fusion.1) | copy-start | bytes 307204
  28.1 34.7 %copy-start.6 = (f32[160,160]{1,0:T(8,128)}, f32[160,160]{1,0:T(8,128)S(1)}, u32[]{:S(2)}) copy-start(f32[160,160]{1,0:T(8,128)S(1)} %add_rsqrt_fusion.1) | copy-start | bytes 307204
  83.5 607.2 %all-gather.5.cloned.1.call-start = ((), (), s32[]{:S(2)}) async-start(), calls=%async_computation.2 | async-start | bytes 32768000 | tf_op jit(solution)/shard_map/all_gather | solution.py:60
  89.5 27.2 %copy-start.4 = (f32[160,160]{1,0:T(8,128)}, f32[160,160]{1,0:T(8,128)S(1)}, u32[]{:S(2)}) copy-start(f32[160,160]{1,0:T(8,128)S(1)} %broadcast_multiply_fusion) | copy-start | bytes 307204
  89.6 27.0 %slice-start = ((s8[6553600]{0:T(1024)(128)(4,1)}), s8[2359296]{0:T(1024)(128)(4,1)S(1)}, s32[]{:S(2)}) async-start(s8[6553600]{0:T(1024)(128)(4,1)} %bitcast.80), calls=%async_computation.5 | async-start | bytes 4718592
  101.4 40.0 %copy-start.8 = (f32[160,160]{1,0:T(8,128)}, f32[160,160]{1,0:T(8,128)S(1)}, u32[]{:S(2)}) copy-start(f32[160,160]{1,0:T(8,128)S(1)} %add_rsqrt_fusion) | copy-start | bytes 307204
  116.6 24.8 %copy-start = (f32[25600,128]{1,0:T(8,128)}, f32[25600,128]{1,0:T(8,128)S(1)}, u32[]{:S(2)}) copy-start(f32[25600,128]{1,0:T(8,128)S(1)} %fusion.21) | copy-start | bytes 39321604
  169.6 889.9 %reduce-scatter.2.cloned.1.call-start = ((), (), s32[]{:S(2)}) async-start(), calls=%async_computation.3 | async-start | bytes 32768000 | tf_op jit(solution)/shard_map/reduce_scatter | solution.py:69
  873.9 404.3 %all-reduce.2.cloned.1.call-start = ((), (), s32[]{:S(2)}) async-start(), calls=%async_computation.4 | async-start | bytes 786432 | tf_op jit(solution)/shard_map/psum | solution.py:109
  875.1 23.7 %slice-start.6 = ((s8[6553600]{0:T(1024)(128)(4,1)}), s8[4194304]{0:T(1024)(128)(4,1)S(1)}, s32[]{:S(2)}) async-start(s8[6553600]{0:T(1024)(128)(4,1)} %bitcast.86), calls=%async_computation.11 | async-start | bytes 8388608
  875.1 23.7 %slice-start.7 = ((s8[6553600]{0:T(1024)(128)(4,1)}), s8[2359296]{0:T(1024)(128)(4,1)S(1)}, s32[]{:S(2)}) async-start(s8[6553600]{0:T(1024)(128)(4,1)} %bitcast.86), calls=%async_computation.12 | async-start | bytes 4718592
  889.3 24.7 %slice-start.12 = ((s8[6553600]{0:T(1024)(128)(4,1)}), s8[2359296]{0:T(1024)(128)(4,1)S(1)}, s32[]{:S(2)}) async-start(s8[6553600]{0:T(1024)(128)(4,1)} %bitcast.97), calls=%async_computation.17 | async-start | bytes 4718592
  898.8 15.2 %slice-start.13 = ((s8[6553600]{0:T(1024)(128)(4,1)}), s8[4194304]{0:T(1024)(128)(4,1)S(1)}, s32[]{:S(2)}) async-start(s8[6553600]{0:T(1024)(128)(4,1)} %bitcast.97), calls=%async_computation.18 | async-start | bytes 8388608
  919.4 172.7 %slice-start.14 = ((s8[6553600]{0:T(1024)(128)(4,1)}), s8[2359296]{0:T(1024)(128)(4,1)S(1)}, s32[]{:S(2)}) async-start(s8[6553600]{0:T(1024)(128)(4,1)} %bitcast.103), calls=%async_computation.19 | async-start | bytes 4718592
  1059.5 19.3 %copy-start.1 = (bf16[160,160,128]{2,1,0:T(8,128)(2,1)S(1)}, bf16[160,160,128]{2,1,0:T(8,128)(2,1)}, u32[]{:S(2)}) copy-start(bf16[160,160,128]{2,1,0:T(8,128)(2,1)} %reduce-scatter.2.cloned.1.call-done) | copy-start | bytes 19660804
  1059.5 32.6 %slice-start.15 = ((s8[6553600]{0:T(1024)(128)(4,1)}), s8[4194304]{0:T(1024)(128)(4,1)S(1)}, s32[]{:S(2)}) async-start(s8[6553600]{0:T(1024)(128)(4,1)} %bitcast.103), calls=%async_computation.20 | async-start | bytes 8388608
  1078.8 24.3 %slice-start.8 = ((s8[6553600]{0:T(1024)(128)(4,1)}), s8[4194304]{0:T(1024)(128)(4,1)S(1)}, s32[]{:S(2)}) async-start(s8[6553600]{0:T(1024)(128)(4,1)} %bitcast.88), calls=%async_computation.13 | async-start | bytes 8388608
  1187.6 21.6 %copy-start.15 = (f32[128]{0:T(128)S(1)}, f32[128]{0:T(128)}, u32[]{:S(2)}) copy-start(f32[128]{0:T(128)} %get-tuple-element.11) | copy-start | bytes 1540
  1187.6 21.6 %copy-start.16 = (f32[128]{0:T(128)S(1)}, f32[128]{0:T(128)}, u32[]{:S(2)}) copy-start(f32[128]{0:T(128)} %get-tuple-element.12) | copy-start | bytes 1540
  (13 other events, 115.4 us)
Sparse Core Ops, SparseCore 0:
  83.6 163.2 all-gather.2
  248.5 442.1 all-gather.4
  874.0 185.4 reduce-scatter.1
  1187.8 90.4 all-reduce.1
where the time goes:
time: 1300 us; the launch traced here: 1290 us
  waiting for transfers between devices  655 us (50%)
  local copies, waits for them, and re-layouts  214 us (16%)
  other arithmetic  203 us (16%)
  matrix products  167 us (13%)
  blocking collectives  33.1 us (3%)
  between operations  14.7 us (1%)
    all_gather x1, waiting for transfers between devices, shards(): gathered = lax.all_gather(input_gradient, 'col', axis=1, tiled=True)  405 us
    reduce_scatter x1, waiting for transfers between devices, shards(): lax.psum_scatter(jnp.einsum('ijc,ikc->jkc', block, a_proj, preferred_elem...  137 us
    all_gather x1, waiting for transfers between devices, shards(): lax.all_gather(b_proj, 'row', axis=0, tiled=True)  77 us
    dot_general x1, local copies, waits for them, and re-layouts, shards(): lax.dot_general(zn, dcat, (((0,), (0,)), ((), ())), preferred_element_typ...  40.6 us
    all_gather x1, local copies, waits for them, and re-layouts, shards(): lax.all_gather(b_proj, 'row', axis=0, tiled=True)  38.9 us
    convert_element_type x1, local copies, waits for them, and re-layouts, shards(): jnp.einsum('ijc,ikc->jkc', block, a_proj, preferred_element_type=jnp.floa...  38.1 us
    all_gather x1, local copies, waits for them, and re-layouts, shards(): gathered = lax.all_gather(input_gradient, 'col', axis=1, tiled=True)  37.9 us
    psum x1, waiting for transfers between devices, shards(): lax.psum((local_weights, local_norms), ('row', 'col'))  35.9 us
  transfers between devices with their start and end apart: 4, of which 4 were waited for; matrix products, arithmetic and copies ran while one was open for 15% of the time, Pallas kernels for 0%

commit v1 on v0

v1 whole, which is shorter than its diff:
```python
import functools

import jax
import jax.numpy as jnp
from jax import lax
from jax.experimental import pallas as pl
from jax.experimental.pallas import tpu as pltpu
from jax.sharding import PartitionSpec as P

eps = 1e-05
F32 = jnp.float32
BF16 = jnp.bfloat16
VMEM_LIMIT = 48 * 1024 * 1024


def dot(x, y):
    return jnp.dot(x, y, preferred_element_type=F32)


def dot_t(x, y):
    return lax.dot_general(x, y, (((1,), (1,)), ((), ())), preferred_element_type=F32)


def t_dot(x, y):
    return lax.dot_general(x, y, (((0,), (0,)), ((), ())), preferred_element_type=F32)


def layer_normalize(v):
    mean = jnp.mean(v, axis=-1, keepdims=True)
    cent = v - mean
    inv = lax.rsqrt(jnp.mean(cent * cent, axis=-1, keepdims=True) + eps)
    return cent * inv, inv


def layer_norm_backward(grad, hat, inv):
    return inv * (
        grad
        - jnp.mean(grad, axis=-1, keepdims=True)
        - hat * jnp.mean(grad * hat, axis=-1, keepdims=True)
    )


def tile(ref, s, step):
    block = ref[pl.ds(s * step, step)]
    return block.reshape(-1, block.shape[-1])


def put(ref, s, step, value):
    ref[pl.ds(s * step, step)] = value.reshape((step,) + ref.shape[1:]).astype(ref.dtype)


def first_step(axes):
    first = pl.program_id(0) == 0
    for axis in range(1, axes):
        first = jnp.logical_and(first, pl.program_id(axis) == 0)
    return first


def dx_kernel(step, chained, pair, product, go, w, norms, *rest):
    acc_in = rest[1] if chained else None
    dx, dol, acc = rest[-3:]
    c = pair.shape[-1]

    @pl.when(first_step(2))
    def _():
        acc[...] = acc_in[...] if chained else jnp.zeros_like(acc)

    def body(s, carry):
        hat, _ = layer_normalize(tile(pair, s, step).astype(F32))
        zn = (hat * norms[0:1] + norms[1:2]).astype(BF16)
        og = jax.nn.sigmoid(dot(zn, w[4]))
        xhat, inv2 = layer_normalize(tile(product, s, step).astype(F32))
        xn = (xhat * norms[2:3] + norms[3:4]).astype(BF16)
        y = dot(xn, w[5])
        gof = tile(go, s, step).astype(F32)
        d_y = (gof * og).astype(BF16)
        d_xn = dot_t(d_y, w[5])
        put(dx, s, step, layer_norm_backward(d_xn * norms[2:3], xhat, inv2))
        put(dol, s, step, gof * y * og * (1.0 - og))
        acc[5 * c : 6 * c] += t_dot(xn, d_y)
        acc[6 * c + 2 : 6 * c + 3] += jnp.sum(d_xn * xhat, axis=0, keepdims=True)
        acc[6 * c + 3 : 6 * c + 4] += jnp.sum(d_xn, axis=0, keepdims=True)
        return carry

    lax.fori_loop(0, pair.shape[0] // step, body, 0)


def dx_chunk(pair, product, go, weights, norms, off, size, chain):
    rows, cols, c = pair.shape
    jb = 16 if size % 16 == 0 else size
    ib = 80 if rows % 80 == 0 else rows // 2 if rows % 2 == 0 else rows
    step = 16 if ib % 16 == 0 else ib
    base = off // jb
    blk = pl.BlockSpec((ib, jb, c), lambda i, j: (i, base + j, 0))
    out = pl.BlockSpec((ib, jb, c), lambda i, j: (i, j, 0))
    full = lambda shape: pl.BlockSpec(shape, lambda i, j: (0,) * len(shape))
    n = rows * size
    acc = (6 * c + 32, c)
    return pl.pallas_call(
        functools.partial(dx_kernel, step, bool(chain)),
        grid=(rows // ib, size // jb),
        in_specs=[blk, blk, blk, full(weights.shape), full(norms.shape)]
        + ([pl.BlockSpec(memory_space=pl.ANY), full(acc)] if chain else []),
        out_specs=[out, blk, full(acc)],
        out_shape=[
            jax.ShapeDtypeStruct((rows, size, c), BF16),
            jax.ShapeDtypeStruct((rows, cols, c), BF16),
            jax.ShapeDtypeStruct(acc, F32),
        ],
        input_output_aliases={5: 1} if chain else {},
        compiler_params=pltpu.CompilerParams(vmem_limit_bytes=VMEM_LIMIT),
        cost_estimate=pl.CostEstimate(
            flops=8 * n * c * c, bytes_accessed=10 * n * c, transcendentals=n * c
        ),
        name="dx_part",
    )(pair, product, go, weights, norms, *chain)


def proj_kernel(step, pair, valid, w, norms, a, b, g_ga, g_pa, g_gb, g_pb, flip):
    cols, c = pair.shape[1:]

    def body(s, carry):
        hat, _ = layer_normalize(tile(pair, s, step).astype(F32))
        zn = (hat * norms[0:1] + norms[1:2]).astype(BF16)
        m = tile(valid, s, step).astype(F32)
        for at, d_gate, d_value in ((0, g_ga, g_pa), (2, g_gb, g_pb)):
            gate = jax.nn.sigmoid(dot(zn, w[at]))
            p = dot(zn, w[at + 1])
            mg = m * gate
            mgp = mg * p
            if at == 0:
                put(a, s, step, mgp)
            else:
                flip[pl.ds(s * step, step)] = mgp.reshape(step, cols, c)
            put(d_value, s, step, mg)
            put(d_gate, s, step, mgp * (1.0 - gate))
        return carry

    lax.fori_loop(0, pair.shape[0] // step, body, 0)
    b[...] = jnp.swapaxes(flip[...], 0, 1).astype(b.dtype)


def projections(pair, valid, weights, norms):
    rows, cols, c = pair.shape
    ib = 16 if rows % 16 == 0 else rows
    step = 2
    blk = pl.BlockSpec((ib, cols, c), lambda i: (i, 0, 0))
    swapped = pl.BlockSpec((cols, ib, c), lambda i: (0, i, 0))
    full = lambda shape: pl.BlockSpec(shape, lambda i: (0,) * len(shape))
    n = rows * cols
    kept = jax.ShapeDtypeStruct((rows, cols, c), BF16)
    return pl.pallas_call(
        functools.partial(proj_kernel, step),
        grid=(rows // ib,),
        in_specs=[blk, blk, full(weights.shape), full(norms.shape)],
        out_specs=[blk, swapped] + [blk] * 4,
        out_shape=[kept, jax.ShapeDtypeStruct((cols, rows, c), BF16)] + [kept] * 4,
        scratch_shapes=[pltpu.VMEM((ib, cols, c), F32)],
        compiler_params=pltpu.CompilerParams(vmem_limit_bytes=VMEM_LIMIT),
        cost_estimate=pl.CostEstimate(
            flops=8 * n * c * c, bytes_accessed=16 * n * c, transcendentals=2 * n * c
        ),
        name="projections",
    )(pair, valid, weights, norms)


def to_channels_kernel(slots, r, *refs):
    out = refs[-1]
    blocks = [ref[...].reshape(ref.shape[-3:]) for ref in refs[:-1]]
    x = jnp.concatenate(blocks, axis=1)
    out[...] = jnp.transpose(x, (2, 0, 1))


def to_channels(arrays, specs, r, lead, size, c):
    slots = len(specs)
    lanes = slots * size
    n = lead * lanes * c
    return pl.pallas_call(
        functools.partial(to_channels_kernel, slots),
        grid_spec=pltpu.PrefetchScalarGridSpec(
            num_scalar_prefetch=1,
            grid=(lead // 16,),
            in_specs=specs,
            out_specs=pl.BlockSpec((c, 16, lanes), lambda i, r: (0, i, 0)),
        ),
        out_shape=jax.ShapeDtypeStruct((c, lead, lanes), BF16),
        compiler_params=pltpu.CompilerParams(vmem_limit_bytes=VMEM_LIMIT),
        cost_estimate=pl.CostEstimate(flops=4 * n, bytes_accessed=4 * n, transcendentals=0),
        name="to_channels",
    )(r, *arrays)


def gathered_to_channels(g, r):
    n, rows, size, c = g.shape
    specs = [
        pl.BlockSpec((1, 16, size, c), lambda i, r, t=t: (r[0] ^ t, i, 0, 0)) for t in range(n)
    ]
    return to_channels([g] * n, specs, r, rows, size, c)


def slots_to_channels(slots, r, off, size):
    lead, _, c = slots[0].shape
    specs = [pl.BlockSpec((16, size, c), lambda i, r: (i, off // size, 0))] * len(slots)
    return to_channels(slots, specs, r, lead, size, c)


def from_channels_kernel(slots, x, kept, sent):
    y = jnp.transpose(x[...], (1, 2, 0))
    size = y.shape[1] // slots
    for t in range(slots):
        out = sent if t % 2 else kept
        out[t // 2] = y[:, t * size : (t + 1) * size]


def from_channels(x, slots):
    c, lead, lanes = x.shape
    size = lanes // slots
    n = x.size
    out = pl.BlockSpec((slots // 2, 16, size, c), lambda i: (0, i, 0, 0))
    return pl.pallas_call(
        functools.partial(from_channels_kernel, slots),
        grid=(lead // 16,),
        in_specs=[pl.BlockSpec((c, 16, lanes), lambda i: (0, i, 0))],
        out_specs=[out, out],
        out_shape=[jax.ShapeDtypeStruct((slots // 2, lead, size, c), BF16)] * 2,
        compiler_params=pltpu.CompilerParams(vmem_limit_bytes=VMEM_LIMIT),
        cost_estimate=pl.CostEstimate(flops=4 * n, bytes_accessed=4 * n, transcendentals=0),
        name="from_channels",
    )(x)


def final_kernel(step, chained, pair, da, db0, db1, g_ga, g_pa, g_gb, g_pb, dol, w, norms, acc_in, *rest):
    gp, acc, flip = rest[-3:]
    c = pair.shape[-1]

    @pl.when(first_step(1))
    def _():
        acc[...] = acc_in[...]

    flip[...] = jnp.swapaxes(db0[...].astype(F32) + db1[...].astype(F32), 0, 1)

    def body(s, carry):
        hat, inv = layer_normalize(tile(pair, s, step).astype(F32))
        zn = (hat * norms[0:1] + norms[1:2]).astype(BF16)
        dav = tile(da, s, step).astype(F32)
        dbv = tile(flip, s, step)
        parts = [
            (dav * tile(g_ga, s, step).astype(F32)).astype(BF16),
            (dav * tile(g_pa, s, step).astype(F32)).astype(BF16),
            (dbv * tile(g_gb, s, step).astype(F32)).astype(BF16),
            (dbv * tile(g_pb, s, step).astype(F32)).astype(BF16),
            tile(dol, s, step),
        ]
        dzn = dot_t(parts[0], w[0])
        for at in range(1, 5):
            dzn = dzn + dot_t(parts[at], w[at])
        put(gp, s, step, layer_norm_backward(dzn * norms[0:1], hat, inv))
        for at in range(5):
            acc[at * c : (at + 1) * c] += t_dot(zn, parts[at])
        acc[6 * c : 6 * c + 1] += jnp.sum(dzn * hat, axis=0, keepdims=True)
        acc[6 * c + 1 : 6 * c + 2] += jnp.sum(dzn, axis=0, keepdims=True)
        return carry

    lax.fori_loop(0, pair.shape[0] // step, body, 0)


def final_chunk(pair, da, db0, db1, gs, dol, weights, norms, acc, off, size, chain):
    rows, cols, c = pair.shape
    ib = 16 if size % 16 == 0 else size
    step = 2
    base = off // ib
    blk = pl.BlockSpec((ib, cols, c), lambda i: (base + i, 0, 0))
    own = pl.BlockSpec((cols, ib, c), lambda i: (0, i, 0))
    full = lambda shape: pl.BlockSpec(shape, lambda i: (0,) * len(shape))
    n = size * cols
    return pl.pallas_call(
        functools.partial(final_kernel, step, bool(chain)),
        grid=(size // ib,),
        in_specs=[blk, blk, own, own]
        + [blk] * 5
        + [full(weights.shape), full(norms.shape), full(acc.shape)]
        + ([pl.BlockSpec(memory_space=pl.ANY)] if chain else []),
        out_specs=[blk, full(acc.shape)],
        out_shape=[
            jax.ShapeDtypeStruct((rows, cols, c), BF16),
            jax.ShapeDtypeStruct(acc.shape, F32),
        ],
        input_output_aliases={12: 0} if chain else {},
        scratch_shapes=[pltpu.VMEM((ib, cols, c), F32)],
        compiler_params=pltpu.CompilerParams(vmem_limit_bytes=VMEM_LIMIT),
        cost_estimate=pl.CostEstimate(
            flops=20 * n * c * c, bytes_accessed=22 * n * c, transcendentals=n
        ),
        name="final_part",
    )(pair, da, db0, db1, *gs, dol, weights, norms, acc, *chain)


def swap(v, axis, n, bit):
    return lax.ppermute(v, axis, [(r, r ^ bit) for r in range(n)])


def pick(v, at):
    return lax.dynamic_index_in_dim(v, at, 0, keepdims=False)


def bits_of(n):
    return [1 << k for k in range(n.bit_length() - 1)]


def gather_rows(v, n):
    slots = {0: v}
    for bit in bits_of(n)[::-1]:
        slots.update({t ^ bit: swap(x, "row", n, bit) for t, x in slots.items()})
    return [slots[t] for t in range(n)]


def reduce_rows(kept, sent, n):
    come = swap(sent, "row", n, 1)
    for bit in bits_of(n)[1:]:
        v = (kept.astype(F32) + come.astype(F32)).astype(BF16)
        v = v.reshape((-1, 2) + v.shape[1:])
        kept, come = v[:, 0], swap(v[:, 1], "row", n, bit)
    return kept[0], come[0]


def sum_all(v, n_row, n_col):
    steps = [("row", n_row, b) for b in bits_of(n_row)] + [("col", n_col, b) for b in bits_of(n_col)]
    halved = []
    for k, (axis, n, bit) in enumerate(steps):
        half = v.shape[0] // 2
        if 0 < k < len(steps) - 1 and v.shape[0] % 16 == 0:
            at = (lax.axis_index(axis) // bit) % 2
            pairs = v.reshape((2, half) + v.shape[1:])
            v = pick(pairs, at) + swap(pick(pairs, 1 - at), axis, n, bit)
            halved.append((axis, n, bit, at))
        else:
            v = v + swap(v, axis, n, bit)
    for axis, n, bit, at in halved[::-1]:
        got = swap(v, axis, n, bit)
        v = jnp.where(at == 0, jnp.concatenate([v, got]), jnp.concatenate([got, v]))
    return v


def triangles_plain(n_row, n_col, dx, a, b_swapped):
    rows, cols, c = dx.shape
    block = lax.all_gather(dx, "col", axis=1, tiled=True)
    b_all = lax.all_gather(b_swapped, "row", axis=1, tiled=True)
    part = jnp.einsum("ijc,ikc->kjc", block, a, preferred_element_type=F32).astype(BF16)
    db = lax.psum_scatter(part, "row", scatter_dimension=1, tiled=True)
    da = jnp.einsum("ijc,kjc->ikc", block, b_all, preferred_element_type=F32)
    return da.astype(BF16), [(db, jnp.zeros_like(db))], [(0, rows)]


def triangles(n, blocks, spans, a, b_swapped):
    r = lax.axis_index("row").astype(jnp.int32).reshape(1)
    b_slots = gather_rows(b_swapped, n)
    a_t = jnp.transpose(a, (2, 0, 1))
    da = None
    db = []
    for block, (off, size) in zip(blocks, spans):
        if da is not None:
            block, da = lax.optimization_barrier((block, da))
        dx_t = gathered_to_channels(block, r)
        part = jnp.einsum("cik,cij->ckj", a_t, dx_t, preferred_element_type=F32).astype(BF16)
        kept, sent = from_channels(part, n)
        db.append(reduce_rows(kept, sent, n))
        dx_t, sent = lax.optimization_barrier((dx_t, sent))
        b_t = slots_to_channels(b_slots, r, off, size)
        term = jnp.einsum("cij,ckj->cik", dx_t, b_t, preferred_element_type=F32)
        da = term if da is None else da + term
    return jnp.transpose(da.astype(BF16), (1, 2, 0)), db, spans


def shards(n_row, n_col, pair, product, mask, grad_out, weights, norms):
    rows, cols, c = pair.shape
    even = n_row == n_col and n_row & (n_row - 1) == 0 and cols % 32 == 0 and rows % 16 == 0
    size = 32 if even else cols
    spans = [(off, size) for off in range(0, cols, size)]
    pieces, chain = [], []
    for off, size in spans:
        dx, *chain = dx_chunk(pair, product, grad_out, weights, norms, off, size, chain)
        pieces.append(lax.all_gather(dx, "col", axis=0) if even else dx)
    dol, acc = chain
    valid = jnp.broadcast_to(mask.astype(BF16)[:, :, None], pair.shape)
    a, b_swapped, *gs = projections(pair, valid, weights, norms)
    if even:
        da, db, spans = triangles(n_row, pieces, spans, a, b_swapped)
    else:
        da, db, spans = triangles_plain(n_row, n_col, pieces[0], a, b_swapped)
    chain = []
    for (db0, db1), (off, size) in zip(db, spans):
        grad_pair, acc = final_chunk(
            pair, da, db0, db1, gs, dol, weights, norms, acc, off, size, chain
        )
        chain = [grad_pair]
    acc = sum_all(acc, n_row, n_col)
    return (grad_pair, acc[: 6 * c].reshape(6, c, c), acc[6 * c : 6 * c + 4])


def solution(mesh):
    in_specs = (
        P(("groups", "row"), "col", None),
        P(("groups", "row"), "col", None),
        P(("groups", "row"), "col"),
        P(("groups", "row"), "col", None),
        P(),
        P(),
    )
    out_specs = (P(("groups", "row"), "col", None), P("groups", None, None), P("groups", None))
    body = functools.partial(shards, mesh.shape["row"], mesh.shape["col"])
    return jax.shard_map(body, mesh=mesh, in_specs=in_specs, out_specs=out_specs, check_vma=False)
```

time: 1300 us -> 844 us (0.65)
  waiting for transfers between devices: 655 us -> 186 us
  Pallas kernels: 0 us -> 289 us
  other arithmetic: 203 us -> 67.8 us
  local copies, waits for them, and re-layouts: 214 us -> 151 us
  matrix products: 167 us -> 109 us
  blocking collectives: 33.1 us -> 0 us
  starting transfers between devices: 0.55 us -> 17.2 us
    all_gather x2 -> x5, waiting for transfers between devices: 482 us -> 0.01 us  [shards(): pieces.append(lax.all_gather(dx, 'col', axis=0) if even else dx)]
    pallas_call x0 -> x26, Pallas kernels: none -> 289 us  [the longest x10 72.4 us: to_channels(): pl.pallas_call(functools.partial(to_channels_kernel, slots), grid_spec=pl...]
    ppermute x0 -> x19, waiting for transfers between devices: none -> 186 us  [swap(): return lax.ppermute(v, axis, [(r, r ^ bit) for r in range(n)])]
    reduce_scatter x1 -> x0, waiting for transfers between devices: 137 us -> none  [shards(): lax.psum_scatter(jnp.einsum('ijc,ikc->jkc', block, a_proj, preferred_elem...]
    convert_element_type x6 -> x1, other arithmetic: 82 us -> 0.01 us  [shards(): valid = jnp.broadcast_to(mask.astype(BF16)[:, :, None], pair.shape)]
    all_gather x2 -> x0, local copies, waits for them, and re-layouts: 76.9 us -> none  [the longest x1 38.9 us: shards(): lax.all_gather(b_proj, 'row', axis=0, tiled=True)]
    dot_general x8 -> x10, matrix products: 167 us -> 109 us  [the longest x5 62.4 us: triangles(): term = jnp.einsum('cij,ckj->cik', dx_t, b_t, preferred_element_type=F32)]
    add x0 -> x7, other arithmetic: none -> 44.6 us  [the longest x3 44.5 us: triangles(): da = term if da is None else da + term]
  transfers between devices with their start and end apart: 4 -> 24, of which waited for: 4 -> 10; matrix products, arithmetic and copies ran while one was open for 15% -> 36% of each run, Pallas kernels for 0% -> 31%
where the time goes in v1:
time: 844 us; the launch traced here: 835 us
  Pallas kernels  289 us (34%)
  waiting for transfers between devices  186 us (22%)
  local copies, waits for them, and re-layouts  151 us (18%)
  matrix products  109 us (13%)
  other arithmetic  67.8 us (8%)
  starting transfers between devices  17.2 us (2%)
  between operations  14.3 us (2%)
    ppermute x19, waiting for transfers between devices, swap(): return lax.ppermute(v, axis, [(r, r ^ bit) for r in range(n)])  186 us
    dot_general x4, local copies, waits for them, and re-layouts, triangles(): term = jnp.einsum('cij,ckj->cik', dx_t, b_t, preferred_element_type=F32)  76.2 us
    pallas_call x10, Pallas kernels, to_channels(): pl.pallas_call(functools.partial(to_channels_kernel, slots), grid_spec=pl...  72.4 us
    pallas_call x5, Pallas kernels, dx_chunk(): pl.pallas_call(functools.partial(dx_kernel, step, bool(chain)), grid=(row...  68.8 us
    pallas_call x5, Pallas kernels, final_chunk(): pl.pallas_call(functools.partial(final_kernel, step, bool(chain)), grid=(...  68.3 us
    dot_general x5, matrix products, triangles(): term = jnp.einsum('cij,ckj->cik', dx_t, b_t, preferred_element_type=F32)  62.4 us
    dot_general x5, matrix products, triangles(): jnp.einsum('cik,cij->ckj', a_t, dx_t, preferred_element_type=F32)  46.6 us
    add x3, other arithmetic, triangles(): da = term if da is None else da + term  44.5 us
  transfers between devices with their start and end apart: 24, of which 10 were waited for; matrix products, arithmetic and copies ran while one was open for 36% of the time, Pallas kernels for 31%

profile of v1, /device:TPU:0, one launch (start us, length us, event | category | flops | bytes accessed | tf_op | source)
XLA Modules:
  0.0 835.4 jit_solution(6140097269330570702)
XLA Ops:
  8.8 13.8 %dx_part.5 = (bf16[160,32,128]{2,1,0:T(8,128)(2,1)}, bf16[160,160,128]{2,1,0:T(8,128)(2,1)}, f32[800,128]{1,0:T(8,128)S(1)}) custom-call(bf16[160,160,128]{2,1,0:T(8,128)(2,1)} %pair.21, bf16[160,160,128]{2,1,0:T(8,128)(2,1)} %product.9, bf16[160,160,128]{2,1,0:T(8,128)(2,1)} %go.9, bf16[6,128,128]{2,1,0:T(8,128)(2,1)S(1)} %copy-done.3, f32[4,128]{1,0:T(4,128)S(1)} %copy-done.21), custom_call_target="tpu_custom_call" | custom-call | flops 671088640 | bytes 6553600 | tf_op jit(solution)/shard_map/dx_part/pallas_call | solution.py:99
  22.7 13.8 %dx_part.6 = (bf16[160,32,128]{2,1,0:T(8,128)(2,1)}, bf16[160,160,128]{2,1,0:T(8,128)(2,1)}, f32[800,128]{1,0:T(8,128)S(1)}) custom-call(bf16[160,160,128]{2,1,0:T(8,128)(2,1)} %pair.21, bf16[160,160,128]{2,1,0:T(8,128)(2,1)} %product.9, bf16[160,160,128]{2,1,0:T(8,128)(2,1)} %go.9, ...), custom_call_target="tpu_custom_call", output_to_operand_aliasing={{1}: (5, {})} | custom-call | flops 671088640 | bytes 6553600 | tf_op jit(solution)/shard_map/dx_part/pallas_call | solution.py:99
  36.5 13.8 %dx_part.7 = (bf16[160,32,128]{2,1,0:T(8,128)(2,1)}, bf16[160,160,128]{2,1,0:T(8,128)(2,1)}, f32[800,128]{1,0:T(8,128)S(1)}) custom-call(bf16[160,160,128]{2,1,0:T(8,128)(2,1)} %pair.21, bf16[160,160,128]{2,1,0:T(8,128)(2,1)} %product.9, bf16[160,160,128]{2,1,0:T(8,128)(2,1)} %go.9, ...), custom_call_target="tpu_custom_call", output_to_operand_aliasing={{1}: (5, {})} | custom-call | flops 671088640 | bytes 6553600 | tf_op jit(solution)/shard_map/dx_part/pallas_call | solution.py:99
  56.6 38.1 %projections.1 = (bf16[160,160,128]{2,1,0:T(8,128)(2,1)}, bf16[160,160,128]{2,1,0:T(8,128)(2,1)}, bf16[160,160,128]{2,1,0:T(8,128)(2,1)}, bf16[160,160,128]{2,1,...) custom-call(bf16[160,160,128]{2,1,0:T(8,128)(2,1)} %pair.21, ...), custom_call_target="tpu_custom_call" | custom-call | flops 3355443200 | bytes 52428800 | tf_op jit(solution)/shard_map/projections/pallas_call | solution.py:152
  97.7 13.8 %dx_part.8 = (bf16[160,32,128]{2,1,0:T(8,128)(2,1)}, bf16[160,160,128]{2,1,0:T(8,128)(2,1)}, f32[800,128]{1,0:T(8,128)S(1)}) custom-call(bf16[160,160,128]{2,1,0:T(8,128)(2,1)} %pair.21, bf16[160,160,128]{2,1,0:T(8,128)(2,1)} %product.9, bf16[160,160,128]{2,1,0:T(8,128)(2,1)} %go.9, ...), custom_call_target="tpu_custom_call", output_to_operand_aliasing={{1}: (5, {})} | custom-call | flops 671088640 | bytes 6553600 | tf_op jit(solution)/shard_map/dx_part/pallas_call | solution.py:99
  111.6 127.5 %collective-permute-done.1.refs_2_ = bf16[160,160,128]{2,1,0:T(8,128)(2,1)} collective-permute-done((bf16[160,160,128]{2,1,0:T(8,128)(2,1)}, bf16[160,160,128]{2,1,0:T(8,128)(2,1)}, u32[]{:S(2)}, u32[]{:S(2)}) %collective-permute-start.1) | collective-permute-done | bytes 6553632 | tf_op jit(solution)/shard_map/ppermute | solution.py:299
  239.1 16.1 %copy.27 = bf16[128,160,160]{1,2,0:T(8,128)(2,1)} copy(bf16[128,160,160]{0,2,1:T(8,128)(2,1)} %bitcast.103) | data formatting | bytes 13107200 | tf_op jit(solution)/shard_map/transpose | solution.py:357
  282.8 13.7 %dx_part.9 = (bf16[160,32,128]{2,1,0:T(8,128)(2,1)S(1)}, bf16[160,160,128]{2,1,0:T(8,128)(2,1)}, f32[800,128]{1,0:T(8,128)S(1)}) custom-call(bf16[160,160,128]{2,1,0:T(8,128)(2,1)} %pair.21, bf16[160,160,128]{2,1,0:T(8,128)(2,1)} %product.9, bf16[160,160,128]{2,1,0:T(8,128)(2,1)} %go.9, ...), custom_call_target="tpu_custom_call", output_to_operand_aliasing={{1}: (5, {})} | custom-call | flops 671088640 | bytes 6553600 | tf_op jit(solution)/shard_map/dx_part/pallas_call | solution.py:99
  313.6 12.6 %fusion.6 = f32[128,160,160]{2,1,0:T(8,128)} fusion(bf16[128,160,128]{2,1,0:T(8,128)(2,1)S(1)} %bitcast.76, bf16[128,160,128]{2,1,0:T(8,128)(2,1)} %copy-done.7), kind=kOutput, calls=%fused_computation.33 | convolution fusion | flops 838860800 | bytes 23592960 | tf_op jit(solution)/shard_map/cij,ckj->cik/dot_general | solution.py:369
  355.2 19.0 %copy.29 = f32[128,160,160]{0,2,1:T(8,128)} copy(f32[128,160,160]{2,1,0:T(8,128)} %fusion.6) | data formatting | bytes 26214400 | tf_op jit(solution)/shard_map/optimization_barrier | solution.py:362
  396.6 19.0 %copy.30 = f32[128,160,160]{0,2,1:T(8,128)} copy(f32[128,160,160]{2,1,0:T(8,128)} %fusion.7) | data formatting | bytes 26214400 | tf_op jit(solution)/shard_map/cij,ckj->cik/dot_general | solution.py:369
  415.6 15.2 %add.64 = f32[128,160,160]{0,2,1:T(8,128)} add(f32[128,160,160]{0,2,1:T(8,128)} %copy.29, f32[128,160,160]{0,2,1:T(8,128)} %copy.30) | non-fusion elementwise | flops 3276800 | bytes 39321600 | tf_op jit(solution)/shard_map/add | solution.py:370
  479.8 19.2 %copy.32 = f32[128,160,160]{0,2,1:T(8,128)} copy(f32[128,160,160]{2,1,0:T(8,128)} %fusion.8) | data formatting | bytes 26214400 | tf_op jit(solution)/shard_map/cij,ckj->cik/dot_general | solution.py:369
  499.0 14.7 %add.65 = f32[128,160,160]{0,2,1:T(8,128)} add(f32[128,160,160]{0,2,1:T(8,128)} %add.64, f32[128,160,160]{0,2,1:T(8,128)} %copy.32) | non-fusion elementwise | flops 3276800 | bytes 39321600 | tf_op jit(solution)/shard_map/add | solution.py:370
  561.9 19.0 %copy.34 = f32[128,160,160]{0,2,1:T(8,128)} copy(f32[128,160,160]{2,1,0:T(8,128)} %fusion.9) | data formatting | bytes 26214400 | tf_op jit(solution)/shard_map/cij,ckj->cik/dot_general | solution.py:369
  580.9 14.7 %add.66 = f32[128,160,160]{0,2,1:T(8,128)} add(f32[128,160,160]{0,2,1:T(8,128)} %add.65, f32[128,160,160]{0,2,1:T(8,128)} %copy.34) | non-fusion elementwise | flops 3276800 | bytes 39321600 | tf_op jit(solution)/shard_map/add | solution.py:370
  644.6 19.0 %copy.36 = f32[128,160,160]{0,2,1:T(8,128)} copy(f32[128,160,160]{2,1,0:T(8,128)} %fusion.10) | data formatting | bytes 26214400 | tf_op jit(solution)/shard_map/cij,ckj->cik/dot_general | solution.py:369
  693.3 13.8 %final_part.5 = (bf16[160,160,128]{2,1,0:T(8,128)(2,1)}, f32[800,128]{1,0:T(8,128)S(1)}) custom-call(bf16[160,160,128]{2,1,0:T(8,128)(2,1)} %pair.21, bf16[160,160,128]{2,1,0:T(8,128)(2,1)} %fusion.da, bf16[160,32,128]{2,1,0:T(8,128)(2,1)S(1)} %get-tuple-element.112.db0, bf16[160,32,128]{2,1,0:T(8,128)(2,1)} %bitcast.27.db1, ...), custom_call_target="tpu_custom_call" | custom-call | flops 1677721600 | bytes 14417920 | tf_op jit(solution)/shard_map/final_part/pallas_call | solution.py:276
  707.1 13.6 %final_part.6 = (bf16[160,160,128]{2,1,0:T(8,128)(2,1)}, f32[800,128]{1,0:T(8,128)S(1)}) custom-call(bf16[160,160,128]{2,1,0:T(8,128)(2,1)} %pair.21, bf16[160,160,128]{2,1,0:T(8,128)(2,1)} %fusion.da, bf16[160,32,128]{2,1,0:T(8,128)(2,1)S(1)} %get-tuple-element.114.db0, bf16[160,32,128]{2,1,0:T(8,128)(2,1)S(1)} %bitcast.77, ...), custom_call_target="tpu_custom_call", output_to_operand_aliasing={{0}: (12, {})} | custom-call | flops 1677721600 | bytes 14417920 | tf_op jit(solution)/shard_map/final_part/pallas_call | solution.py:276
  728.4 13.6 %final_part.7 = (bf16[160,160,128]{2,1,0:T(8,128)(2,1)}, f32[800,128]{1,0:T(8,128)S(1)}) custom-call(bf16[160,160,128]{2,1,0:T(8,128)(2,1)} %pair.21, bf16[160,160,128]{2,1,0:T(8,128)(2,1)} %fusion.da, bf16[160,32,128]{2,1,0:T(8,128)(2,1)S(1)} %get-tuple-element.116.db0, bf16[160,32,128]{2,1,0:T(8,128)(2,1)S(1)} %bitcast.78, ...), custom_call_target="tpu_custom_call", output_to_operand_aliasing={{0}: (12, {})} | custom-call | flops 1677721600 | bytes 14417920 | tf_op jit(solution)/shard_map/final_part/pallas_call | solution.py:276
  742.0 14.5 %collective-permute-done.6 = bf16[1,160,32,128]{3,2,1,0:T(8,128)(2,1)S(1)} collective-permute-done((bf16[1,160,32,128]{3,2,1,0:T(8,128)(2,1)}, bf16[1,160,32,128]{3,2,1,0:T(8,128)(2,1)S(1)}, u32[]{:S(2)}, u32[]{:S(2)}) %collective-permute-start.6) | collective-permute-done | bytes 1310752 | tf_op jit(solution)/shard_map/ppermute | solution.py:299
  756.5 13.7 %final_part.8 = (bf16[160,160,128]{2,1,0:T(8,128)(2,1)}, f32[800,128]{1,0:T(8,128)S(1)}) custom-call(bf16[160,160,128]{2,1,0:T(8,128)(2,1)} %pair.21, bf16[160,160,128]{2,1,0:T(8,128)(2,1)} %fusion.da, bf16[160,32,128]{2,1,0:T(8,128)(2,1)S(1)} %get-tuple-element.118.db0, bf16[160,32,128]{2,1,0:T(8,128)(2,1)S(1)} %bitcast.80, ...), custom_call_target="tpu_custom_call", output_to_operand_aliasing={{0}: (12, {})} | custom-call | flops 1677721600 | bytes 14417920 | tf_op jit(solution)/shard_map/final_part/pallas_call | solution.py:276
  770.2 13.5 %collective-permute-done.4 = bf16[1,160,32,128]{3,2,1,0:T(8,128)(2,1)S(1)} collective-permute-done((bf16[1,160,32,128]{3,2,1,0:T(8,128)(2,1)S(1)}, bf16[1,160,32,128]{3,2,1,0:T(8,128)(2,1)S(1)}, u32[]{:S(2)}, u32[]{:S(2)}) %collective-permute-start.4) | collective-permute-done | bytes 1310752 | tf_op jit(solution)/shard_map/ppermute | solution.py:299
  783.7 13.6 %final_part.9 = (bf16[160,160,128]{2,1,0:T(8,128)(2,1)}, f32[800,128]{1,0:T(8,128)S(1)}) custom-call(bf16[160,160,128]{2,1,0:T(8,128)(2,1)} %pair.21, bf16[160,160,128]{2,1,0:T(8,128)(2,1)} %fusion.da, bf16[160,32,128]{2,1,0:T(8,128)(2,1)S(1)} %get-tuple-element.120.db0, bf16[160,32,128]{2,1,0:T(8,128)(2,1)S(1)} %bitcast.79, ...), custom_call_target="tpu_custom_call", output_to_operand_aliasing={{0}: (12, {})} | custom-call | flops 1677721600 | bytes 14417920 | tf_op jit(solution)/shard_map/final_part/pallas_call | solution.py:276
  (159 shorter events, 321.9 us)
Async XLA Ops:
  7.2 248.1 %all-gather.19.cloned.1.call-start = ((), (), s32[]{:S(2)}) async-start(), calls=%async_computation.4 | async-start | bytes 6553600 | tf_op jit(solution)/shard_map/all_gather | solution.py:382
  22.6 303.6 %all-gather.17.cloned.1.call-start = ((), (), s32[]{:S(2)}) async-start(), calls=%async_computation.3 | async-start | bytes 6553600 | tf_op jit(solution)/shard_map/all_gather | solution.py:382
  36.5 394.3 %all-gather.15.cloned.1.call-start = ((), (), s32[]{:S(2)}) async-start(), calls=%async_computation.2 | async-start | bytes 6553600 | tf_op jit(solution)/shard_map/all_gather | solution.py:382
  50.4 463.3 %all-gather.13.cloned.1.call-start = ((), (), s32[]{:S(2)}) async-start(), calls=%async_computation.1 | async-start | bytes 6553600 | tf_op jit(solution)/shard_map/all_gather | solution.py:382
  94.8 144.4 %collective-permute-start.1 = (bf16[160,160,128]{2,1,0:T(8,128)(2,1)}, bf16[160,160,128]{2,1,0:T(8,128)(2,1)}, u32[]{:S(2)}, u32[]{:S(2)}) collective-permute-start(bf16[160,160,128]{2,1,0:T(8,128)(2,1)} %get-tuple-element.73.refs_0_), channel_id=1, source_target_pairs={{0,8},{4,12},{8,0},{12,4},{1,9},{5,13},{9,1},{13,5},{2,10},{6,14},... | collective-permute-start | bytes 19660808 | tf_op jit(solution)/shard_map/ppermute | solution.py:299
  111.5 484.1 %all-gather.11.cloned.1.call-start = ((), (), s32[]{:S(2)}) async-start(), calls=%async_computation | async-start | bytes 6553600 | tf_op jit(solution)/shard_map/all_gather | solution.py:382
  111.5 192.6 %collective-permute-start = (bf16[160,160,128]{2,1,0:T(8,128)(2,1)}, bf16[160,160,128]{2,1,0:T(8,128)(2,1)}, u32[]{:S(2)}, u32[]{:S(2)}) collective-permute-start(bf16[160,160,128]{2,1,0:T(8,128)(2,1)} %get-tuple-element.73.refs_0_), channel_id=1, source_target_pairs={{0,4},{4,0},{8,12},{12,8},{1,5},{5,1},{9,13},{13,9},{2,6},{6,2},{1... | collective-permute-start | bytes 19660808 | tf_op jit(solution)/shard_map/ppermute | solution.py:299
  239.1 65.0 %collective-permute-start.2 = (bf16[160,160,128]{2,1,0:T(8,128)(2,1)}, bf16[160,160,128]{2,1,0:T(8,128)(2,1)}, u32[]{:S(2)}, u32[]{:S(2)}) collective-permute-start(bf16[160,160,128]{2,1,0:T(8,128)(2,1)} %collective-permute-done.1.refs_2_), channel_id=1, source_target_pairs={{0,4},{4,0},{8,12},{12,8},{1,5},{5,1},{9,13},{13,9},{2,6},{6,2},{1... | collective-permute-start | bytes 19660808 | tf_op jit(solution)/shard_map/ppermute | solution.py:299
  282.4 16.1 %collective-permute-start.11 = (bf16[2,160,32,128]{3,2,1,0:T(8,128)(2,1)}, bf16[2,160,32,128]{3,2,1,0:T(8,128)(2,1)}, u32[]{:S(2)}, u32[]{:S(2)}) collective-permute-start(bf16[2,160,32,128]{3,2,1,0:T(8,128)(2,1)} %get-tuple-element.71), channel_id=1, source_target_pairs={{0,4},{4,0},{8,12},{12,8},{1,5},{5,1},{9,13},{13,9},{2,6},{6,2},{1... | collective-permute-start | bytes 7864328 | tf_op jit(solution)/shard_map/ppermute | solution.py:299
  302.4 390.9 %collective-permute-start.12 = (bf16[1,160,32,128]{3,2,1,0:T(8,128)(2,1)}, bf16[1,160,32,128]{3,2,1,0:T(8,128)(2,1)}, u32[]{:S(2)}, u32[]{:S(2)}) collective-permute-start(bf16[1,160,32,128]{3,2,1,0:T(8,128)(2,1)} %get-tuple-element.111), channel_id=1, source_target_pairs={{0,8},{4,12},{8,0},{12,4},{1,9},{5,13},{9,1},{13,5},{2,10},{6,14},... | collective-permute-start | bytes 3932168 | tf_op jit(solution)/shard_map/ppermute | solution.py:299
  355.2 308.4 %collective-permute-start.9 = (bf16[2,160,32,128]{3,2,1,0:T(8,128)(2,1)}, bf16[2,160,32,128]{3,2,1,0:T(8,128)(2,1)}, u32[]{:S(2)}, u32[]{:S(2)}) collective-permute-start(bf16[2,160,32,128]{3,2,1,0:T(8,128)(2,1)} %get-tuple-element.76), channel_id=1, source_target_pairs={{0,4},{4,0},{8,12},{12,8},{1,5},{5,1},{9,13},{13,9},{2,6},{6,2},{1... | collective-permute-start | bytes 7864328 | tf_op jit(solution)/shard_map/ppermute | solution.py:299
  457.2 211.4 %collective-permute-start.7 = (bf16[2,160,32,128]{3,2,1,0:T(8,128)(2,1)}, bf16[2,160,32,128]{3,2,1,0:T(8,128)(2,1)}, u32[]{:S(2)}, u32[]{:S(2)}) collective-permute-start(bf16[2,160,32,128]{3,2,1,0:T(8,128)(2,1)} %get-tuple-element.80), channel_id=1, source_target_pairs={{0,4},{4,0},{8,12},{12,8},{1,5},{5,1},{9,13},{13,9},{2,6},{6,2},{1... | collective-permute-start | bytes 7864328 | tf_op jit(solution)/shard_map/ppermute | solution.py:299
  539.9 134.7 %collective-permute-start.5 = (bf16[2,160,32,128]{3,2,1,0:T(8,128)(2,1)}, bf16[2,160,32,128]{3,2,1,0:T(8,128)(2,1)}, u32[]{:S(2)}, u32[]{:S(2)}) collective-permute-start(bf16[2,160,32,128]{3,2,1,0:T(8,128)(2,1)} %get-tuple-element.84), channel_id=1, source_target_pairs={{0,4},{4,0},{8,12},{12,8},{1,5},{5,1},{9,13},{13,9},{2,6},{6,2},{1... | collective-permute-start | bytes 7864328 | tf_op jit(solution)/shard_map/ppermute | solution.py:299
  622.2 56.6 %collective-permute-start.3 = (bf16[2,160,32,128]{3,2,1,0:T(8,128)(2,1)}, bf16[2,160,32,128]{3,2,1,0:T(8,128)(2,1)}, u32[]{:S(2)}, u32[]{:S(2)}) collective-permute-start(bf16[2,160,32,128]{3,2,1,0:T(8,128)(2,1)} %get-tuple-element.88), channel_id=1, source_target_pairs={{0,4},{4,0},{8,12},{12,8},{1,5},{5,1},{9,13},{13,9},{2,6},{6,2},{1... | collective-permute-start | bytes 7864328 | tf_op jit(solution)/shard_map/ppermute | solution.py:299
  668.5 38.6 %collective-permute-start.10 = (bf16[1,160,32,128]{3,2,1,0:T(8,128)(2,1)}, bf16[1,160,32,128]{3,2,1,0:T(8,128)(2,1)S(1)}, u32[]{:S(2)}, u32[]{:S(2)}) collective-permute-start(bf16[1,160,32,128]{3,2,1,0:T(8,128)(2,1)} %get-tuple-element.113), channel_id=1, source_target_pairs={{0,8},{4,12},{8,0},{12,4},{1,9},{5,13},{9,1},{13,5},{2,10},{6,14},... | collective-permute-start | bytes 3932168 | tf_op jit(solution)/shard_map/ppermute | solution.py:299
  672.6 55.8 %collective-permute-start.8 = (bf16[1,160,32,128]{3,2,1,0:T(8,128)(2,1)}, bf16[1,160,32,128]{3,2,1,0:T(8,128)(2,1)S(1)}, u32[]{:S(2)}, u32[]{:S(2)}) collective-permute-start(bf16[1,160,32,128]{3,2,1,0:T(8,128)(2,1)} %get-tuple-element.115), channel_id=1, source_target_pairs={{0,8},{4,12},{8,0},{12,4},{1,9},{5,13},{9,1},{13,5},{2,10},{6,14},... | collective-permute-start | bytes 3932168 | tf_op jit(solution)/shard_map/ppermute | solution.py:299
  678.7 77.8 %collective-permute-start.6 = (bf16[1,160,32,128]{3,2,1,0:T(8,128)(2,1)}, bf16[1,160,32,128]{3,2,1,0:T(8,128)(2,1)S(1)}, u32[]{:S(2)}, u32[]{:S(2)}) collective-permute-start(bf16[1,160,32,128]{3,2,1,0:T(8,128)(2,1)} %get-tuple-element.117), channel_id=1, source_target_pairs={{0,8},{4,12},{8,0},{12,4},{1,9},{5,13},{9,1},{13,5},{2,10},{6,14},... | collective-permute-start | bytes 3932168 | tf_op jit(solution)/shard_map/ppermute | solution.py:299
  682.0 101.7 %collective-permute-start.4 = (bf16[1,160,32,128]{3,2,1,0:T(8,128)(2,1)S(1)}, bf16[1,160,32,128]{3,2,1,0:T(8,128)(2,1)S(1)}, u32[]{:S(2)}, u32[]{:S(2)}) collective-permute-start(bf16[1,160,32,128]{3,2,1,0:T(8,128)(2,1)S(1)} %get-tuple-element.119), channel_id=1, source_target_pairs={{0,8},{4,12},{8,0},{12,4},{1,9},{5,13},{9,1},{13,5},{2,10},{6,14},... | collective-permute-start | bytes 3932168 | tf_op jit(solution)/shard_map/ppermute | solution.py:299
  797.3 1.7 collective-permute-start.13
  799.1 7.2 collective-permute-start.14
  806.3 4.7 collective-permute-start.15
  811.1 5.6 collective-permute-start.16
  816.7 4.7 collective-permute-start.17
  821.5 5.8 collective-permute-start.18
  (30 other events, 171.3 us)
Sparse Core Ops, SparseCore 0:
  22.7 100.7 all-gather.18
  125.1 96.5 all-gather.16
  223.3 96.4 all-gather.14
  321.2 96.4 all-gather.12
  419.1 96.4 all-gather.10

commit v2 on v1

--- a/solution.py
+++ b/solution.py
@@ -4,6 +4,7 @@
 import jax.numpy as jnp
 from jax import lax
 from jax.experimental import pallas as pl
+from jax.experimental.layout import Layout, with_layout_constraint
 from jax.experimental.pallas import tpu as pltpu
 from jax.sharding import PartitionSpec as P
 
@@ -15,6 +16,10 @@
 
 def dot(x, y):
     return jnp.dot(x, y, preferred_element_type=F32)
+
+
+def sigmoid(x):
+    return 0.5 * jnp.tanh(0.5 * x) + 0.5
 
 
 def dot_t(x, y):
@@ -68,7 +73,7 @@
     def body(s, carry):
         hat, _ = layer_normalize(tile(pair, s, step).astype(F32))
         zn = (hat * norms[0:1] + norms[1:2]).astype(BF16)
-        og = jax.nn.sigmoid(dot(zn, w[4]))
+        og = sigmoid(dot(zn, w[4]))
         xhat, inv2 = layer_normalize(tile(product, s, step).astype(F32))
         xn = (xhat * norms[2:3] + norms[3:4]).astype(BF16)
         y = dot(xn, w[5])
@@ -89,7 +94,7 @@
     rows, cols, c = pair.shape
     jb = 16 if size % 16 == 0 else size
     ib = 80 if rows % 80 == 0 else rows // 2 if rows % 2 == 0 else rows
-    step = 16 if ib % 16 == 0 else ib
+    step = 40 if ib % 40 == 0 else ib
     base = off // jb
     blk = pl.BlockSpec((ib, jb, c), lambda i, j: (i, base + j, 0))
     out = pl.BlockSpec((ib, jb, c), lambda i, j: (i, j, 0))
@@ -124,7 +129,7 @@
         zn = (hat * norms[0:1] + norms[1:2]).astype(BF16)
         m = tile(valid, s, step).astype(F32)
         for at, d_gate, d_value in ((0, g_ga, g_pa), (2, g_gb, g_pb)):
-            gate = jax.nn.sigmoid(dot(zn, w[at]))
+            gate = sigmoid(dot(zn, w[at]))
             p = dot(zn, w[at + 1])
             mg = m * gate
             mgp = mg * p
@@ -143,7 +148,7 @@
 def projections(pair, valid, weights, norms):
     rows, cols, c = pair.shape
     ib = 16 if rows % 16 == 0 else rows
-    step = 2
+    step = ib
     blk = pl.BlockSpec((ib, cols, c), lambda i: (i, 0, 0))
     swapped = pl.BlockSpec((cols, ib, c), lambda i: (0, i, 0))
     full = lambda shape: pl.BlockSpec(shape, lambda i: (0,) * len(shape))
@@ -190,10 +195,10 @@
     )(r, *arrays)
 
 
-def gathered_to_channels(g, r):
-    n, rows, size, c = g.shape
+def gathered_to_channels(g, r, at, size):
+    n, rows, _, c = g.shape
     specs = [
-        pl.BlockSpec((1, 16, size, c), lambda i, r, t=t: (r[0] ^ t, i, 0, 0)) for t in range(n)
+        pl.BlockSpec((1, 16, size, c), lambda i, r, t=t: (r[0] ^ t, i, at, 0)) for t in range(n)
     ]
     return to_channels([g] * n, specs, r, rows, size, c)
 
@@ -229,7 +234,7 @@
     )(x)
 
 
-def final_kernel(step, chained, pair, da, db0, db1, g_ga, g_pa, g_gb, g_pb, dol, w, norms, acc_in, *rest):
+def final_kernel(step, chained, pair, da, db0, db1, g_ga, g_pa, g_gb, g_pb, dol, wcat, norms, acc_in, *rest):
     gp, acc, flip = rest[-3:]
     c = pair.shape[-1]
 
@@ -251,12 +256,12 @@
             (dbv * tile(g_pb, s, step).astype(F32)).astype(BF16),
             tile(dol, s, step),
         ]
-        dzn = dot_t(parts[0], w[0])
-        for at in range(1, 5):
-            dzn = dzn + dot_t(parts[at], w[at])
+        cat = jnp.concatenate(parts, axis=1)
+        dzn = dot_t(cat, wcat[...])
         put(gp, s, step, layer_norm_backward(dzn * norms[0:1], hat, inv))
+        grads = t_dot(zn, cat)
         for at in range(5):
-            acc[at * c : (at + 1) * c] += t_dot(zn, parts[at])
+            acc[at * c : (at + 1) * c] += grads[:, at * c : (at + 1) * c]
         acc[6 * c : 6 * c + 1] += jnp.sum(dzn * hat, axis=0, keepdims=True)
         acc[6 * c + 1 : 6 * c + 2] += jnp.sum(dzn, axis=0, keepdims=True)
         return carry
@@ -264,10 +269,10 @@
     lax.fori_loop(0, pair.shape[0] // step, body, 0)
 
 
-def final_chunk(pair, da, db0, db1, gs, dol, weights, norms, acc, off, size, chain):
+def final_chunk(pair, da, db0, db1, gs, dol, wcat, norms, acc, off, size, chain):
     rows, cols, c = pair.shape
     ib = 16 if size % 16 == 0 else size
-    step = 2
+    step = ib
     base = off // ib
     blk = pl.BlockSpec((ib, cols, c), lambda i: (base + i, 0, 0))
     own = pl.BlockSpec((cols, ib, c), lambda i: (0, i, 0))
@@ -278,7 +283,7 @@
         grid=(size // ib,),
         in_specs=[blk, blk, own, own]
         + [blk] * 5
-        + [full(weights.shape), full(norms.shape), full(acc.shape)]
+        + [full(wcat.shape), full(norms.shape), full(acc.shape)]
         + ([pl.BlockSpec(memory_space=pl.ANY)] if chain else []),
         out_specs=[blk, full(acc.shape)],
         out_shape=[
@@ -292,7 +297,7 @@
             flops=20 * n * c * c, bytes_accessed=22 * n * c, transcendentals=n
         ),
         name="final_part",
-    )(pair, da, db0, db1, *gs, dol, weights, norms, acc, *chain)
+    )(pair, da, db0, db1, *gs, dol, wcat, norms, acc, *chain)
 
 
 def swap(v, axis, n, bit):
@@ -351,46 +356,60 @@
     return da.astype(BF16), [(db, jnp.zeros_like(db))], [(0, rows)]
 
 
-def triangles(n, blocks, spans, a, b_swapped):
+def triangles(n, groups, size, a, b_swapped):
     r = lax.axis_index("row").astype(jnp.int32).reshape(1)
     b_slots = gather_rows(b_swapped, n)
     a_t = jnp.transpose(a, (2, 0, 1))
+    major = Layout(major_to_minor=(0, 1, 2))
     da = None
-    db = []
-    for block, (off, size) in zip(blocks, spans):
-        if da is not None:
-            block, da = lax.optimization_barrier((block, da))
-        dx_t = gathered_to_channels(block, r)
-        part = jnp.einsum("cik,cij->ckj", a_t, dx_t, preferred_element_type=F32).astype(BF16)
-        kept, sent = from_channels(part, n)
-        db.append(reduce_rows(kept, sent, n))
-        dx_t, sent = lax.optimization_barrier((dx_t, sent))
-        b_t = slots_to_channels(b_slots, r, off, size)
-        term = jnp.einsum("cij,ckj->cik", dx_t, b_t, preferred_element_type=F32)
-        da = term if da is None else da + term
-    return jnp.transpose(da.astype(BF16), (1, 2, 0)), db, spans
+    db, spans = [], []
+    for group in groups:
+        for at in range(group.shape[2] // size):
+            off = len(spans) * size
+            if da is not None:
+                group, da = lax.optimization_barrier((group, da))
+            dx_t = gathered_to_channels(group, r, at, size)
+            part = jnp.einsum("cik,cij->ckj", a_t, dx_t, preferred_element_type=F32).astype(BF16)
+            kept, sent = from_channels(part, n)
+            db.append(reduce_rows(kept, sent, n))
+            if da is None:
+                dx_t, sent, *b_slots = lax.optimization_barrier((dx_t, sent, *b_slots))
+            else:
+                dx_t, sent = lax.optimization_barrier((dx_t, sent))
+            b_t = slots_to_channels(b_slots, r, off, size)
+            term = jnp.einsum("cij,ckj->cik", dx_t, b_t, preferred_element_type=F32)
+            da = with_layout_constraint(term if da is None else da + term, major)
+            spans.append((off, size))
+    da = with_layout_constraint(da.astype(BF16), major)
+    return jnp.transpose(da, (1, 2, 0)), db, spans
 
 
 def shards(n_row, n_col, pair, product, mask, grad_out, weights, norms):
     rows, cols, c = pair.shape
     even = n_row == n_col and n_row & (n_row - 1) == 0 and cols % 32 == 0 and rows % 16 == 0
     size = 32 if even else cols
-    spans = [(off, size) for off in range(0, cols, size)]
-    pieces, chain = [], []
-    for off, size in spans:
-        dx, *chain = dx_chunk(pair, product, grad_out, weights, norms, off, size, chain)
-        pieces.append(lax.all_gather(dx, "col", axis=0) if even else dx)
+    widths = [size] * (cols // size)
+    if len(widths) > 3:
+        widths[1:3] = [2 * size]
+    groups, chain, off = [], [], 0
+    for width in widths:
+        dx, *chain = dx_chunk(pair, product, grad_out, weights, norms, off, width, chain)
+        groups.append(lax.all_gather(dx, "col", axis=0) if even else dx)
+        if off == 0:
+            valid = jnp.broadcast_to(mask.astype(BF16)[:, :, None], pair.shape)
+            a, b_swapped, *gs = projections(pair, valid, weights, norms)
+            chain[1], b_swapped = lax.optimization_barrier((chain[1], b_swapped))
+        off += width
     dol, acc = chain
-    valid = jnp.broadcast_to(mask.astype(BF16)[:, :, None], pair.shape)
-    a, b_swapped, *gs = projections(pair, valid, weights, norms)
     if even:
-        da, db, spans = triangles(n_row, pieces, spans, a, b_swapped)
+        da, db, spans = triangles(n_row, groups, size, a, b_swapped)
     else:
-        da, db, spans = triangles_plain(n_row, n_col, pieces[0], a, b_swapped)
+        da, db, spans = triangles_plain(n_row, n_col, groups[0], a, b_swapped)
+    wcat = jnp.transpose(weights[:5], (1, 0, 2)).reshape(c, 5 * c)
     chain = []
     for (db0, db1), (off, size) in zip(db, spans):
         grad_pair, acc = final_chunk(
-            pair, da, db0, db1, gs, dol, weights, norms, acc, off, size, chain
+            pair, da, db0, db1, gs, dol, wcat, norms, acc, off, size, chain
         )
         chain = [grad_pair]
     acc = sum_all(acc, n_row, n_col)

time: 844 us -> 728 us (0.86)
  local copies, waits for them, and re-layouts: 151 us -> 65 us
  Pallas kernels: 289 us -> 220 us
  waiting for transfers between devices: 186 us -> 253 us
  other arithmetic: 67.8 us -> 15.4 us
  matrix products: 109 us -> 138 us
    dot_general x4 -> x0, local copies, waits for them, and re-layouts: 76.2 us -> none  [triangles(): term = jnp.einsum('cij,ckj->cik', dx_t, b_t, preferred_element_type=F32)]
    all_gather x5 -> x4, waiting for transfers between devices: 0.01 us -> 46.1 us  [shards(): groups.append(lax.all_gather(dx, 'col', axis=0) if even else dx)]
    add x3 -> x0, other arithmetic: 44.5 us -> none  [triangles(): da = term if da is None else da + term]
    pallas_call x5 -> x4, Pallas kernels: 68.8 us -> 40.2 us  [dx_chunk(): pl.pallas_call(functools.partial(dx_kernel, step, bool(chain)), grid=(row...]
    pallas_call x5, Pallas kernels: 68.3 us -> 42.1 us  [final_chunk(): pl.pallas_call(functools.partial(final_kernel, step, bool(chain)), grid=(...]
    dot_general x5, matrix products: 62.4 us -> 86.2 us  [triangles(): term = jnp.einsum('cij,ckj->cik', dx_t, b_t, preferred_element_type=F32)]
    ppermute x19, waiting for transfers between devices: 186 us -> 207 us  [swap(): return lax.ppermute(v, axis, [(r, r ^ bit) for r in range(n)])]
    optimization_barrier x1 -> x0, local copies, waits for them, and re-layouts: 19 us -> none  [triangles(): block, da = lax.optimization_barrier((block, da))]
  transfers between devices with their start and end apart: 24 -> 23, of which waited for: 10 -> 11; matrix products, arithmetic and copies ran while one was open for 36% -> 28% of each run, Pallas kernels for 31% -> 28%
where the time goes in v2:
time: 728 us; the launch traced here: 720 us
  waiting for transfers between devices  253 us (35%)
  Pallas kernels  220 us (30%)
  matrix products  138 us (19%)
  local copies, waits for them, and re-layouts  65 us (9%)
  other arithmetic  15.4 us (2%)
  between operations  14.4 us (2%)
  starting transfers between devices  13.8 us (2%)
    ppermute x19, waiting for transfers between devices, swap(): return lax.ppermute(v, axis, [(r, r ^ bit) for r in range(n)])  207 us
    dot_general x5, matrix products, triangles(): term = jnp.einsum('cij,ckj->cik', dx_t, b_t, preferred_element_type=F32)  86.2 us
    pallas_call x10, Pallas kernels, to_channels(): pl.pallas_call(functools.partial(to_channels_kernel, slots), grid_spec=pl...  72.8 us
    dot_general x5, matrix products, triangles(): jnp.einsum('cik,cij->ckj', a_t, dx_t, preferred_element_type=F32)  52.1 us
    all_gather x4, waiting for transfers between devices, shards(): groups.append(lax.all_gather(dx, 'col', axis=0) if even else dx)  46.1 us
    pallas_call x5, Pallas kernels, final_chunk(): pl.pallas_call(functools.partial(final_kernel, step, bool(chain)), grid=(...  42.1 us
    pallas_call x5, Pallas kernels, from_channels(): pl.pallas_call(functools.partial(from_channels_kernel, slots), grid=(lead...  41.4 us
    pallas_call x4, Pallas kernels, dx_chunk(): pl.pallas_call(functools.partial(dx_kernel, step, bool(chain)), grid=(row...  40.2 us
  transfers between devices with their start and end apart: 23, of which 11 were waited for; matrix products, arithmetic and copies ran while one was open for 28% of the time, Pallas kernels for 28%

profile of v2, /device:TPU:0, one launch (start us, length us, event | category | flops | bytes accessed | tf_op | source)
XLA Modules:
  0.0 719.7 jit_solution(15951103074121886650)
XLA Ops:
  8.8 8.4 %dx_part.4 = (bf16[160,32,128]{2,1,0:T(8,128)(2,1)}, bf16[160,160,128]{2,1,0:T(8,128)(2,1)}, f32[800,128]{1,0:T(8,128)S(1)}) custom-call(bf16[160,160,128]{2,1,0:T(8,128)(2,1)} %pair.19, bf16[160,160,128]{2,1,0:T(8,128)(2,1)} %product.7, bf16[160,160,128]{2,1,0:T(8,128)(2,1)} %go.7, bf16[6,128,128]{2,1,0:T(8,128)(2,1)S(1)} %copy-done.9, f32[4,128]{1,0:T(4,128)S(1)} %copy-done.24), custom_call_target="tpu_custom_call" | custom-call | flops 671088640 | bytes 6553600 | tf_op jit(solution)/shard_map/dx_part/pallas_call | solution.py:104
  23.5 23.6 %projections.1 = (bf16[160,160,128]{2,1,0:T(8,128)(2,1)}, bf16[160,160,128]{2,1,0:T(8,128)(2,1)}, bf16[160,160,128]{2,1,0:T(8,128)(2,1)}, bf16[160,160,128]{2,1,...) custom-call(bf16[160,160,128]{2,1,0:T(8,128)(2,1)} %pair.19, ...), custom_call_target="tpu_custom_call" | custom-call | flops 3355443200 | bytes 52428800 | tf_op jit(solution)/shard_map/projections/pallas_call | solution.py:157
  47.2 14.9 %dx_part.5 = (bf16[160,64,128]{2,1,0:T(8,128)(2,1)}, bf16[160,160,128]{2,1,0:T(8,128)(2,1)}, f32[800,128]{1,0:T(8,128)S(1)}) custom-call(bf16[160,160,128]{2,1,0:T(8,128)(2,1)} %pair.19, bf16[160,160,128]{2,1,0:T(8,128)(2,1)} %product.7, bf16[160,160,128]{2,1,0:T(8,128)(2,1)} %go.7, ...), custom_call_target="tpu_custom_call", output_to_operand_aliasing={{1}: (5, {})} | custom-call | flops 1342177280 | bytes 13107200 | tf_op jit(solution)/shard_map/dx_part/pallas_call | solution.py:104
  73.8 132.8 %collective-permute-done.1.refs_2_ = bf16[160,160,128]{2,1,0:T(8,128)(2,1)} collective-permute-done((bf16[160,160,128]{2,1,0:T(8,128)(2,1)}, bf16[160,160,128]{2,1,0:T(8,128)(2,1)}, u32[]{:S(2)}, u32[]{:S(2)}) %collective-permute-start.1) | collective-permute-done | bytes 6553632 | tf_op jit(solution)/shard_map/ppermute | solution.py:304
  206.6 8.5 %dx_part.7 = (bf16[160,32,128]{2,1,0:T(8,128)(2,1)}, bf16[160,160,128]{2,1,0:T(8,128)(2,1)}, f32[800,128]{1,0:T(8,128)S(1)}) custom-call(bf16[160,160,128]{2,1,0:T(8,128)(2,1)} %pair.19, bf16[160,160,128]{2,1,0:T(8,128)(2,1)} %product.7, bf16[160,160,128]{2,1,0:T(8,128)(2,1)} %go.7, ...), custom_call_target="tpu_custom_call", output_to_operand_aliasing={{1}: (5, {})} | custom-call | flops 671088640 | bytes 6553600 | tf_op jit(solution)/shard_map/dx_part/pallas_call | solution.py:104
  215.9 15.6 %copy.35 = bf16[128,160,160]{1,2,0:T(8,128)(2,1)} copy(bf16[128,160,160]{0,2,1:T(8,128)(2,1)} %bitcast.101) | data formatting | bytes 13107200 | tf_op jit(solution)/shard_map/transpose | solution.py:362
  239.1 9.4 %convolution_convert_fusion.4.x = bf16[128,160,128]{2,1,0:T(8,128)(2,1)} fusion(bf16[128,160,160]{1,2,0:T(8,128)(2,1)} %copy.35, bf16[128,160,128]{2,1,0:T(8,128)(2,1)S(1)} %to_channels.10), kind=kOutput, calls=%fused_computation.13 | convolution fusion | flops 841482240 | bytes 17039360 | tf_op jit(solution)/shard_map/cik,cij->ckj/dot_general | solution.py:372
  266.7 12.4 %fusion.5 = f32[128,160,160]{2,1,0:T(8,128)} fusion(bf16[128,160,128]{2,1,0:T(8,128)(2,1)S(1)} %to_channels.10, bf16[128,160,128]{2,1,0:T(8,128)(2,1)} %copy-done.8), kind=kOutput, calls=%fused_computation.35 | convolution fusion | flops 838860800 | bytes 23592960 | tf_op jit(solution)/shard_map/cij,ckj->cik/dot_general | solution.py:380
  315.0 11.1 %convolution_convert_fusion.3.x = bf16[128,160,128]{2,1,0:T(8,128)(2,1)} fusion(bf16[128,160,160]{1,2,0:T(8,128)(2,1)} %copy.35, bf16[128,160,128]{2,1,0:T(8,128)(2,1)S(1)} %to_channels.12), kind=kOutput, calls=%fused_computation.12 | convolution fusion | flops 841482240 | bytes 17039360 | tf_op jit(solution)/shard_map/cik,cij->ckj/dot_general | solution.py:372
  335.8 19.4 %convolution_add_fusion.2 = f32[128,160,160]{2,1,0:T(8,128)} fusion(f32[128,160,160]{2,1,0:T(8,128)} %fusion.5, bf16[128,160,128]{2,1,0:T(8,128)(2,1)} %copy-done.1, bf16[128,160,128]{2,1,0:T(8,128)(2,1)} %copy-done.7), kind=kOutput, calls=%fused_computation.3 | convolution fusion | flops 842137600 | bytes 36700160 | tf_op jit(solution)/shard_map/cij,ckj->cik/dot_general | solution.py:380
  364.8 9.4 %convolution_convert_fusion.2.x = bf16[128,160,128]{2,1,0:T(8,128)(2,1)} fusion(bf16[128,160,160]{1,2,0:T(8,128)(2,1)} %copy.35, bf16[128,160,128]{2,1,0:T(8,128)(2,1)S(1)} %to_channels.14), kind=kOutput, calls=%fused_computation.11 | convolution fusion | flops 841482240 | bytes 17039360 | tf_op jit(solution)/shard_map/cik,cij->ckj/dot_general | solution.py:372
  384.5 19.2 %convolution_add_fusion.1 = f32[128,160,160]{2,1,0:T(8,128)} fusion(f32[128,160,160]{2,1,0:T(8,128)} %convolution_add_fusion.2, bf16[128,160,128]{2,1,0:T(8,128)(2,1)} %copy-done, bf16[128,160,128]{2,1,0:T(8,128)(2,1)} %copy-done.6), kind=kOutput, calls=%fused_computation.2 | convolution fusion | flops 842137600 | bytes 36700160 | tf_op jit(solution)/shard_map/cij,ckj->cik/dot_general | solution.py:380
  411.6 11.1 %convolution_convert_fusion.1.x = bf16[128,160,128]{2,1,0:T(8,128)(2,1)} fusion(bf16[128,160,160]{1,2,0:T(8,128)(2,1)} %copy.35, bf16[128,160,128]{2,1,0:T(8,128)(2,1)S(1)} %to_channels.16), kind=kOutput, calls=%fused_computation.10 | convolution fusion | flops 841482240 | bytes 17039360 | tf_op jit(solution)/shard_map/cik,cij->ckj/dot_general | solution.py:372
  432.4 19.4 %convolution_add_fusion = f32[128,160,160]{2,1,0:T(8,128)} fusion(f32[128,160,160]{2,1,0:T(8,128)} %convolution_add_fusion.1, bf16[128,160,128]{2,1,0:T(8,128)(2,1)} %copy-done.3, bf16[128,160,128]{2,1,0:T(8,128)(2,1)} %copy-done.5), kind=kOutput, calls=%fused_computation.1 | convolution fusion | flops 842137600 | bytes 36700160 | tf_op jit(solution)/shard_map/cij,ckj->cik/dot_general | solution.py:380
  451.8 46.0 %all-gather.9.cloned.1.call-done = bf16[640,32,128]{2,1,0:T(8,128)(2,1)} async-done(((bf16[160,32,128]{2,1,0:T(8,128)(2,1)}), bf16[640,32,128]{2,1,0:T(8,128)(2,1)}) %all-gather.9.cloned.1.call-update) | async-done | bytes 5242896 | tf_op jit(solution)/shard_map/all_gather | solution.py:397
  505.0 11.2 %convolution_convert_fusion.x = bf16[128,160,128]{2,1,0:T(8,128)(2,1)} fusion(bf16[128,160,160]{1,2,0:T(8,128)(2,1)} %copy.35, bf16[128,160,128]{2,1,0:T(8,128)(2,1)S(1)} %to_channels.18), kind=kOutput, calls=%fused_computation.9 | convolution fusion | flops 841482240 | bytes 17039360 | tf_op jit(solution)/shard_map/cik,cij->ckj/dot_general | solution.py:372
  561.4 15.8 %add_convert_fusion = bf16[128,160,160]{2,1,0:T(8,128)(2,1)} fusion(f32[128,160,160]{2,1,0:T(8,128)} %convolution_add_fusion, bf16[128,160,128]{2,1,0:T(8,128)(2,1)} %copy-done.2, bf16[128,160,128]{2,1,0:T(8,128)(2,1)} %copy-done.4), kind=kOutput, calls=%fused_computation | convolution fusion | flops 845414400 | bytes 30146560 | tf_op jit(solution)/shard_map/cij,ckj->cik/dot_general | solution.py:380
  577.2 14.2 %copy.40 = bf16[128,160,160]{0,2,1:T(8,128)(2,1)} copy(bf16[128,160,160]{2,1,0:T(8,128)(2,1)} %add_convert_fusion) | data formatting | bytes 13107200 | tf_op jit(solution)/shard_map/layout_constraint | solution.py:383
  599.7 8.7 %final_part.6 = (bf16[160,160,128]{2,1,0:T(8,128)(2,1)}, f32[800,128]{1,0:T(8,128)S(1)}) custom-call(bf16[160,160,128]{2,1,0:T(8,128)(2,1)} %pair.19, bf16[160,160,128]{2,1,0:T(8,128)(2,1)} %bitcast.85, bf16[160,32,128]{2,1,0:T(8,128)(2,1)S(1)} %get-tuple-element.120.db0, bf16[160,32,128]{2,1,0:T(8,128)(2,1)} %bitcast.25.db1, ...), custom_call_target="tpu_custom_call", output_to_operand_aliasing={{0}: (12, {})} | custom-call | flops 1677721600 | bytes 14417920 | tf_op jit(solution)/shard_map/final_part/pallas_call | solution.py:281
  608.4 9.1 %collective-permute-done.8 = bf16[1,160,32,128]{3,2,1,0:T(8,128)(2,1)} collective-permute-done((bf16[1,160,32,128]{3,2,1,0:T(8,128)(2,1)}, bf16[1,160,32,128]{3,2,1,0:T(8,128)(2,1)}, u32[]{:S(2)}, u32[]{:S(2)}) %collective-permute-start.8) | collective-permute-done | bytes 1310752 | tf_op jit(solution)/shard_map/ppermute | solution.py:304
  617.5 8.4 %final_part.7 = (bf16[160,160,128]{2,1,0:T(8,128)(2,1)}, f32[800,128]{1,0:T(8,128)S(1)}) custom-call(bf16[160,160,128]{2,1,0:T(8,128)(2,1)} %pair.19, bf16[160,160,128]{2,1,0:T(8,128)(2,1)} %bitcast.86, bf16[160,32,128]{2,1,0:T(8,128)(2,1)S(1)} %copy-done.11, bf16[160,32,128]{2,1,0:T(8,128)(2,1)} %bitcast.21.db1, ...), custom_call_target="tpu_custom_call", output_to_operand_aliasing={{0}: (12, {})} | custom-call | flops 1677721600 | bytes 14417920 | tf_op jit(solution)/shard_map/final_part/pallas_call | solution.py:281
  625.9 19.7 %collective-permute-done.6 = bf16[1,160,32,128]{3,2,1,0:T(8,128)(2,1)} collective-permute-done((bf16[1,160,32,128]{3,2,1,0:T(8,128)(2,1)}, bf16[1,160,32,128]{3,2,1,0:T(8,128)(2,1)}, u32[]{:S(2)}, u32[]{:S(2)}) %collective-permute-start.6) | collective-permute-done | bytes 1310752 | tf_op jit(solution)/shard_map/ppermute | solution.py:304
  645.6 8.4 %final_part.8 = (bf16[160,160,128]{2,1,0:T(8,128)(2,1)}, f32[800,128]{1,0:T(8,128)S(1)}) custom-call(bf16[160,160,128]{2,1,0:T(8,128)(2,1)} %pair.19, bf16[160,160,128]{2,1,0:T(8,128)(2,1)} %bitcast.87, bf16[160,32,128]{2,1,0:T(8,128)(2,1)S(1)} %copy-done.13, bf16[160,32,128]{2,1,0:T(8,128)(2,1)} %bitcast.16.db1, ...), custom_call_target="tpu_custom_call", output_to_operand_aliasing={{0}: (12, {})} | custom-call | flops 1677721600 | bytes 14417920 | tf_op jit(solution)/shard_map/final_part/pallas_call | solution.py:281
  654.0 18.7 %collective-permute-done.4 = bf16[1,160,32,128]{3,2,1,0:T(8,128)(2,1)} collective-permute-done((bf16[1,160,32,128]{3,2,1,0:T(8,128)(2,1)}, bf16[1,160,32,128]{3,2,1,0:T(8,128)(2,1)}, u32[]{:S(2)}, u32[]{:S(2)}) %collective-permute-start.4) | collective-permute-done | bytes 1310752 | tf_op jit(solution)/shard_map/ppermute | solution.py:304
  (145 shorter events, 230.0 us)
Async XLA Ops:
  7.2 224.7 %all-gather.15.cloned.1.call-start = ((), (), s32[]{:S(2)}) async-start(), calls=%async_computation.3 | async-start | bytes 6553600 | tf_op jit(solution)/shard_map/all_gather | solution.py:397
  17.3 290.0 %all-gather.13.cloned.1.call-start = ((), (), s32[]{:S(2)}) async-start(), calls=%async_computation.2 | async-start | bytes 13107200 | tf_op jit(solution)/shard_map/all_gather | solution.py:397
  62.1 341.6 %all-gather.11.cloned.1.call-start = ((), (), s32[]{:S(2)}) async-start(), calls=%async_computation.1 | async-start | bytes 6553600 | tf_op jit(solution)/shard_map/all_gather | solution.py:397
  62.2 144.4 %collective-permute-start.1 = (bf16[160,160,128]{2,1,0:T(8,128)(2,1)}, bf16[160,160,128]{2,1,0:T(8,128)(2,1)}, u32[]{:S(2)}, u32[]{:S(2)}) collective-permute-start(bf16[160,160,128]{2,1,0:T(8,128)(2,1)} %get-tuple-element.76.refs_0_), channel_id=1, source_target_pairs={{0,8},{4,12},{8,0},{12,4},{1,9},{5,13},{9,1},{13,5},{2,10},{6,14},... | collective-permute-start | bytes 19660808 | tf_op jit(solution)/shard_map/ppermute | solution.py:304
  73.5 424.3 %all-gather.9.cloned.1.call-start = ((), (), s32[]{:S(2)}) async-start(), calls=%async_computation | async-start | bytes 6553600 | tf_op jit(solution)/shard_map/all_gather | solution.py:397
  73.7 183.5 %collective-permute-start = (bf16[160,160,128]{2,1,0:T(8,128)(2,1)}, bf16[160,160,128]{2,1,0:T(8,128)(2,1)}, u32[]{:S(2)}, u32[]{:S(2)}) collective-permute-start(bf16[160,160,128]{2,1,0:T(8,128)(2,1)} %get-tuple-element.76.refs_0_), channel_id=1, source_target_pairs={{0,4},{4,0},{8,12},{12,8},{1,5},{5,1},{9,13},{13,9},{2,6},{6,2},{1... | collective-permute-start | bytes 19660808 | tf_op jit(solution)/shard_map/ppermute | solution.py:304
  206.6 50.6 %collective-permute-start.2 = (bf16[160,160,128]{2,1,0:T(8,128)(2,1)}, bf16[160,160,128]{2,1,0:T(8,128)(2,1)}, u32[]{:S(2)}, u32[]{:S(2)}) collective-permute-start(bf16[160,160,128]{2,1,0:T(8,128)(2,1)} %collective-permute-done.1.refs_2_), channel_id=1, source_target_pairs={{0,4},{4,0},{8,12},{12,8},{1,5},{5,1},{9,13},{13,9},{2,6},{6,2},{1... | collective-permute-start | bytes 19660808 | tf_op jit(solution)/shard_map/ppermute | solution.py:304
  256.7 267.7 %collective-permute-start.11 = (bf16[2,160,32,128]{3,2,1,0:T(8,128)(2,1)}, bf16[2,160,32,128]{3,2,1,0:T(8,128)(2,1)}, u32[]{:S(2)}, u32[]{:S(2)}) collective-permute-start(bf16[2,160,32,128]{3,2,1,0:T(8,128)(2,1)} %get-tuple-element.73), channel_id=1, source_target_pairs={{0,4},{4,0},{8,12},{12,8},{1,5},{5,1},{9,13},{13,9},{2,6},{6,2},{1... | collective-permute-start | bytes 7864328 | tf_op jit(solution)/shard_map/ppermute | solution.py:304
  335.8 202.3 %collective-permute-start.9 = (bf16[2,160,32,128]{3,2,1,0:T(8,128)(2,1)}, bf16[2,160,32,128]{3,2,1,0:T(8,128)(2,1)}, u32[]{:S(2)}, u32[]{:S(2)}) collective-permute-start(bf16[2,160,32,128]{3,2,1,0:T(8,128)(2,1)} %get-tuple-element.82), channel_id=1, source_target_pairs={{0,4},{4,0},{8,12},{12,8},{1,5},{5,1},{9,13},{13,9},{2,6},{6,2},{1... | collective-permute-start | bytes 7864328 | tf_op jit(solution)/shard_map/ppermute | solution.py:304
  384.0 160.8 %collective-permute-start.7 = (bf16[2,160,32,128]{3,2,1,0:T(8,128)(2,1)}, bf16[2,160,32,128]{3,2,1,0:T(8,128)(2,1)}, u32[]{:S(2)}, u32[]{:S(2)}) collective-permute-start(bf16[2,160,32,128]{3,2,1,0:T(8,128)(2,1)} %get-tuple-element.86), channel_id=1, source_target_pairs={{0,4},{4,0},{8,12},{12,8},{1,5},{5,1},{9,13},{13,9},{2,6},{6,2},{1... | collective-permute-start | bytes 7864328 | tf_op jit(solution)/shard_map/ppermute | solution.py:304
  432.4 118.1 %collective-permute-start.5 = (bf16[2,160,32,128]{3,2,1,0:T(8,128)(2,1)}, bf16[2,160,32,128]{3,2,1,0:T(8,128)(2,1)}, u32[]{:S(2)}, u32[]{:S(2)}) collective-permute-start(bf16[2,160,32,128]{3,2,1,0:T(8,128)(2,1)} %get-tuple-element.90), channel_id=1, source_target_pairs={{0,4},{4,0},{8,12},{12,8},{1,5},{5,1},{9,13},{13,9},{2,6},{6,2},{1... | collective-permute-start | bytes 7864328 | tf_op jit(solution)/shard_map/ppermute | solution.py:304
  524.4 31.4 %collective-permute-start.3 = (bf16[2,160,32,128]{3,2,1,0:T(8,128)(2,1)}, bf16[2,160,32,128]{3,2,1,0:T(8,128)(2,1)}, u32[]{:S(2)}, u32[]{:S(2)}) collective-permute-start(bf16[2,160,32,128]{3,2,1,0:T(8,128)(2,1)} %get-tuple-element.94), channel_id=1, source_target_pairs={{0,4},{4,0},{8,12},{12,8},{1,5},{5,1},{9,13},{13,9},{2,6},{6,2},{1... | collective-permute-start | bytes 7864328 | tf_op jit(solution)/shard_map/ppermute | solution.py:304
  529.4 62.0 %collective-permute-start.12 = (bf16[1,160,32,128]{3,2,1,0:T(8,128)(2,1)}, bf16[1,160,32,128]{3,2,1,0:T(8,128)(2,1)}, u32[]{:S(2)}, u32[]{:S(2)}) collective-permute-start(bf16[1,160,32,128]{3,2,1,0:T(8,128)(2,1)} %get-tuple-element.117), channel_id=1, source_target_pairs={{0,8},{4,12},{8,0},{12,4},{1,9},{5,13},{9,1},{13,5},{2,10},{6,14},... | collective-permute-start | bytes 3932168 | tf_op jit(solution)/shard_map/ppermute | solution.py:304
  544.0 55.7 %collective-permute-start.10 = (bf16[1,160,32,128]{3,2,1,0:T(8,128)(2,1)}, bf16[1,160,32,128]{3,2,1,0:T(8,128)(2,1)}, u32[]{:S(2)}, u32[]{:S(2)}) collective-permute-start(bf16[1,160,32,128]{3,2,1,0:T(8,128)(2,1)} %get-tuple-element.119), channel_id=1, source_target_pairs={{0,8},{4,12},{8,0},{12,4},{1,9},{5,13},{9,1},{13,5},{2,10},{6,14},... | collective-permute-start | bytes 3932168 | tf_op jit(solution)/shard_map/ppermute | solution.py:304
  549.3 68.2 %collective-permute-start.8 = (bf16[1,160,32,128]{3,2,1,0:T(8,128)(2,1)}, bf16[1,160,32,128]{3,2,1,0:T(8,128)(2,1)}, u32[]{:S(2)}, u32[]{:S(2)}) collective-permute-start(bf16[1,160,32,128]{3,2,1,0:T(8,128)(2,1)} %get-tuple-element.121), channel_id=1, source_target_pairs={{0,8},{4,12},{8,0},{12,4},{1,9},{5,13},{9,1},{13,5},{2,10},{6,14},... | collective-permute-start | bytes 3932168 | tf_op jit(solution)/shard_map/ppermute | solution.py:304
  555.0 90.6 %collective-permute-start.6 = (bf16[1,160,32,128]{3,2,1,0:T(8,128)(2,1)}, bf16[1,160,32,128]{3,2,1,0:T(8,128)(2,1)}, u32[]{:S(2)}, u32[]{:S(2)}) collective-permute-start(bf16[1,160,32,128]{3,2,1,0:T(8,128)(2,1)} %get-tuple-element.123), channel_id=1, source_target_pairs={{0,8},{4,12},{8,0},{12,4},{1,9},{5,13},{9,1},{13,5},{2,10},{6,14},... | collective-permute-start | bytes 3932168 | tf_op jit(solution)/shard_map/ppermute | solution.py:304
  560.2 112.5 %collective-permute-start.4 = (bf16[1,160,32,128]{3,2,1,0:T(8,128)(2,1)}, bf16[1,160,32,128]{3,2,1,0:T(8,128)(2,1)}, u32[]{:S(2)}, u32[]{:S(2)}) collective-permute-start(bf16[1,160,32,128]{3,2,1,0:T(8,128)(2,1)} %get-tuple-element.125), channel_id=1, source_target_pairs={{0,8},{4,12},{8,0},{12,4},{1,9},{5,13},{9,1},{13,5},{2,10},{6,14},... | collective-permute-start | bytes 3932168 | tf_op jit(solution)/shard_map/ppermute | solution.py:304
  617.5 28.1 %copy-start.13 = (bf16[160,32,128]{2,1,0:T(8,128)(2,1)S(1)}, bf16[160,32,128]{2,1,0:T(8,128)(2,1)}, u32[]{:S(2)}) copy-start(bf16[160,32,128]{2,1,0:T(8,128)(2,1)} %get-tuple-element.124.db0) | copy-start | bytes 3932164
  681.0 1.7 collective-permute-start.13
  682.8 7.2 collective-permute-start.14
  690.1 4.7 collective-permute-start.15
  694.8 6.2 collective-permute-start.16
  701.0 4.7 collective-permute-start.17
  705.7 5.8 collective-permute-start.18
  (28 other events, 199.1 us)
Sparse Core Ops, SparseCore 0:
  17.4 100.7 all-gather.14
  119.8 182.2 all-gather.12
  303.7 96.2 all-gather.10
  401.4 96.4 all-gather.8

commit v3 on v2

--- a/solution.py
+++ b/solution.py
@@ -319,12 +319,20 @@
     return [slots[t] for t in range(n)]
 
 
-def reduce_rows(kept, sent, n):
+def reduce_cores(kept, sent, n):
     come = swap(sent, "row", n, 1)
+    if n == 2:
+        return kept, come
+    return (kept.astype(F32) + come.astype(F32)).astype(BF16), None
+
+
+def reduce_chips(v, come, n):
+    if come is not None:
+        return v[0], come[0]
     for bit in bits_of(n)[1:]:
-        v = (kept.astype(F32) + come.astype(F32)).astype(BF16)
         v = v.reshape((-1, 2) + v.shape[1:])
         kept, come = v[:, 0], swap(v[:, 1], "row", n, bit)
+        v = (kept.astype(F32) + come.astype(F32)).astype(BF16)
     return kept[0], come[0]
 
 
@@ -361,24 +369,27 @@
     b_slots = gather_rows(b_swapped, n)
     a_t = jnp.transpose(a, (2, 0, 1))
     major = Layout(major_to_minor=(0, 1, 2))
-    da = None
+    da, b_t = None, None
     db, spans = [], []
     for group in groups:
         for at in range(group.shape[2] // size):
             off = len(spans) * size
             if da is not None:
-                group, da = lax.optimization_barrier((group, da))
+                b_t = slots_to_channels(b_slots, r, off, size)
+                group, da, b_t = lax.optimization_barrier((group, da, b_t))
             dx_t = gathered_to_channels(group, r, at, size)
             part = jnp.einsum("cik,cij->ckj", a_t, dx_t, preferred_element_type=F32).astype(BF16)
             kept, sent = from_channels(part, n)
-            db.append(reduce_rows(kept, sent, n))
+            half, come = reduce_cores(kept, sent, n)
             if da is None:
                 dx_t, sent, *b_slots = lax.optimization_barrier((dx_t, sent, *b_slots))
+                b_t = slots_to_channels(b_slots, r, off, size)
             else:
                 dx_t, sent = lax.optimization_barrier((dx_t, sent))
-            b_t = slots_to_channels(b_slots, r, off, size)
             term = jnp.einsum("cij,ckj->cik", dx_t, b_t, preferred_element_type=F32)
             da = with_layout_constraint(term if da is None else da + term, major)
+            da, half = lax.optimization_barrier((da, half))
+            db.append(reduce_chips(half, come, n))
             spans.append((off, size))
     da = with_layout_constraint(da.astype(BF16), major)
     return jnp.transpose(da, (1, 2, 0)), db, spans

time: 728 us -> 726 us (level)
    all_gather x4, waiting for transfers between devices: 46.1 us -> 14.2 us  [shards(): groups.append(lax.all_gather(dx, 'col', axis=0) if even else dx)]
    ppermute x19, waiting for transfers between devices: 207 us -> 235 us  [swap(): return lax.ppermute(v, axis, [(r, r ^ bit) for r in range(n)])]
    convert_element_type x0 -> x5, other arithmetic: none -> 17.3 us  [reduce_cores(): return ((kept.astype(F32) + come.astype(F32)).astype(BF16), None)]
    reshape x5 -> x0, other arithmetic: 15.3 us -> none  [reduce_rows(): v = v.reshape((-1, 2) + v.shape[1:])]
    unnamed x57 -> x55, local copies, waits for them, and re-layouts: 18.6 us -> 17.4 us
  transfers between devices with their start and end apart: 23 -> 23, of which waited for: 11 -> 14; matrix products, arithmetic and copies ran while one was open for 28% -> 27% of each run, Pallas kernels for 28% -> 26%
where the time goes in v3:
time: 726 us; the launch traced here: 717 us
  waiting for transfers between devices  249 us (34%)
  Pallas kernels  218 us (30%)
  matrix products  141 us (19%)
  local copies, waits for them, and re-layouts  63.7 us (9%)
  other arithmetic  17.5 us (2%)
  starting transfers between devices  14.4 us (2%)
  between operations  14.3 us (2%)
    ppermute x19, waiting for transfers between devices, swap(): return lax.ppermute(v, axis, [(r, r ^ bit) for r in range(n)])  235 us
    dot_general x5, matrix products, triangles(): term = jnp.einsum('cij,ckj->cik', dx_t, b_t, preferred_element_type=F32)  86.9 us
    pallas_call x10, Pallas kernels, to_channels(): pl.pallas_call(functools.partial(to_channels_kernel, slots), grid_spec=pl...  71.7 us
    dot_general x5, matrix products, triangles(): jnp.einsum('cik,cij->ckj', a_t, dx_t, preferred_element_type=F32)  54.1 us
    pallas_call x5, Pallas kernels, final_chunk(): pl.pallas_call(functools.partial(final_kernel, step, bool(chain)), grid=(...  41.9 us
    pallas_call x4, Pallas kernels, dx_chunk(): pl.pallas_call(functools.partial(dx_kernel, step, bool(chain)), grid=(row...  40.3 us
    pallas_call x5, Pallas kernels, from_channels(): pl.pallas_call(functools.partial(from_channels_kernel, slots), grid=(lead...  40.1 us
    pallas_call x1, Pallas kernels, projections(): pl.pallas_call(functools.partial(proj_kernel, step), grid=(rows // ib,),...  23.6 us
  transfers between devices with their start and end apart: 23, of which 14 were waited for; matrix products, arithmetic and copies ran while one was open for 27% of the time, Pallas kernels for 26%

profile of v3, /device:TPU:0, one launch (start us, length us, event | category | flops | bytes accessed | tf_op | source)
XLA Modules:
  0.0 717.4 jit_solution(13405055755518190651)
XLA Ops:
  8.8 8.4 %dx_part.4 = (bf16[160,32,128]{2,1,0:T(8,128)(2,1)}, bf16[160,160,128]{2,1,0:T(8,128)(2,1)}, f32[800,128]{1,0:T(8,128)S(1)}) custom-call(bf16[160,160,128]{2,1,0:T(8,128)(2,1)} %pair.19, bf16[160,160,128]{2,1,0:T(8,128)(2,1)} %product.7, bf16[160,160,128]{2,1,0:T(8,128)(2,1)} %go.7, bf16[6,128,128]{2,1,0:T(8,128)(2,1)S(1)} %copy-done.9, f32[4,128]{1,0:T(4,128)S(1)} %copy-done.20), custom_call_target="tpu_custom_call" | custom-call | flops 671088640 | bytes 6553600 | tf_op jit(solution)/shard_map/dx_part/pallas_call | solution.py:104
  23.6 23.6 %projections.1 = (bf16[160,160,128]{2,1,0:T(8,128)(2,1)}, bf16[160,160,128]{2,1,0:T(8,128)(2,1)}, bf16[160,160,128]{2,1,0:T(8,128)(2,1)}, bf16[160,160,128]{2,1,...) custom-call(bf16[160,160,128]{2,1,0:T(8,128)(2,1)} %pair.19, ...), custom_call_target="tpu_custom_call" | custom-call | flops 3355443200 | bytes 52428800 | tf_op jit(solution)/shard_map/projections/pallas_call | solution.py:157
  47.2 14.9 %dx_part.5 = (bf16[160,64,128]{2,1,0:T(8,128)(2,1)}, bf16[160,160,128]{2,1,0:T(8,128)(2,1)}, f32[800,128]{1,0:T(8,128)S(1)}) custom-call(bf16[160,160,128]{2,1,0:T(8,128)(2,1)} %pair.19, bf16[160,160,128]{2,1,0:T(8,128)(2,1)} %product.7, bf16[160,160,128]{2,1,0:T(8,128)(2,1)} %go.7, ...), custom_call_target="tpu_custom_call", output_to_operand_aliasing={{1}: (5, {})} | custom-call | flops 1342177280 | bytes 13107200 | tf_op jit(solution)/shard_map/dx_part/pallas_call | solution.py:104
  65.1 141.5 %collective-permute-done.1.refs_2_ = bf16[160,160,128]{2,1,0:T(8,128)(2,1)} collective-permute-done((bf16[160,160,128]{2,1,0:T(8,128)(2,1)}, bf16[160,160,128]{2,1,0:T(8,128)(2,1)}, u32[]{:S(2)}, u32[]{:S(2)}) %collective-permute-start.1) | collective-permute-done | bytes 6553632 | tf_op jit(solution)/shard_map/ppermute | solution.py:304
  206.5 8.5 %dx_part.6 = (bf16[160,32,128]{2,1,0:T(8,128)(2,1)}, bf16[160,160,128]{2,1,0:T(8,128)(2,1)}, f32[800,128]{1,0:T(8,128)S(1)}) custom-call(bf16[160,160,128]{2,1,0:T(8,128)(2,1)} %pair.19, bf16[160,160,128]{2,1,0:T(8,128)(2,1)} %product.7, bf16[160,160,128]{2,1,0:T(8,128)(2,1)} %go.7, ...), custom_call_target="tpu_custom_call", output_to_operand_aliasing={{1}: (5, {})} | custom-call | flops 671088640 | bytes 6553600 | tf_op jit(solution)/shard_map/dx_part/pallas_call | solution.py:104
  216.4 15.5 %copy.35 = bf16[128,160,160]{1,2,0:T(8,128)(2,1)} copy(bf16[128,160,160]{0,2,1:T(8,128)(2,1)} %bitcast.101) | data formatting | bytes 13107200 | tf_op jit(solution)/shard_map/transpose | solution.py:370
  239.1 9.4 %convolution_convert_fusion.4.x = bf16[128,160,128]{2,1,0:T(8,128)(2,1)} fusion(bf16[128,160,160]{1,2,0:T(8,128)(2,1)} %copy.35, bf16[128,160,128]{2,1,0:T(8,128)(2,1)S(1)} %to_channels.10), kind=kOutput, calls=%fused_computation.13 | convolution fusion | flops 841482240 | bytes 17039360 | tf_op jit(solution)/shard_map/cik,cij->ckj/dot_general | solution.py:381
  272.0 12.4 %fusion = f32[128,160,160]{2,1,0:T(8,128)} fusion(bf16[128,160,128]{2,1,0:T(8,128)(2,1)S(1)} %to_channels.10, bf16[128,160,128]{2,1,0:T(8,128)(2,1)} %copy-done.8), kind=kOutput, calls=%fused_computation.30 | convolution fusion | flops 838860800 | bytes 23592960 | tf_op jit(solution)/shard_map/cij,ckj->cik/dot_general | solution.py:389
  309.4 11.3 %convolution_convert_fusion.3.x = bf16[128,160,128]{2,1,0:T(8,128)(2,1)} fusion(bf16[128,160,160]{1,2,0:T(8,128)(2,1)} %copy.35, bf16[128,160,128]{2,1,0:T(8,128)(2,1)S(1)} %to_channels.13), kind=kOutput, calls=%fused_computation.12 | convolution fusion | flops 841482240 | bytes 17039360 | tf_op jit(solution)/shard_map/cik,cij->ckj/dot_general | solution.py:381
  329.1 8.6 %dx_part.7 = (bf16[160,32,128]{2,1,0:T(8,128)(2,1)S(1)}, bf16[160,160,128]{2,1,0:T(8,128)(2,1)}, f32[800,128]{1,0:T(8,128)S(1)}) custom-call(bf16[160,160,128]{2,1,0:T(8,128)(2,1)} %pair.19, bf16[160,160,128]{2,1,0:T(8,128)(2,1)} %product.7, bf16[160,160,128]{2,1,0:T(8,128)(2,1)} %go.7, ...), custom_call_target="tpu_custom_call", output_to_operand_aliasing={{1}: (5, {})} | custom-call | flops 671088640 | bytes 6553600 | tf_op jit(solution)/shard_map/dx_part/pallas_call | solution.py:104
  348.9 19.4 %convolution_add_fusion.3 = f32[128,160,160]{2,1,0:T(8,128)} fusion(f32[128,160,160]{2,1,0:T(8,128)} %fusion, bf16[128,160,128]{2,1,0:T(8,128)(2,1)} %copy-done, bf16[128,160,128]{2,1,0:T(8,128)(2,1)} %copy-done.6), kind=kOutput, calls=%fused_computation.3 | convolution fusion | flops 842137600 | bytes 36700160 | tf_op jit(solution)/shard_map/cij,ckj->cik/dot_general | solution.py:389
  379.5 11.1 %convolution_convert_fusion.2.x = bf16[128,160,128]{2,1,0:T(8,128)(2,1)} fusion(bf16[128,160,160]{1,2,0:T(8,128)(2,1)} %copy.35, bf16[128,160,128]{2,1,0:T(8,128)(2,1)S(1)} %to_channels.15), kind=kOutput, calls=%fused_computation.11 | convolution fusion | flops 841482240 | bytes 17039360 | tf_op jit(solution)/shard_map/cik,cij->ckj/dot_general | solution.py:381
  408.7 19.7 %convolution_add_fusion.2 = f32[128,160,160]{2,1,0:T(8,128)} fusion(f32[128,160,160]{2,1,0:T(8,128)} %convolution_add_fusion.3, bf16[128,160,128]{2,1,0:T(8,128)(2,1)} %copy-done.1, bf16[128,160,128]{2,1,0:T(8,128)(2,1)} %copy-done.7), kind=kOutput, calls=%fused_computation.2 | convolution fusion | flops 842137600 | bytes 36700160 | tf_op jit(solution)/shard_map/cij,ckj->cik/dot_general | solution.py:389
  439.7 11.2 %convolution_convert_fusion.1.x = bf16[128,160,128]{2,1,0:T(8,128)(2,1)} fusion(bf16[128,160,160]{1,2,0:T(8,128)(2,1)} %copy.35, bf16[128,160,128]{2,1,0:T(8,128)(2,1)S(1)} %to_channels.17), kind=kOutput, calls=%fused_computation.10 | convolution fusion | flops 841482240 | bytes 17039360 | tf_op jit(solution)/shard_map/cik,cij->ckj/dot_general | solution.py:381
  468.8 19.3 %convolution_add_fusion.1 = f32[128,160,160]{2,1,0:T(8,128)} fusion(f32[128,160,160]{2,1,0:T(8,128)} %convolution_add_fusion.2, bf16[128,160,128]{2,1,0:T(8,128)(2,1)} %copy-done.3, bf16[128,160,128]{2,1,0:T(8,128)(2,1)} %copy-done.5), kind=kOutput, calls=%fused_computation.1 | convolution fusion | flops 842137600 | bytes 36700160 | tf_op jit(solution)/shard_map/cij,ckj->cik/dot_general | solution.py:389
  505.0 11.2 %convolution_convert_fusion.x = bf16[128,160,128]{2,1,0:T(8,128)(2,1)} fusion(bf16[128,160,160]{1,2,0:T(8,128)(2,1)} %copy.35, bf16[128,160,128]{2,1,0:T(8,128)(2,1)S(1)} %to_channels.19), kind=kOutput, calls=%fused_computation.9 | convolution fusion | flops 841482240 | bytes 17039360 | tf_op jit(solution)/shard_map/cik,cij->ckj/dot_general | solution.py:381
  516.2 8.4 %from_channels.9 = (bf16[2,160,32,128]{3,2,1,0:T(8,128)(2,1)S(1)}, bf16[2,160,32,128]{3,2,1,0:T(8,128)(2,1)}) custom-call(bf16[128,160,128]{2,1,0:T(8,128)(2,1)} %convolution_convert_fusion.x), custom_call_target="tpu_custom_call" | custom-call | flops 10485760 | bytes 10485760 | tf_op jit(solution)/shard_map/from_channels/pallas_call | solution.py:225
  537.1 16.2 %convolution_add_fusion = bf16[128,160,160]{2,1,0:T(8,128)(2,1)} fusion(f32[128,160,160]{2,1,0:T(8,128)} %convolution_add_fusion.1, bf16[128,160,128]{2,1,0:T(8,128)(2,1)} %copy-done.2, bf16[128,160,128]{2,1,0:T(8,128)(2,1)} %copy-done.4), kind=kOutput, calls=%fused_computation | convolution fusion | flops 845414400 | bytes 30146560 | tf_op jit(solution)/shard_map/cij,ckj->cik/dot_general | solution.py:389
  559.1 14.1 %copy.40 = bf16[128,160,160]{0,2,1:T(8,128)(2,1)} copy(bf16[128,160,160]{2,1,0:T(8,128)(2,1)} %convolution_add_fusion) | data formatting | bytes 13107200 | tf_op jit(solution)/shard_map/layout_constraint | solution.py:394
  586.6 8.4 %final_part.6 = (bf16[160,160,128]{2,1,0:T(8,128)(2,1)}, f32[800,128]{1,0:T(8,128)S(1)}) custom-call(bf16[160,160,128]{2,1,0:T(8,128)(2,1)} %pair.19, bf16[160,160,128]{2,1,0:T(8,128)(2,1)} %bitcast.80, bf16[160,32,128]{2,1,0:T(8,128)(2,1)S(1)} %copy-done.12, bf16[160,32,128]{2,1,0:T(8,128)(2,1)} %bitcast.25.db1, ...), custom_call_target="tpu_custom_call", output_to_operand_aliasing={{0}: (12, {})} | custom-call | flops 1677721600 | bytes 14417920 | tf_op jit(solution)/shard_map/final_part/pallas_call | solution.py:281
  595.0 19.7 %collective-permute-done.10 = bf16[1,160,32,128]{3,2,1,0:T(8,128)(2,1)} collective-permute-done((bf16[1,160,32,128]{3,2,1,0:T(8,128)(2,1)}, bf16[1,160,32,128]{3,2,1,0:T(8,128)(2,1)}, u32[]{:S(2)}, u32[]{:S(2)}) %collective-permute-start.10) | collective-permute-done | bytes 1310752 | tf_op jit(solution)/shard_map/ppermute | solution.py:304
  623.0 19.8 %collective-permute-done.9 = bf16[1,160,32,128]{3,2,1,0:T(8,128)(2,1)} collective-permute-done((bf16[1,160,32,128]{3,2,1,0:T(8,128)(2,1)}, bf16[1,160,32,128]{3,2,1,0:T(8,128)(2,1)}, u32[]{:S(2)}, u32[]{:S(2)}) %collective-permute-start.9) | collective-permute-done | bytes 1310752 | tf_op jit(solution)/shard_map/ppermute | solution.py:304
  642.7 8.5 %final_part.8 = (bf16[160,160,128]{2,1,0:T(8,128)(2,1)}, f32[800,128]{1,0:T(8,128)S(1)}) custom-call(bf16[160,160,128]{2,1,0:T(8,128)(2,1)} %pair.19, bf16[160,160,128]{2,1,0:T(8,128)(2,1)} %bitcast.82, bf16[160,32,128]{2,1,0:T(8,128)(2,1)S(1)} %get-tuple-element.152.db0, bf16[160,32,128]{2,1,0:T(8,128)(2,1)} %bitcast.16.db1, ...), custom_call_target="tpu_custom_call", output_to_operand_aliasing={{0}: (12, {})} | custom-call | flops 1677721600 | bytes 14417920 | tf_op jit(solution)/shard_map/final_part/pallas_call | solution.py:281
  651.2 19.2 %collective-permute-done.8 = bf16[1,160,32,128]{3,2,1,0:T(8,128)(2,1)} collective-permute-done((bf16[1,160,32,128]{3,2,1,0:T(8,128)(2,1)}, bf16[1,160,32,128]{3,2,1,0:T(8,128)(2,1)}, u32[]{:S(2)}, u32[]{:S(2)}) %collective-permute-start.8) | collective-permute-done | bytes 1310752 | tf_op jit(solution)/shard_map/ppermute | solution.py:304
  (143 shorter events, 243.0 us)
Async XLA Ops:
  7.2 224.7 %all-gather.15.cloned.1.call-start = ((), (), s32[]{:S(2)}) async-start(), calls=%async_computation.3 | async-start | bytes 6553600 | tf_op jit(solution)/shard_map/all_gather | solution.py:408
  17.3 284.8 %all-gather.13.cloned.1.call-start = ((), (), s32[]{:S(2)}) async-start(), calls=%async_computation.2 | async-start | bytes 13107200 | tf_op jit(solution)/shard_map/all_gather | solution.py:408
  62.1 370.3 %all-gather.11.cloned.1.call-start = ((), (), s32[]{:S(2)}) async-start(), calls=%async_computation.1 | async-start | bytes 6553600 | tf_op jit(solution)/shard_map/all_gather | solution.py:408
  62.1 144.4 %collective-permute-start.1 = (bf16[160,160,128]{2,1,0:T(8,128)(2,1)}, bf16[160,160,128]{2,1,0:T(8,128)(2,1)}, u32[]{:S(2)}, u32[]{:S(2)}) collective-permute-start(bf16[160,160,128]{2,1,0:T(8,128)(2,1)} %get-tuple-element.90.refs_0_), channel_id=1, source_target_pairs={{0,8},{4,12},{8,0},{12,4},{1,9},{5,13},{9,1},{13,5},{2,10},{6,14},... | collective-permute-start | bytes 19660808 | tf_op jit(solution)/shard_map/ppermute | solution.py:304
  65.1 197.5 %collective-permute-start = (bf16[160,160,128]{2,1,0:T(8,128)(2,1)}, bf16[160,160,128]{2,1,0:T(8,128)(2,1)}, u32[]{:S(2)}, u32[]{:S(2)}) collective-permute-start(bf16[160,160,128]{2,1,0:T(8,128)(2,1)} %get-tuple-element.90.refs_0_), channel_id=1, source_target_pairs={{0,4},{4,0},{8,12},{12,8},{1,5},{5,1},{9,13},{13,9},{2,6},{6,2},{1... | collective-permute-start | bytes 19660808 | tf_op jit(solution)/shard_map/ppermute | solution.py:304
  206.5 56.0 %collective-permute-start.2 = (bf16[160,160,128]{2,1,0:T(8,128)(2,1)}, bf16[160,160,128]{2,1,0:T(8,128)(2,1)}, u32[]{:S(2)}, u32[]{:S(2)}) collective-permute-start(bf16[160,160,128]{2,1,0:T(8,128)(2,1)} %collective-permute-done.1.refs_2_), channel_id=1, source_target_pairs={{0,4},{4,0},{8,12},{12,8},{1,5},{5,1},{9,13},{13,9},{2,6},{6,2},{1... | collective-permute-start | bytes 19660808 | tf_op jit(solution)/shard_map/ppermute | solution.py:304
  215.8 282.1 %all-gather.9.cloned.1.call-start = ((), (), s32[]{:S(2)}) async-start(), calls=%async_computation | async-start | bytes 6553600 | tf_op jit(solution)/shard_map/all_gather | solution.py:408
  255.3 5.1 collective-permute-start.3
  309.4 28.3 %copy-start = (bf16[128,160,128]{2,1,0:T(8,128)(2,1)}, bf16[128,160,128]{2,1,0:T(8,128)(2,1)S(1)}, u32[]{:S(2)}) copy-start(bf16[128,160,128]{2,1,0:T(8,128)(2,1)S(1)} %to_channels.13) | copy-start | bytes 15728644
  329.0 39.3 %collective-permute-start.4 = (bf16[2,160,32,128]{3,2,1,0:T(8,128)(2,1)}, bf16[2,160,32,128]{3,2,1,0:T(8,128)(2,1)}, u32[]{:S(2)}, u32[]{:S(2)}) collective-permute-start(bf16[2,160,32,128]{3,2,1,0:T(8,128)(2,1)} %get-tuple-element.98), channel_id=1, source_target_pairs={{0,4},{4,0},{8,12},{12,8},{1,5},{5,1},{9,13},{13,9},{2,6},{6,2},{1... | collective-permute-start | bytes 7864328 | tf_op jit(solution)/shard_map/ppermute | solution.py:304
  398.8 29.6 %collective-permute-start.5 = (bf16[2,160,32,128]{3,2,1,0:T(8,128)(2,1)}, bf16[2,160,32,128]{3,2,1,0:T(8,128)(2,1)}, u32[]{:S(2)}, u32[]{:S(2)}) collective-permute-start(bf16[2,160,32,128]{3,2,1,0:T(8,128)(2,1)} %get-tuple-element.105), channel_id=1, source_target_pairs={{0,4},{4,0},{8,12},{12,8},{1,5},{5,1},{9,13},{13,9},{2,6},{6,2},{1... | collective-permute-start | bytes 7864328 | tf_op jit(solution)/shard_map/ppermute | solution.py:304
  459.2 28.9 %collective-permute-start.6 = (bf16[2,160,32,128]{3,2,1,0:T(8,128)(2,1)}, bf16[2,160,32,128]{3,2,1,0:T(8,128)(2,1)}, u32[]{:S(2)}, u32[]{:S(2)}) collective-permute-start(bf16[2,160,32,128]{3,2,1,0:T(8,128)(2,1)} %get-tuple-element.112), channel_id=1, source_target_pairs={{0,4},{4,0},{8,12},{12,8},{1,5},{5,1},{9,13},{13,9},{2,6},{6,2},{1... | collective-permute-start | bytes 7864328 | tf_op jit(solution)/shard_map/ppermute | solution.py:304
  524.6 28.8 %collective-permute-start.7 = (bf16[2,160,32,128]{3,2,1,0:T(8,128)(2,1)}, bf16[2,160,32,128]{3,2,1,0:T(8,128)(2,1)}, u32[]{:S(2)}, u32[]{:S(2)}) collective-permute-start(bf16[2,160,32,128]{3,2,1,0:T(8,128)(2,1)} %get-tuple-element.119), channel_id=1, source_target_pairs={{0,4},{4,0},{8,12},{12,8},{1,5},{5,1},{9,13},{13,9},{2,6},{6,2},{1... | collective-permute-start | bytes 7864328 | tf_op jit(solution)/shard_map/ppermute | solution.py:304
  526.6 46.6 %collective-permute-start.12 = (bf16[1,160,32,128]{3,2,1,0:T(8,128)(2,1)}, bf16[1,160,32,128]{3,2,1,0:T(8,128)(2,1)}, u32[]{:S(2)}, u32[]{:S(2)}) collective-permute-start(bf16[1,160,32,128]{3,2,1,0:T(8,128)(2,1)} %get-tuple-element.145), channel_id=1, source_target_pairs={{0,8},{4,12},{8,0},{12,4},{1,9},{5,13},{9,1},{13,5},{2,10},{6,14},... | collective-permute-start | bytes 3932168 | tf_op jit(solution)/shard_map/ppermute | solution.py:304
  530.2 56.4 %collective-permute-start.11 = (bf16[1,160,32,128]{3,2,1,0:T(8,128)(2,1)}, bf16[1,160,32,128]{3,2,1,0:T(8,128)(2,1)}, u32[]{:S(2)}, u32[]{:S(2)}) collective-permute-start(bf16[1,160,32,128]{3,2,1,0:T(8,128)(2,1)} %get-tuple-element.147), channel_id=1, source_target_pairs={{0,8},{4,12},{8,0},{12,4},{1,9},{5,13},{9,1},{13,5},{2,10},{6,14},... | collective-permute-start | bytes 3932168 | tf_op jit(solution)/shard_map/ppermute | solution.py:304
  533.6 81.0 %collective-permute-start.10 = (bf16[1,160,32,128]{3,2,1,0:T(8,128)(2,1)}, bf16[1,160,32,128]{3,2,1,0:T(8,128)(2,1)}, u32[]{:S(2)}, u32[]{:S(2)}) collective-permute-start(bf16[1,160,32,128]{3,2,1,0:T(8,128)(2,1)} %get-tuple-element.149), channel_id=1, source_target_pairs={{0,8},{4,12},{8,0},{12,4},{1,9},{5,13},{9,1},{13,5},{2,10},{6,14},... | collective-permute-start | bytes 3932168 | tf_op jit(solution)/shard_map/ppermute | solution.py:304
  535.7 107.0 %collective-permute-start.9 = (bf16[1,160,32,128]{3,2,1,0:T(8,128)(2,1)}, bf16[1,160,32,128]{3,2,1,0:T(8,128)(2,1)}, u32[]{:S(2)}, u32[]{:S(2)}) collective-permute-start(bf16[1,160,32,128]{3,2,1,0:T(8,128)(2,1)} %get-tuple-element.151), channel_id=1, source_target_pairs={{0,8},{4,12},{8,0},{12,4},{1,9},{5,13},{9,1},{13,5},{2,10},{6,14},... | collective-permute-start | bytes 3932168 | tf_op jit(solution)/shard_map/ppermute | solution.py:304
  558.1 112.3 %collective-permute-start.8 = (bf16[1,160,32,128]{3,2,1,0:T(8,128)(2,1)}, bf16[1,160,32,128]{3,2,1,0:T(8,128)(2,1)}, u32[]{:S(2)}, u32[]{:S(2)}) collective-permute-start(bf16[1,160,32,128]{3,2,1,0:T(8,128)(2,1)} %get-tuple-element.153), channel_id=1, source_target_pairs={{0,8},{4,12},{8,0},{12,4},{1,9},{5,13},{9,1},{13,5},{2,10},{6,14},... | collective-permute-start | bytes 3932168 | tf_op jit(solution)/shard_map/ppermute | solution.py:304
  678.7 1.7 collective-permute-start.13
  680.5 7.2 %collective-permute-start.14 = (f32[400,128]{1,0:T(8,128)S(1)}, f32[400,128]{1,0:T(8,128)S(1)}, u32[]{:S(2)}, u32[]{:S(2)}) collective-permute-start(f32[400,128]{1,0:T(8,128)S(1)} %dynamic-slice_bitcast_fusion), channel_id=1, source_target_pairs={{0,8},{4,12},{8,0},{12,4},{1,9},{5,13},{9,1},{13,5},{2,10},{6,14},... | collective-permute-start | bytes 614408 | tf_op jit(solution)/shard_map/ppermute | solution.py:304
  687.8 4.7 collective-permute-start.15
  692.5 6.2 collective-permute-start.16
  698.7 4.7 collective-permute-start.17
  703.5 5.8 collective-permute-start.18
  (27 other events, 170.2 us)
Sparse Core Ops, SparseCore 0:
  17.4 100.7 all-gather.14
  119.8 182.2 all-gather.12
  303.7 96.2 all-gather.10
  401.4 96.4 all-gather.8

commit v4 on v3

--- a/solution.py
+++ b/solution.py
@@ -312,11 +312,15 @@
     return [1 << k for k in range(n.bit_length() - 1)]
 
 
-def gather_rows(v, n):
+def chip_slots(v, n):
     slots = {0: v}
-    for bit in bits_of(n)[::-1]:
+    for bit in bits_of(n)[:0:-1]:
         slots.update({t ^ bit: swap(x, "row", n, bit) for t, x in slots.items()})
-    return [slots[t] for t in range(n)]
+    return [slots[t] for t in range(0, n, 2)]
+
+
+def core_slots(slots, n):
+    return [x for v in slots for x in (v, swap(v, "row", n, 1))]
 
 
 def reduce_cores(kept, sent, n):
@@ -364,35 +368,47 @@
     return da.astype(BF16), [(db, jnp.zeros_like(db))], [(0, rows)]
 
 
-def triangles(n, groups, size, a, b_swapped):
+def triangles(n, groups, size, a, b_swapped, acc):
     r = lax.axis_index("row").astype(jnp.int32).reshape(1)
-    b_slots = gather_rows(b_swapped, n)
+    cols = b_swapped.shape[1]
+    split = 2 * size if cols > 2 * size else cols
+    early = chip_slots(b_swapped[:, :split], n)
+    late = chip_slots(b_swapped[:, split:], n) if split < cols else []
     a_t = jnp.transpose(a, (2, 0, 1))
+    first, a_t, acc = lax.optimization_barrier((groups[0], a_t, acc))
+    groups = [first] + groups[1:]
     major = Layout(major_to_minor=(0, 1, 2))
     da, b_t = None, None
     db, spans = [], []
     for group in groups:
         for at in range(group.shape[2] // size):
-            off = len(spans) * size
-            if da is not None:
-                b_t = slots_to_channels(b_slots, r, off, size)
+            q = len(spans)
+            off = q * size
+            if q > 0:
+                slots, start = (b_early, off) if off < split else (b_late, off - split)
+                b_t = slots_to_channels(slots, r, start, size)
                 group, da, b_t = lax.optimization_barrier((group, da, b_t))
             dx_t = gathered_to_channels(group, r, at, size)
             part = jnp.einsum("cik,cij->ckj", a_t, dx_t, preferred_element_type=F32).astype(BF16)
             kept, sent = from_channels(part, n)
+            if q == 0:
+                dx_t, kept, sent, *early = lax.optimization_barrier((dx_t, kept, sent, *early))
+                b_early = core_slots(early, n)
+                b_t = slots_to_channels(b_early, r, off, size)
+            else:
+                dx_t, kept, sent = lax.optimization_barrier((dx_t, kept, sent))
             half, come = reduce_cores(kept, sent, n)
-            if da is None:
-                dx_t, sent, *b_slots = lax.optimization_barrier((dx_t, sent, *b_slots))
-                b_t = slots_to_channels(b_slots, r, off, size)
+            term = jnp.einsum("cij,ckj->cik", dx_t, b_t, preferred_element_type=F32)
+            da = with_layout_constraint(term if q == 0 else da + term, major)
+            if q == 0:
+                da, half, *late = lax.optimization_barrier((da, half, *late))
+                b_late = core_slots(late, n)
             else:
-                dx_t, sent = lax.optimization_barrier((dx_t, sent))
-            term = jnp.einsum("cij,ckj->cik", dx_t, b_t, preferred_element_type=F32)
-            da = with_layout_constraint(term if da is None else da + term, major)
-            da, half = lax.optimization_barrier((da, half))
-            db.append(reduce_chips(half, come, n))
+                da, half, db[-1][1] = lax.optimization_barrier((da, half, db[-1][1]))
+            db.append(list(reduce_chips(half, come, n)))
             spans.append((off, size))
     da = with_layout_constraint(da.astype(BF16), major)
-    return jnp.transpose(da, (1, 2, 0)), db, spans
+    return jnp.transpose(da, (1, 2, 0)), db, spans, acc
 
 
 def shards(n_row, n_col, pair, product, mask, grad_out, weights, norms):
@@ -413,7 +429,7 @@
         off += width
     dol, acc = chain
     if even:
-        da, db, spans = triangles(n_row, groups, size, a, b_swapped)
+        da, db, spans, acc = triangles(n_row, groups, size, a, b_swapped, acc)
     else:
         da, db, spans = triangles_plain(n_row, n_col, groups[0], a, b_swapped)
     wcat = jnp.transpose(weights[:5], (1, 0, 2)).reshape(c, 5 * c)

time: 726 us -> 713 us (0.982)
  waiting for transfers between devices: 249 us -> 159 us
  other arithmetic: 17.5 us -> 106 us
  matrix products: 141 us -> 109 us
  local copies, waits for them, and re-layouts: 63.7 us -> 72.9 us
  Pallas kernels: 218 us -> 227 us
    ppermute x19 -> x22, waiting for transfers between devices: 235 us -> 88.8 us  [swap(): return lax.ppermute(v, axis, [(r, r ^ bit) for r in range(n)])]
    add x0 -> x4, other arithmetic: none -> 89.1 us  [triangles(): da = with_layout_constraint(term if q == 0 else da + term, major)]
    all_gather x4, waiting for transfers between devices: 14.2 us -> 70.2 us  [shards(): groups.append(lax.all_gather(dx, 'col', axis=0) if even else dx)]
    dot_general x5, matrix products: 86.9 us -> 62.3 us  [triangles(): term = jnp.einsum('cij,ckj->cik', dx_t, b_t, preferred_element_type=F32)]
    optimization_barrier x0 -> x1, local copies, waits for them, and re-layouts: none -> 15.9 us  [triangles(): first, a_t, acc = lax.optimization_barrier((groups[0], a_t, acc))]
    transpose x1 -> x0, local copies, waits for them, and re-layouts: 15.5 us -> none  [triangles(): a_t = jnp.transpose(a, (2, 0, 1))]
    pallas_call x10, Pallas kernels: 71.7 us -> 81.5 us  [to_channels(): pl.pallas_call(functools.partial(to_channels_kernel, slots), grid_spec=pl...]
    another operation x0 -> x4, local copies, waits for them, and re-layouts: none -> 8.66 us  [reduce_chips(): return (kept[0], come[0])]
  transfers between devices with their start and end apart: 23 -> 26, of which waited for: 14 -> 11; matrix products, arithmetic and copies ran while one was open for 27% -> 37% of each run, Pallas kernels for 26% -> 28%
where the time goes in v4:
time: 713 us; the launch traced here: 704 us
  Pallas kernels  227 us (32%)
  waiting for transfers between devices  159 us (22%)
  matrix products  109 us (15%)
  other arithmetic  106 us (15%)
  local copies, waits for them, and re-layouts  72.9 us (10%)
  starting transfers between devices  15 us (2%)
  between operations  14.3 us (2%)
    add x4, other arithmetic, triangles(): da = with_layout_constraint(term if q == 0 else da + term, major)  89.1 us
    ppermute x22, waiting for transfers between devices, swap(): return lax.ppermute(v, axis, [(r, r ^ bit) for r in range(n)])  88.8 us
    pallas_call x10, Pallas kernels, to_channels(): pl.pallas_call(functools.partial(to_channels_kernel, slots), grid_spec=pl...  81.5 us
    all_gather x4, waiting for transfers between devices, shards(): groups.append(lax.all_gather(dx, 'col', axis=0) if even else dx)  70.2 us
    dot_general x5, matrix products, triangles(): term = jnp.einsum('cij,ckj->cik', dx_t, b_t, preferred_element_type=F32)  62.3 us
    dot_general x5, matrix products, triangles(): jnp.einsum('cik,cij->ckj', a_t, dx_t, preferred_element_type=F32)  46.5 us
    pallas_call x5, Pallas kernels, final_chunk(): pl.pallas_call(functools.partial(final_kernel, step, bool(chain)), grid=(...  41.9 us
    pallas_call x4, Pallas kernels, dx_chunk(): pl.pallas_call(functools.partial(dx_kernel, step, bool(chain)), grid=(row...  40.3 us
  transfers between devices with their start and end apart: 26, of which 11 were waited for; matrix products, arithmetic and copies ran while one was open for 37% of the time, Pallas kernels for 28%

profile of v4, /device:TPU:0, one launch (start us, length us, event | category | flops | bytes accessed | tf_op | source)
XLA Modules:
  0.0 703.6 jit_solution(17747977600718242493)
XLA Ops:
  23.6 23.6 %projections.1 = (bf16[160,160,128]{2,1,0:T(8,128)(2,1)}, bf16[160,160,128]{2,1,0:T(8,128)(2,1)}, bf16[160,160,128]{2,1,0:T(8,128)(2,1)}, bf16[160,160,128]{2,1,...) custom-call(bf16[160,160,128]{2,1,0:T(8,128)(2,1)} %pair.19, ...), custom_call_target="tpu_custom_call" | custom-call | flops 3355443200 | bytes 52428800 | tf_op jit(solution)/shard_map/projections/pallas_call | solution.py:157
  47.2 15.0 %dx_part.5 = (bf16[160,64,128]{2,1,0:T(8,128)(2,1)}, bf16[160,160,128]{2,1,0:T(8,128)(2,1)}, f32[800,128]{1,0:T(8,128)S(1)}) custom-call(bf16[160,160,128]{2,1,0:T(8,128)(2,1)} %pair.19, bf16[160,160,128]{2,1,0:T(8,128)(2,1)} %product.7, bf16[160,160,128]{2,1,0:T(8,128)(2,1)} %go.7, ...), custom_call_target="tpu_custom_call", output_to_operand_aliasing={{1}: (5, {})} | custom-call | flops 1342177280 | bytes 13107200 | tf_op jit(solution)/shard_map/dx_part/pallas_call | solution.py:104
  87.6 30.7 %all-gather.15.cloned.1.call-done = bf16[640,32,128]{2,1,0:T(8,128)(2,1)} async-done(((bf16[160,32,128]{2,1,0:T(8,128)(2,1)}), bf16[640,32,128]{2,1,0:T(8,128)(2,1)}) %all-gather.15.cloned.1.call-update) | async-done | bytes 5242896 | tf_op jit(solution)/shard_map/all_gather | solution.py:424
  118.3 15.9 %copy.35 = bf16[128,160,160]{1,2,0:T(8,128)(2,1)} copy(bf16[128,160,160]{0,2,1:T(8,128)(2,1)} %bitcast.104) | data formatting | bytes 13107200 | tf_op jit(solution)/shard_map/optimization_barrier | solution.py:378
  141.3 9.3 %convolution_convert_fusion.4.x = bf16[128,160,128]{2,1,0:T(8,128)(2,1)} fusion(bf16[128,160,160]{1,2,0:T(8,128)(2,1)} %copy.35, bf16[128,160,128]{2,1,0:T(8,128)(2,1)S(1)} %to_channels.10), kind=kOutput, calls=%fused_computation.9 | convolution fusion | flops 841482240 | bytes 17039360 | tf_op jit(solution)/shard_map/cik,cij->ckj/dot_general | solution.py:392
  180.5 12.5 %fusion = f32[128,160,160]{2,1,0:T(8,128)} fusion(bf16[128,160,128]{2,1,0:T(8,128)(2,1)S(1)} %to_channels.10, bf16[128,160,128]{2,1,0:T(8,128)(2,1)} %to_channels.11), kind=kOutput, calls=%fused_computation.26 | convolution fusion | flops 838860800 | bytes 23592960 | tf_op jit(solution)/shard_map/cij,ckj->cik/dot_general | solution.py:401
  192.9 59.0 %collective-permute-done.4.refs_2_ = bf16[160,96,128]{2,1,0:T(8,128)(2,1)} collective-permute-done((bf16[160,96,128]{2,1,0:T(8,128)(2,1)}, bf16[160,96,128]{2,1,0:T(8,128)(2,1)}, u32[]{:S(2)}, u32[]{:S(2)}) %collective-permute-start.4) | collective-permute-done | bytes 3932192 | tf_op jit(solution)/shard_map/ppermute | solution.py:304
  262.6 39.5 %all-gather.13.cloned.1.call-done = bf16[640,64,128]{2,1,0:T(8,128)(2,1)} async-done(((bf16[160,64,128]{2,1,0:T(8,128)(2,1)}), bf16[640,64,128]{2,1,0:T(8,128)(2,1)}) %all-gather.13.cloned.1.call-update) | async-done | bytes 10485776 | tf_op jit(solution)/shard_map/all_gather | solution.py:424
  312.3 9.3 %convolution_convert_fusion.3.x = bf16[128,160,128]{2,1,0:T(8,128)(2,1)} fusion(bf16[128,160,160]{1,2,0:T(8,128)(2,1)} %copy.35, bf16[128,160,128]{2,1,0:T(8,128)(2,1)S(1)} %to_channels.13), kind=kOutput, calls=%fused_computation.8 | convolution fusion | flops 841482240 | bytes 17039360 | tf_op jit(solution)/shard_map/cik,cij->ckj/dot_general | solution.py:392
  336.3 9.1 %to_channels.14 = bf16[128,160,128]{2,1,0:T(8,128)(2,1)} custom-call(s32[1]{0:T(128)} %bitcast.3.r, bf16[160,96,128]{2,1,0:T(8,128)(2,1)} %slice.46.refs_0_, bf16[160,96,128]{2,1,0:T(8,128)(2,1)} %collective-permute-done.7.refs_1_, bf16[160,96,128]{2,1,0:T(8,128)(2,1)} %collective-permute-done.4.refs_2_, bf16[160,96,128]{2,1,0:T(8,128)(2,1)} %collective-permute-done.8.refs_3_), custom_call_target="tpu_custom_call" | custom-call | flops 10485760 | bytes 10485760 | tf_op jit(solution)/shard_map/to_channels/pallas_call | solution.py:183
  345.4 12.5 %fusion.1 = f32[128,160,160]{2,1,0:T(8,128)} fusion(bf16[128,160,128]{2,1,0:T(8,128)(2,1)S(1)} %bitcast.72, bf16[128,160,128]{2,1,0:T(8,128)(2,1)} %to_channels.12), kind=kOutput, calls=%fused_computation.27 | convolution fusion | flops 838860800 | bytes 23592960 | tf_op jit(solution)/shard_map/cij,ckj->cik/dot_general | solution.py:401
  357.9 23.4 %add.65 = f32[128,160,160]{2,1,0:T(8,128)} add(f32[128,160,160]{2,1,0:T(8,128)} %fusion, f32[128,160,160]{2,1,0:T(8,128)} %fusion.1) | non-fusion elementwise | flops 3276800 | bytes 39321600 | tf_op jit(solution)/shard_map/add | solution.py:402
  391.5 9.3 %convolution_convert_fusion.2.x = bf16[128,160,128]{2,1,0:T(8,128)(2,1)} fusion(bf16[128,160,160]{1,2,0:T(8,128)(2,1)} %copy.35, bf16[128,160,128]{2,1,0:T(8,128)(2,1)S(1)} %to_channels.15), kind=kOutput, calls=%fused_computation.7 | convolution fusion | flops 841482240 | bytes 17039360 | tf_op jit(solution)/shard_map/cik,cij->ckj/dot_general | solution.py:392
  411.0 9.0 %to_channels.16 = bf16[128,160,128]{2,1,0:T(8,128)(2,1)} custom-call(s32[1]{0:T(128)} %bitcast.3.r, bf16[160,96,128]{2,1,0:T(8,128)(2,1)} %slice.46.refs_0_, bf16[160,96,128]{2,1,0:T(8,128)(2,1)} %collective-permute-done.7.refs_1_, bf16[160,96,128]{2,1,0:T(8,128)(2,1)} %collective-permute-done.4.refs_2_, bf16[160,96,128]{2,1,0:T(8,128)(2,1)} %collective-permute-done.8.refs_3_), custom_call_target="tpu_custom_call" | custom-call | flops 10485760 | bytes 10485760 | tf_op jit(solution)/shard_map/to_channels/pallas_call | solution.py:183
  422.5 12.5 %fusion.2 = f32[128,160,160]{2,1,0:T(8,128)} fusion(bf16[128,160,128]{2,1,0:T(8,128)(2,1)S(1)} %to_channels.15, bf16[128,160,128]{2,1,0:T(8,128)(2,1)} %to_channels.14), kind=kOutput, calls=%fused_computation.28 | convolution fusion | flops 838860800 | bytes 23592960 | tf_op jit(solution)/shard_map/cij,ckj->cik/dot_general | solution.py:401
  434.9 23.4 %add.67 = f32[128,160,160]{2,1,0:T(8,128)} add(f32[128,160,160]{2,1,0:T(8,128)} %add.65, f32[128,160,160]{2,1,0:T(8,128)} %fusion.2) | non-fusion elementwise | flops 3276800 | bytes 39321600 | tf_op jit(solution)/shard_map/add | solution.py:402
  469.6 9.3 %convolution_convert_fusion.1.x = bf16[128,160,128]{2,1,0:T(8,128)(2,1)} fusion(bf16[128,160,160]{1,2,0:T(8,128)(2,1)} %copy.35, bf16[128,160,128]{2,1,0:T(8,128)(2,1)S(1)} %to_channels.17), kind=kOutput, calls=%fused_computation.6 | convolution fusion | flops 841482240 | bytes 17039360 | tf_op jit(solution)/shard_map/cik,cij->ckj/dot_general | solution.py:392
  488.7 9.3 %to_channels.18 = bf16[128,160,128]{2,1,0:T(8,128)(2,1)} custom-call(s32[1]{0:T(128)} %bitcast.3.r, bf16[160,96,128]{2,1,0:T(8,128)(2,1)} %slice.46.refs_0_, bf16[160,96,128]{2,1,0:T(8,128)(2,1)} %collective-permute-done.7.refs_1_, bf16[160,96,128]{2,1,0:T(8,128)(2,1)} %collective-permute-done.4.refs_2_, bf16[160,96,128]{2,1,0:T(8,128)(2,1)} %collective-permute-done.8.refs_3_), custom_call_target="tpu_custom_call" | custom-call | flops 10485760 | bytes 10485760 | tf_op jit(solution)/shard_map/to_channels/pallas_call | solution.py:183
  501.1 12.4 %fusion.3 = f32[128,160,160]{2,1,0:T(8,128)} fusion(bf16[128,160,128]{2,1,0:T(8,128)(2,1)S(1)} %to_channels.17, bf16[128,160,128]{2,1,0:T(8,128)(2,1)} %to_channels.16), kind=kOutput, calls=%fused_computation.29 | convolution fusion | flops 838860800 | bytes 23592960 | tf_op jit(solution)/shard_map/cij,ckj->cik/dot_general | solution.py:401
  513.5 23.2 %add.69 = f32[128,160,160]{2,1,0:T(8,128)} add(f32[128,160,160]{2,1,0:T(8,128)} %add.67, f32[128,160,160]{2,1,0:T(8,128)} %fusion.3) | non-fusion elementwise | flops 3276800 | bytes 39321600 | tf_op jit(solution)/shard_map/add | solution.py:402
  547.9 9.3 %convolution_convert_fusion.x = bf16[128,160,128]{2,1,0:T(8,128)(2,1)} fusion(bf16[128,160,160]{1,2,0:T(8,128)(2,1)} %copy.35, bf16[128,160,128]{2,1,0:T(8,128)(2,1)S(1)} %to_channels.19), kind=kOutput, calls=%fused_computation.5 | convolution fusion | flops 841482240 | bytes 17039360 | tf_op jit(solution)/shard_map/cik,cij->ckj/dot_general | solution.py:392
  570.0 12.4 %fusion.4 = f32[128,160,160]{2,1,0:T(8,128)} fusion(bf16[128,160,128]{2,1,0:T(8,128)(2,1)S(1)} %to_channels.19, bf16[128,160,128]{2,1,0:T(8,128)(2,1)} %to_channels.18), kind=kOutput, calls=%fused_computation.30 | convolution fusion | flops 838860800 | bytes 23592960 | tf_op jit(solution)/shard_map/cij,ckj->cik/dot_general | solution.py:401
  582.5 19.1 %add.71 = bf16[128,160,160]{2,1,0:T(8,128)(2,1)} add(f32[128,160,160]{2,1,0:T(8,128)} %add.69, f32[128,160,160]{2,1,0:T(8,128)} %fusion.4) | non-fusion elementwise | flops 3276800 | bytes 32768000 | tf_op jit(solution)/shard_map/add | solution.py:402
  607.5 14.1 %copy.40 = bf16[128,160,160]{0,2,1:T(8,128)(2,1)} copy(bf16[128,160,160]{2,1,0:T(8,128)(2,1)} %add.71) | data formatting | bytes 13107200 | tf_op jit(solution)/shard_map/layout_constraint | solution.py:410
  (160 shorter events, 266.3 us)
Async XLA Ops:
  7.2 111.1 %all-gather.15.cloned.1.call-start = ((), (), s32[]{:S(2)}) async-start(), calls=%async_computation.3 | async-start | bytes 6553600 | tf_op jit(solution)/shard_map/all_gather | solution.py:424
  17.3 284.8 %all-gather.13.cloned.1.call-start = ((), (), s32[]{:S(2)}) async-start(), calls=%async_computation.2 | async-start | bytes 13107200 | tf_op jit(solution)/shard_map/all_gather | solution.py:424
  62.2 400.2 %all-gather.11.cloned.1.call-start = ((), (), s32[]{:S(2)}) async-start(), calls=%async_computation.1 | async-start | bytes 6553600 | tf_op jit(solution)/shard_map/all_gather | solution.py:424
  64.6 94.4 %collective-permute-start = (bf16[160,64,128]{2,1,0:T(8,128)(2,1)S(1)}, bf16[160,64,128]{2,1,0:T(8,128)(2,1)}, u32[]{:S(2)}, u32[]{:S(2)}) collective-permute-start(bf16[160,64,128]{2,1,0:T(8,128)(2,1)S(1)} %slice.45.refs_0_), channel_id=1, source_target_pairs={{0,8},{4,12},{8,0},{12,4},{1,9},{5,13},{9,1},{13,5},{2,10},{6,14},... | collective-permute-start | bytes 7864328 | tf_op jit(solution)/shard_map/ppermute | solution.py:304
  77.8 462.9 %all-gather.9.cloned.1.call-start = ((), (), s32[]{:S(2)}) async-start(), calls=%async_computation | async-start | bytes 6553600 | tf_op jit(solution)/shard_map/all_gather | solution.py:424
  159.0 8.6 %collective-permute-start.1 = (bf16[160,64,128]{2,1,0:T(8,128)(2,1)S(1)}, bf16[160,64,128]{2,1,0:T(8,128)(2,1)S(1)}, u32[]{:S(2)}, u32[]{:S(2)}) collective-permute-start(bf16[160,64,128]{2,1,0:T(8,128)(2,1)S(1)} %slice.45.refs_0_), channel_id=1, source_target_pairs={{0,4},{4,0},{8,12},{12,8},{1,5},{5,1},{9,13},{13,9},{2,6},{6,2},{1... | collective-permute-start | bytes 7864328 | tf_op jit(solution)/shard_map/ppermute | solution.py:304
  159.0 9.0 %collective-permute-start.2 = (bf16[160,64,128]{2,1,0:T(8,128)(2,1)}, bf16[160,64,128]{2,1,0:T(8,128)(2,1)}, u32[]{:S(2)}, u32[]{:S(2)}) collective-permute-start(bf16[160,64,128]{2,1,0:T(8,128)(2,1)} %collective-permute-done.refs_2_), channel_id=1, source_target_pairs={{0,4},{4,0},{8,12},{12,8},{1,5},{5,1},{9,13},{13,9},{2,6},{6,2},{1... | collective-permute-start | bytes 7864328 | tf_op jit(solution)/shard_map/ppermute | solution.py:304
  159.5 17.1 %collective-permute-start.3 = (bf16[2,160,32,128]{3,2,1,0:T(8,128)(2,1)}, bf16[2,160,32,128]{3,2,1,0:T(8,128)(2,1)}, u32[]{:S(2)}, u32[]{:S(2)}) collective-permute-start(bf16[2,160,32,128]{3,2,1,0:T(8,128)(2,1)} %copy-done.23), channel_id=1, source_target_pairs={{0,4},{4,0},{8,12},{12,8},{1,5},{5,1},{9,13},{13,9},{2,6},{6,2},{1... | collective-permute-start | bytes 7864328 | tf_op jit(solution)/shard_map/ppermute | solution.py:304
  164.2 87.7 %collective-permute-start.4 = (bf16[160,96,128]{2,1,0:T(8,128)(2,1)}, bf16[160,96,128]{2,1,0:T(8,128)(2,1)}, u32[]{:S(2)}, u32[]{:S(2)}) collective-permute-start(bf16[160,96,128]{2,1,0:T(8,128)(2,1)} %slice.46.refs_0_), channel_id=1, source_target_pairs={{0,8},{4,12},{8,0},{12,4},{1,9},{5,13},{9,1},{13,5},{2,10},{6,14},... | collective-permute-start | bytes 11796488 | tf_op jit(solution)/shard_map/ppermute | solution.py:304
  251.9 84.4 %collective-permute-start.7 = (bf16[160,96,128]{2,1,0:T(8,128)(2,1)}, bf16[160,96,128]{2,1,0:T(8,128)(2,1)}, u32[]{:S(2)}, u32[]{:S(2)}) collective-permute-start(bf16[160,96,128]{2,1,0:T(8,128)(2,1)} %slice.46.refs_0_), channel_id=1, source_target_pairs={{0,4},{4,0},{8,12},{12,8},{1,5},{5,1},{9,13},{13,9},{2,6},{6,2},{1... | collective-permute-start | bytes 11796488 | tf_op jit(solution)/shard_map/ppermute | solution.py:304
  251.9 84.4 %collective-permute-start.8 = (bf16[160,96,128]{2,1,0:T(8,128)(2,1)}, bf16[160,96,128]{2,1,0:T(8,128)(2,1)}, u32[]{:S(2)}, u32[]{:S(2)}) collective-permute-start(bf16[160,96,128]{2,1,0:T(8,128)(2,1)} %collective-permute-done.4.refs_2_), channel_id=1, source_target_pairs={{0,4},{4,0},{8,12},{12,8},{1,5},{5,1},{9,13},{13,9},{2,6},{6,2},{1... | collective-permute-start | bytes 11796488 | tf_op jit(solution)/shard_map/ppermute | solution.py:304
  331.4 49.9 %collective-permute-start.5 = (bf16[2,160,32,128]{3,2,1,0:T(8,128)(2,1)}, bf16[2,160,32,128]{3,2,1,0:T(8,128)(2,1)}, u32[]{:S(2)}, u32[]{:S(2)}) collective-permute-start(bf16[2,160,32,128]{3,2,1,0:T(8,128)(2,1)} %get-tuple-element.123), channel_id=1, source_target_pairs={{0,4},{4,0},{8,12},{12,8},{1,5},{5,1},{9,13},{13,9},{2,6},{6,2},{1... | collective-permute-start | bytes 7864328 | tf_op jit(solution)/shard_map/ppermute | solution.py:304
  334.8 48.9 %collective-permute-start.6 = (bf16[1,160,32,128]{3,2,1,0:T(8,128)(2,1)}, bf16[1,160,32,128]{3,2,1,0:T(8,128)(2,1)S(1)}, u32[]{:S(2)}, u32[]{:S(2)}) collective-permute-start(bf16[1,160,32,128]{3,2,1,0:T(8,128)(2,1)} %get-tuple-element.180), channel_id=1, source_target_pairs={{0,8},{4,12},{8,0},{12,4},{1,9},{5,13},{9,1},{13,5},{2,10},{6,14},... | collective-permute-start | bytes 3932168 | tf_op jit(solution)/shard_map/ppermute | solution.py:304
  410.7 47.7 %collective-permute-start.9 = (bf16[2,160,32,128]{3,2,1,0:T(8,128)(2,1)}, bf16[2,160,32,128]{3,2,1,0:T(8,128)(2,1)}, u32[]{:S(2)}, u32[]{:S(2)}) collective-permute-start(bf16[2,160,32,128]{3,2,1,0:T(8,128)(2,1)} %get-tuple-element.135), channel_id=1, source_target_pairs={{0,4},{4,0},{8,12},{12,8},{1,5},{5,1},{9,13},{13,9},{2,6},{6,2},{1... | collective-permute-start | bytes 7864328 | tf_op jit(solution)/shard_map/ppermute | solution.py:304
  421.6 40.8 %collective-permute-start.10 = (bf16[1,160,32,128]{3,2,1,0:T(8,128)(2,1)}, bf16[1,160,32,128]{3,2,1,0:T(8,128)(2,1)}, u32[]{:S(2)}, u32[]{:S(2)}) collective-permute-start(bf16[1,160,32,128]{3,2,1,0:T(8,128)(2,1)} %get-tuple-element.182), channel_id=1, source_target_pairs={{0,8},{4,12},{8,0},{12,4},{1,9},{5,13},{9,1},{13,5},{2,10},{6,14},... | collective-permute-start | bytes 3932168 | tf_op jit(solution)/shard_map/ppermute | solution.py:304
  488.7 48.1 %collective-permute-start.11 = (bf16[2,160,32,128]{3,2,1,0:T(8,128)(2,1)}, bf16[2,160,32,128]{3,2,1,0:T(8,128)(2,1)}, u32[]{:S(2)}, u32[]{:S(2)}) collective-permute-start(bf16[2,160,32,128]{3,2,1,0:T(8,128)(2,1)} %get-tuple-element.145), channel_id=1, source_target_pairs={{0,4},{4,0},{8,12},{12,8},{1,5},{5,1},{9,13},{13,9},{2,6},{6,2},{1... | collective-permute-start | bytes 7864328 | tf_op jit(solution)/shard_map/ppermute | solution.py:304
  499.9 40.8 %collective-permute-start.12 = (bf16[1,160,32,128]{3,2,1,0:T(8,128)(2,1)}, bf16[1,160,32,128]{3,2,1,0:T(8,128)(2,1)}, u32[]{:S(2)}, u32[]{:S(2)}) collective-permute-start(bf16[1,160,32,128]{3,2,1,0:T(8,128)(2,1)} %get-tuple-element.184), channel_id=1, source_target_pairs={{0,8},{4,12},{8,0},{12,4},{1,9},{5,13},{9,1},{13,5},{2,10},{6,14},... | collective-permute-start | bytes 3932168 | tf_op jit(solution)/shard_map/ppermute | solution.py:304
  567.1 34.4 %collective-permute-start.13 = (bf16[2,160,32,128]{3,2,1,0:T(8,128)(2,1)}, bf16[2,160,32,128]{3,2,1,0:T(8,128)(2,1)}, u32[]{:S(2)}, u32[]{:S(2)}) collective-permute-start(bf16[2,160,32,128]{3,2,1,0:T(8,128)(2,1)} %get-tuple-element.155), channel_id=1, source_target_pairs={{0,4},{4,0},{8,12},{12,8},{1,5},{5,1},{9,13},{13,9},{2,6},{6,2},{1... | collective-permute-start | bytes 7864328 | tf_op jit(solution)/shard_map/ppermute | solution.py:304
  569.3 34.7 %collective-permute-start.14 = (bf16[1,160,32,128]{3,2,1,0:T(8,128)(2,1)}, bf16[1,160,32,128]{3,2,1,0:T(8,128)(2,1)}, u32[]{:S(2)}, u32[]{:S(2)}) collective-permute-start(bf16[1,160,32,128]{3,2,1,0:T(8,128)(2,1)} %get-tuple-element.186), channel_id=1, source_target_pairs={{0,8},{4,12},{8,0},{12,4},{1,9},{5,13},{9,1},{13,5},{2,10},{6,14},... | collective-permute-start | bytes 3932168 | tf_op jit(solution)/shard_map/ppermute | solution.py:304
  605.9 50.7 %collective-permute-start.15 = (bf16[1,160,32,128]{3,2,1,0:T(8,128)(2,1)}, bf16[1,160,32,128]{3,2,1,0:T(8,128)(2,1)}, u32[]{:S(2)}, u32[]{:S(2)}) collective-permute-start(bf16[1,160,32,128]{3,2,1,0:T(8,128)(2,1)} %get-tuple-element.187), channel_id=1, source_target_pairs={{0,8},{4,12},{8,0},{12,4},{1,9},{5,13},{9,1},{13,5},{2,10},{6,14},... | collective-permute-start | bytes 3932168 | tf_op jit(solution)/shard_map/ppermute | solution.py:304
  666.8 7.2 %collective-permute-start.17 = (f32[400,128]{1,0:T(8,128)S(1)}, f32[400,128]{1,0:T(8,128)S(1)}, u32[]{:S(2)}, u32[]{:S(2)}) collective-permute-start(f32[400,128]{1,0:T(8,128)S(1)} %dynamic-slice_bitcast_fusion), channel_id=1, source_target_pairs={{0,8},{4,12},{8,0},{12,4},{1,9},{5,13},{9,1},{13,5},{2,10},{6,14},... | collective-permute-start | bytes 614408 | tf_op jit(solution)/shard_map/ppermute | solution.py:304
  674.0 4.7 collective-permute-start.18
  678.8 6.2 collective-permute-start.19
  689.7 5.8 collective-permute-start.21
  (32 other events, 222.7 us)
Sparse Core Ops, SparseCore 0:
  17.5 100.7 all-gather.14
  119.8 182.2 all-gather.12
  303.7 96.2 all-gather.10
  401.4 96.4 all-gather.8

commit v5 on v4

--- a/solution.py
+++ b/solution.py
@@ -234,7 +234,7 @@
     )(x)
 
 
-def final_kernel(step, chained, pair, da, db0, db1, g_ga, g_pa, g_gb, g_pb, dol, wcat, norms, acc_in, *rest):
+def final_kernel(step, chained, pair, da0, da1, db0, db1, g_ga, g_pa, g_gb, g_pb, dol, wcat, norms, acc_in, *rest):
     gp, acc, flip = rest[-3:]
     c = pair.shape[-1]
 
@@ -247,7 +247,7 @@
     def body(s, carry):
         hat, inv = layer_normalize(tile(pair, s, step).astype(F32))
         zn = (hat * norms[0:1] + norms[1:2]).astype(BF16)
-        dav = tile(da, s, step).astype(F32)
+        dav = tile(da0, s, step).astype(F32) + tile(da1, s, step).astype(F32)
         dbv = tile(flip, s, step)
         parts = [
             (dav * tile(g_ga, s, step).astype(F32)).astype(BF16),
@@ -281,7 +281,7 @@
     return pl.pallas_call(
         functools.partial(final_kernel, step, bool(chain)),
         grid=(size // ib,),
-        in_specs=[blk, blk, own, own]
+        in_specs=[blk, blk, blk, own, own]
         + [blk] * 5
         + [full(wcat.shape), full(norms.shape), full(acc.shape)]
         + ([pl.BlockSpec(memory_space=pl.ANY)] if chain else []),
@@ -290,14 +290,14 @@
             jax.ShapeDtypeStruct((rows, cols, c), BF16),
             jax.ShapeDtypeStruct(acc.shape, F32),
         ],
-        input_output_aliases={12: 0} if chain else {},
+        input_output_aliases={13: 0} if chain else {},
         scratch_shapes=[pltpu.VMEM((ib, cols, c), F32)],
         compiler_params=pltpu.CompilerParams(vmem_limit_bytes=VMEM_LIMIT),
         cost_estimate=pl.CostEstimate(
             flops=20 * n * c * c, bytes_accessed=22 * n * c, transcendentals=n
         ),
         name="final_part",
-    )(pair, da, db0, db1, *gs, dol, wcat, norms, acc, *chain)
+    )(pair, *da, db0, db1, *gs, dol, wcat, norms, acc, *chain)
 
 
 def swap(v, axis, n, bit):
@@ -340,22 +340,21 @@
     return kept[0], come[0]
 
 
+def tree_sum(terms):
+    while len(terms) > 1:
+        terms = [x + y for x, y in zip(terms[::2], terms[1::2])]
+    return terms[0]
+
+
 def sum_all(v, n_row, n_col):
-    steps = [("row", n_row, b) for b in bits_of(n_row)] + [("col", n_col, b) for b in bits_of(n_col)]
-    halved = []
-    for k, (axis, n, bit) in enumerate(steps):
-        half = v.shape[0] // 2
-        if 0 < k < len(steps) - 1 and v.shape[0] % 16 == 0:
-            at = (lax.axis_index(axis) // bit) % 2
-            pairs = v.reshape((2, half) + v.shape[1:])
-            v = pick(pairs, at) + swap(pick(pairs, 1 - at), axis, n, bit)
-            halved.append((axis, n, bit, at))
-        else:
-            v = v + swap(v, axis, n, bit)
-    for axis, n, bit, at in halved[::-1]:
-        got = swap(v, axis, n, bit)
-        v = jnp.where(at == 0, jnp.concatenate([v, got]), jnp.concatenate([got, v]))
-    return v
+    r = lax.axis_index("row")
+    parts = v.reshape((n_row, -1) + v.shape[1:])
+    terms = [pick(parts, r)]
+    terms += [swap(pick(parts, r ^ t), "row", n_row, t) for t in range(1, n_row)]
+    v = tree_sum(terms)
+    v = tree_sum([v] + [swap(v, "col", n_col, t) for t in range(1, n_col)])
+    slots = jnp.stack([v] + [swap(v, "row", n_row, t) for t in range(1, n_row)])
+    return jnp.concatenate([pick(slots, r ^ p) for p in range(n_row)])
 
 
 def triangles_plain(n_row, n_col, dx, a, b_swapped):
@@ -365,7 +364,14 @@
     part = jnp.einsum("ijc,ikc->kjc", block, a, preferred_element_type=F32).astype(BF16)
     db = lax.psum_scatter(part, "row", scatter_dimension=1, tiled=True)
     da = jnp.einsum("ijc,kjc->ikc", block, b_all, preferred_element_type=F32)
-    return da.astype(BF16), [(db, jnp.zeros_like(db))], [(0, rows)]
+    return [da.astype(BF16)], [(db, jnp.zeros_like(db))], [(0, rows)]
+
+
+def to_pairs(terms, major):
+    total = terms[0]
+    if len(terms) > 1:
+        total = sum(term.astype(F32) for term in terms).astype(BF16)
+    return jnp.transpose(with_layout_constraint(total, major), (1, 2, 0))
 
 
 def triangles(n, groups, size, a, b_swapped, acc):
@@ -379,7 +385,7 @@
     groups = [first] + groups[1:]
     major = Layout(major_to_minor=(0, 1, 2))
     da, b_t = None, None
-    db, spans = [], []
+    db, spans, terms, pairs = [], [], [], []
     for group in groups:
         for at in range(group.shape[2] // size):
             q = len(spans)
@@ -388,6 +394,10 @@
                 slots, start = (b_early, off) if off < split else (b_late, off - split)
                 b_t = slots_to_channels(slots, r, start, size)
                 group, da, b_t = lax.optimization_barrier((group, da, b_t))
+                if pairs:
+                    pairs[-1] = da
+                else:
+                    terms[-1] = da
             dx_t = gathered_to_channels(group, r, at, size)
             part = jnp.einsum("cik,cij->ckj", a_t, dx_t, preferred_element_type=F32).astype(BF16)
             kept, sent = from_channels(part, n)
@@ -398,8 +408,8 @@
             else:
                 dx_t, kept, sent = lax.optimization_barrier((dx_t, kept, sent))
             half, come = reduce_cores(kept, sent, n)
-            term = jnp.einsum("cij,ckj->cik", dx_t, b_t, preferred_element_type=F32)
-            da = with_layout_constraint(term if q == 0 else da + term, major)
+            da = jnp.einsum("cij,ckj->cik", dx_t, b_t, preferred_element_type=F32)
+            da = with_layout_constraint(da.astype(BF16), major)
             if q == 0:
                 da, half, *late = lax.optimization_barrier((da, half, *late))
                 b_late = core_slots(late, n)
@@ -407,8 +417,13 @@
                 da, half, db[-1][1] = lax.optimization_barrier((da, half, db[-1][1]))
             db.append(list(reduce_chips(half, come, n)))
             spans.append((off, size))
-    da = with_layout_constraint(da.astype(BF16), major)
-    return jnp.transpose(da, (1, 2, 0)), db, spans, acc
+            terms.append(da)
+            if off + 2 * size == cols:
+                da = to_pairs(terms, major)
+                terms = []
+                pairs.append(da)
+    pairs.append(to_pairs(terms, major))
+    return pairs, db, spans, acc
 
 
 def shards(n_row, n_col, pair, product, mask, grad_out, weights, norms):
@@ -432,6 +447,7 @@
         da, db, spans, acc = triangles(n_row, groups, size, a, b_swapped, acc)
     else:
         da, db, spans = triangles_plain(n_row, n_col, groups[0], a, b_swapped)
+    da = da if len(da) == 2 else [da[0], jnp.zeros_like(da[0])]
     wcat = jnp.transpose(weights[:5], (1, 0, 2)).reshape(c, 5 * c)
     chain = []
     for (db0, db1), (off, size) in zip(db, spans):

time: 713 us -> 690 us (0.968)
  other arithmetic: 106 us -> 44.3 us
  waiting for transfers between devices: 159 us -> 179 us
  local copies, waits for them, and re-layouts: 72.9 us -> 82.9 us
    add x8 -> x2, other arithmetic: 89.2 us -> 0.06 us  [tree_sum(): terms = [x + y for x, y in zip(terms[::2], terms[1::2])]]
    all_gather x4, waiting for transfers between devices: 70.2 us -> 111 us  [shards(): groups.append(lax.all_gather(dx, 'col', axis=0) if even else dx)]
    convert_element_type x0 -> x1, other arithmetic: none -> 21.2 us  [to_pairs(): total = sum((term.astype(F32) for term in terms)).astype(BF16)]
    ppermute x22 -> x25, waiting for transfers between devices: 88.8 us -> 68.4 us  [swap(): return lax.ppermute(v, axis, [(r, r ^ bit) for r in range(n)])]
    another operation x1 -> x2, local copies, waits for them, and re-layouts: 14.1 us -> 28.1 us  [to_pairs(): return jnp.transpose(with_layout_constraint(total, major), (1, 2, 0))]
    dot_general x5, matrix products: 46.5 us -> 53.9 us  [triangles(): jnp.einsum('cik,cij->ckj', a_t, dx_t, preferred_element_type=F32)]
    ppermute x22 -> x25, starting transfers between devices: 14.5 us -> 20.3 us  [swap(): return lax.ppermute(v, axis, [(r, r ^ bit) for r in range(n)])]
    unnamed x59 -> x49, local copies, waits for them, and re-layouts: 17.6 us -> 13.7 us
  transfers between devices with their start and end apart: 26 -> 29, of which waited for: 11 -> 15; matrix products, arithmetic and copies ran while one was open for 37% -> 31% of each run, Pallas kernels for 28% -> 29%
where the time goes in v5:
time: 690 us; the launch traced here: 682 us
  Pallas kernels  230 us (33%)
  waiting for transfers between devices  179 us (26%)
  matrix products  110 us (16%)
  local copies, waits for them, and re-layouts  82.9 us (12%)
  other arithmetic  44.3 us (6%)
  starting transfers between devices  20.9 us (3%)
  between operations  14.5 us (2%)
    all_gather x4, waiting for transfers between devices, shards(): groups.append(lax.all_gather(dx, 'col', axis=0) if even else dx)  111 us
    pallas_call x10, Pallas kernels, to_channels(): pl.pallas_call(functools.partial(to_channels_kernel, slots), grid_spec=pl...  81.6 us
    ppermute x25, waiting for transfers between devices, swap(): return lax.ppermute(v, axis, [(r, r ^ bit) for r in range(n)])  68.4 us
    dot_general x5, matrix products, triangles(): da = jnp.einsum('cij,ckj->cik', dx_t, b_t, preferred_element_type=F32)  55.6 us
    dot_general x5, matrix products, triangles(): jnp.einsum('cik,cij->ckj', a_t, dx_t, preferred_element_type=F32)  53.9 us
    pallas_call x5, Pallas kernels, final_chunk(): pl.pallas_call(functools.partial(final_kernel, step, bool(chain)), grid=(...  43.1 us
    pallas_call x5, Pallas kernels, from_channels(): pl.pallas_call(functools.partial(from_channels_kernel, slots), grid=(lead...  41.9 us
    pallas_call x4, Pallas kernels, dx_chunk(): pl.pallas_call(functools.partial(dx_kernel, step, bool(chain)), grid=(row...  40.1 us
  transfers between devices with their start and end apart: 29, of which 15 were waited for; matrix products, arithmetic and copies ran while one was open for 31% of the time, Pallas kernels for 29%

profile of v5, /device:TPU:0, one launch (start us, length us, event | category | flops | bytes accessed | tf_op | source)
XLA Modules:
  0.0 681.8 jit_solution(12528141676025258974)
XLA Ops:
  23.6 23.6 %projections.1 = (bf16[160,160,128]{2,1,0:T(8,128)(2,1)}, bf16[160,160,128]{2,1,0:T(8,128)(2,1)}, bf16[160,160,128]{2,1,0:T(8,128)(2,1)}, bf16[160,160,128]{2,1,...) custom-call(bf16[160,160,128]{2,1,0:T(8,128)(2,1)} %pair.19, ...), custom_call_target="tpu_custom_call" | custom-call | flops 3355443200 | bytes 52428800 | tf_op jit(solution)/shard_map/projections/pallas_call | solution.py:157
  47.2 14.9 %dx_part.5 = (bf16[160,64,128]{2,1,0:T(8,128)(2,1)}, bf16[160,160,128]{2,1,0:T(8,128)(2,1)}, f32[800,128]{1,0:T(8,128)S(1)}) custom-call(bf16[160,160,128]{2,1,0:T(8,128)(2,1)} %pair.19, bf16[160,160,128]{2,1,0:T(8,128)(2,1)} %product.7, bf16[160,160,128]{2,1,0:T(8,128)(2,1)} %go.7, ...), custom_call_target="tpu_custom_call", output_to_operand_aliasing={{1}: (5, {})} | custom-call | flops 1342177280 | bytes 13107200 | tf_op jit(solution)/shard_map/dx_part/pallas_call | solution.py:104
  91.3 26.9 %all-gather.13.cloned.1.call-done = bf16[640,32,128]{2,1,0:T(8,128)(2,1)} async-done(((bf16[160,32,128]{2,1,0:T(8,128)(2,1)}), bf16[640,32,128]{2,1,0:T(8,128)(2,1)}) %all-gather.13.cloned.1.call-update) | async-done | bytes 5242896 | tf_op jit(solution)/shard_map/all_gather | solution.py:439
  118.2 15.9 %copy.37 = bf16[128,160,160]{1,2,0:T(8,128)(2,1)} copy(bf16[128,160,160]{0,2,1:T(8,128)(2,1)} %bitcast.124) | data formatting | bytes 13107200 | tf_op jit(solution)/shard_map/optimization_barrier | solution.py:384
  141.3 11.1 %convolution_convert_fusion.9.x = bf16[128,160,128]{2,1,0:T(8,128)(2,1)} fusion(bf16[128,160,160]{1,2,0:T(8,128)(2,1)} %copy.37, bf16[128,160,128]{2,1,0:T(8,128)(2,1)S(1)} %to_channels.10), kind=kOutput, calls=%fused_computation.15 | convolution fusion | flops 841482240 | bytes 17039360 | tf_op jit(solution)/shard_map/cik,cij->ckj/dot_general | solution.py:402
  180.0 10.9 %convolution_convert_fusion.4 = bf16[128,160,160]{2,1,0:T(8,128)(2,1)} fusion(bf16[128,160,128]{2,1,0:T(8,128)(2,1)} %copy-done.2, bf16[128,160,128]{2,1,0:T(8,128)(2,1)} %to_channels.11), kind=kOutput, calls=%fused_computation.5 | convolution fusion | flops 842137600 | bytes 17039360 | tf_op jit(solution)/shard_map/cij,ckj->cik/dot_general | solution.py:411
  195.7 13.3 %collective-permute-done.4.refs_2_ = bf16[160,96,128]{2,1,0:T(8,128)(2,1)} collective-permute-done((bf16[160,96,128]{2,1,0:T(8,128)(2,1)}, bf16[160,96,128]{2,1,0:T(8,128)(2,1)}, u32[]{:S(2)}, u32[]{:S(2)}) %collective-permute-start.4) | collective-permute-done | bytes 3932192 | tf_op jit(solution)/shard_map/ppermute | solution.py:304
  218.3 83.8 %all-gather.11.cloned.1.call-done = bf16[640,64,128]{2,1,0:T(8,128)(2,1)} async-done(((bf16[160,64,128]{2,1,0:T(8,128)(2,1)}), bf16[640,64,128]{2,1,0:T(8,128)(2,1)}) %all-gather.11.cloned.1.call-update) | async-done | bytes 10485776 | tf_op jit(solution)/shard_map/all_gather | solution.py:439
  309.4 11.3 %convolution_convert_fusion.8.x = bf16[128,160,128]{2,1,0:T(8,128)(2,1)} fusion(bf16[128,160,160]{1,2,0:T(8,128)(2,1)} %copy.37, bf16[128,160,128]{2,1,0:T(8,128)(2,1)S(1)} %to_channels.13), kind=kOutput, calls=%fused_computation.14 | convolution fusion | flops 841482240 | bytes 17039360 | tf_op jit(solution)/shard_map/cik,cij->ckj/dot_general | solution.py:402
  333.9 9.5 %to_channels.14 = bf16[128,160,128]{2,1,0:T(8,128)(2,1)} custom-call(s32[1]{0:T(128)} %bitcast.2.r, bf16[160,96,128]{2,1,0:T(8,128)(2,1)} %slice.49.refs_0_, bf16[160,96,128]{2,1,0:T(8,128)(2,1)} %collective-permute-done.7.refs_1_, bf16[160,96,128]{2,1,0:T(8,128)(2,1)} %collective-permute-done.4.refs_2_, bf16[160,96,128]{2,1,0:T(8,128)(2,1)} %collective-permute-done.8.refs_3_), custom_call_target="tpu_custom_call" | custom-call | flops 10485760 | bytes 10485760 | tf_op jit(solution)/shard_map/to_channels/pallas_call | solution.py:183
  343.4 11.0 %convolution_convert_fusion.3 = bf16[128,160,160]{2,1,0:T(8,128)(2,1)} fusion(bf16[128,160,128]{2,1,0:T(8,128)(2,1)} %copy-done.1, bf16[128,160,128]{2,1,0:T(8,128)(2,1)} %to_channels.12), kind=kOutput, calls=%fused_computation.4 | convolution fusion | flops 842137600 | bytes 17039360 | tf_op jit(solution)/shard_map/cij,ckj->cik/dot_general | solution.py:411
  373.3 9.2 %convolution_convert_fusion.7.x = bf16[128,160,128]{2,1,0:T(8,128)(2,1)} fusion(bf16[128,160,160]{1,2,0:T(8,128)(2,1)} %copy.37, bf16[128,160,128]{2,1,0:T(8,128)(2,1)S(1)} %to_channels.15), kind=kOutput, calls=%fused_computation.13 | convolution fusion | flops 841482240 | bytes 17039360 | tf_op jit(solution)/shard_map/cik,cij->ckj/dot_general | solution.py:402
  397.6 9.0 %to_channels.16 = bf16[128,160,128]{2,1,0:T(8,128)(2,1)} custom-call(s32[1]{0:T(128)} %bitcast.2.r, bf16[160,96,128]{2,1,0:T(8,128)(2,1)} %slice.49.refs_0_, bf16[160,96,128]{2,1,0:T(8,128)(2,1)} %collective-permute-done.7.refs_1_, bf16[160,96,128]{2,1,0:T(8,128)(2,1)} %collective-permute-done.4.refs_2_, bf16[160,96,128]{2,1,0:T(8,128)(2,1)} %collective-permute-done.8.refs_3_), custom_call_target="tpu_custom_call" | custom-call | flops 10485760 | bytes 10485760 | tf_op jit(solution)/shard_map/to_channels/pallas_call | solution.py:183
  406.7 11.8 %convolution_convert_fusion.2 = bf16[128,160,160]{2,1,0:T(8,128)(2,1)} fusion(bf16[128,160,128]{2,1,0:T(8,128)(2,1)} %copy-done, bf16[128,160,128]{2,1,0:T(8,128)(2,1)} %to_channels.14), kind=kOutput, calls=%fused_computation.3 | convolution fusion | flops 842137600 | bytes 17039360 | tf_op jit(solution)/shard_map/cij,ckj->cik/dot_general | solution.py:411
  434.9 11.2 %convolution_convert_fusion.6.x = bf16[128,160,128]{2,1,0:T(8,128)(2,1)} fusion(bf16[128,160,160]{1,2,0:T(8,128)(2,1)} %copy.37, bf16[128,160,128]{2,1,0:T(8,128)(2,1)S(1)} %to_channels.17), kind=kOutput, calls=%fused_computation.12 | convolution fusion | flops 841482240 | bytes 17039360 | tf_op jit(solution)/shard_map/cik,cij->ckj/dot_general | solution.py:402
  459.6 9.0 %to_channels.18 = bf16[128,160,128]{2,1,0:T(8,128)(2,1)} custom-call(s32[1]{0:T(128)} %bitcast.2.r, bf16[160,96,128]{2,1,0:T(8,128)(2,1)} %slice.49.refs_0_, bf16[160,96,128]{2,1,0:T(8,128)(2,1)} %collective-permute-done.7.refs_1_, bf16[160,96,128]{2,1,0:T(8,128)(2,1)} %collective-permute-done.4.refs_2_, bf16[160,96,128]{2,1,0:T(8,128)(2,1)} %collective-permute-done.8.refs_3_), custom_call_target="tpu_custom_call" | custom-call | flops 10485760 | bytes 10485760 | tf_op jit(solution)/shard_map/to_channels/pallas_call | solution.py:183
  468.6 11.0 %convolution_convert_fusion.1 = bf16[128,160,160]{2,1,0:T(8,128)(2,1)} fusion(bf16[128,160,128]{2,1,0:T(8,128)(2,1)} %copy-done.3, bf16[128,160,128]{2,1,0:T(8,128)(2,1)} %to_channels.16), kind=kOutput, calls=%fused_computation.2 | convolution fusion | flops 842137600 | bytes 17039360 | tf_op jit(solution)/shard_map/cij,ckj->cik/dot_general | solution.py:411
  489.5 21.2 %add_convert_fusion = bf16[128,160,160]{2,1,0:T(8,128)(2,1)} fusion(bf16[128,160,160]{2,1,0:T(8,128)(2,1)} %convolution_convert_fusion.1, bf16[128,160,160]{2,1,0:T(8,128)(2,1)} %convolution_convert_fusion.2, bf16[128,160,160]{2,1,0:T(8,128)(2,1)} %convolution_convert_fusion.3, bf16[128,160,160]{2,1,0:T(8,128)(2,1)} %convolution_convert_fusion.4), kind=kLoop, calls=%fused_computation | loop fusion | flops 26214400 | bytes 32768000 | tf_op jit(solution)/shard_map/convert_element_type | solution.py:373
  510.7 14.1 %copy.41 = bf16[128,160,160]{0,2,1:T(8,128)(2,1)} copy(bf16[128,160,160]{2,1,0:T(8,128)(2,1)} %add_convert_fusion) | data formatting | bytes 13107200 | tf_op jit(solution)/shard_map/layout_constraint | solution.py:374
  532.2 11.1 %convolution_convert_fusion.5.x = bf16[128,160,128]{2,1,0:T(8,128)(2,1)} fusion(bf16[128,160,160]{1,2,0:T(8,128)(2,1)} %copy.37, bf16[128,160,128]{2,1,0:T(8,128)(2,1)S(1)} %to_channels.19), kind=kOutput, calls=%fused_computation.11 | convolution fusion | flops 841482240 | bytes 17039360 | tf_op jit(solution)/shard_map/cik,cij->ckj/dot_general | solution.py:402
  556.7 11.0 %convolution_convert_fusion = bf16[128,160,160]{2,1,0:T(8,128)(2,1)} fusion(bf16[128,160,128]{2,1,0:T(8,128)(2,1)} %copy-done.4, bf16[128,160,128]{2,1,0:T(8,128)(2,1)} %to_channels.18), kind=kOutput, calls=%fused_computation.1 | convolution fusion | flops 842137600 | bytes 17039360 | tf_op jit(solution)/shard_map/cij,ckj->cik/dot_general | solution.py:411
  570.9 15.7 %collective-permute-done.14 = bf16[1,160,32,128]{3,2,1,0:T(8,128)(2,1)} collective-permute-done((bf16[1,160,32,128]{3,2,1,0:T(8,128)(2,1)}, bf16[1,160,32,128]{3,2,1,0:T(8,128)(2,1)}, u32[]{:S(2)}, u32[]{:S(2)}) %collective-permute-start.14) | collective-permute-done | bytes 1310752 | tf_op jit(solution)/shard_map/ppermute | solution.py:304
  590.6 14.1 %copy.43 = bf16[128,160,160]{0,2,1:T(8,128)(2,1)} copy(bf16[128,160,160]{2,1,0:T(8,128)(2,1)} %convolution_convert_fusion) | data formatting | bytes 13107200 | tf_op jit(solution)/shard_map/layout_constraint | solution.py:374
  613.2 8.9 %final_part.6 = (bf16[160,160,128]{2,1,0:T(8,128)(2,1)}, f32[800,128]{1,0:T(8,128)S(1)}) custom-call(bf16[160,160,128]{2,1,0:T(8,128)(2,1)} %pair.19, bf16[160,160,128]{2,1,0:T(8,128)(2,1)} %bitcast.98, bf16[160,160,128]{2,1,0:T(8,128)(2,1)} %bitcast.103, bf16[160,32,128]{2,1,0:T(8,128)(2,1)S(1)} %copy-done.7, ...), custom_call_target="tpu_custom_call", output_to_operand_aliasing={{0}: (13, {})} | custom-call | flops 1677721600 | bytes 14417920 | tf_op jit(solution)/shard_map/final_part/pallas_call | solution.py:281
  (150 shorter events, 277.9 us)
Async XLA Ops:
  7.2 111.1 %all-gather.13.cloned.1.call-start = ((), (), s32[]{:S(2)}) async-start(), calls=%async_computation.2 | async-start | bytes 6553600 | tf_op jit(solution)/shard_map/all_gather | solution.py:439
  17.3 284.8 %all-gather.11.cloned.1.call-start = ((), (), s32[]{:S(2)}) async-start(), calls=%async_computation.1 | async-start | bytes 13107200 | tf_op jit(solution)/shard_map/all_gather | solution.py:439
  62.1 365.5 %all-gather.15.cloned.1.call-start = ((), (), s32[]{:S(2)}) async-start(), calls=%async_computation.3 | async-start | bytes 6553600 | tf_op jit(solution)/shard_map/all_gather | solution.py:439
  64.7 97.4 %collective-permute-start = (bf16[160,64,128]{2,1,0:T(8,128)(2,1)S(1)}, bf16[160,64,128]{2,1,0:T(8,128)(2,1)}, u32[]{:S(2)}, u32[]{:S(2)}) collective-permute-start(bf16[160,64,128]{2,1,0:T(8,128)(2,1)S(1)} %slice.48.refs_0_), channel_id=1, source_target_pairs={{0,8},{4,12},{8,0},{12,4},{1,9},{5,13},{9,1},{13,5},{2,10},{6,14},... | collective-permute-start | bytes 7864328 | tf_op jit(solution)/shard_map/ppermute | solution.py:304
  72.4 136.6 %collective-permute-start.4 = (bf16[160,96,128]{2,1,0:T(8,128)(2,1)}, bf16[160,96,128]{2,1,0:T(8,128)(2,1)}, u32[]{:S(2)}, u32[]{:S(2)}) collective-permute-start(bf16[160,96,128]{2,1,0:T(8,128)(2,1)} %slice.49.refs_0_), channel_id=1, source_target_pairs={{0,8},{4,12},{8,0},{12,4},{1,9},{5,13},{9,1},{13,5},{2,10},{6,14},... | collective-permute-start | bytes 11796488 | tf_op jit(solution)/shard_map/ppermute | solution.py:304
  162.1 8.8 %collective-permute-start.1 = (bf16[160,64,128]{2,1,0:T(8,128)(2,1)S(1)}, bf16[160,64,128]{2,1,0:T(8,128)(2,1)}, u32[]{:S(2)}, u32[]{:S(2)}) collective-permute-start(bf16[160,64,128]{2,1,0:T(8,128)(2,1)S(1)} %slice.48.refs_0_), channel_id=1, source_target_pairs={{0,4},{4,0},{8,12},{12,8},{1,5},{5,1},{9,13},{13,9},{2,6},{6,2},{1... | collective-permute-start | bytes 7864328 | tf_op jit(solution)/shard_map/ppermute | solution.py:304
  162.1 9.0 %collective-permute-start.2 = (bf16[160,64,128]{2,1,0:T(8,128)(2,1)}, bf16[160,64,128]{2,1,0:T(8,128)(2,1)}, u32[]{:S(2)}, u32[]{:S(2)}) collective-permute-start(bf16[160,64,128]{2,1,0:T(8,128)(2,1)} %collective-permute-done.refs_2_), channel_id=1, source_target_pairs={{0,4},{4,0},{8,12},{12,8},{1,5},{5,1},{9,13},{13,9},{2,6},{6,2},{1... | collective-permute-start | bytes 7864328 | tf_op jit(solution)/shard_map/ppermute | solution.py:304
  162.6 28.3 %collective-permute-start.3 = (bf16[2,160,32,128]{3,2,1,0:T(8,128)(2,1)}, bf16[2,160,32,128]{3,2,1,0:T(8,128)(2,1)}, u32[]{:S(2)}, u32[]{:S(2)}) collective-permute-start(bf16[2,160,32,128]{3,2,1,0:T(8,128)(2,1)} %get-tuple-element.113), channel_id=1, source_target_pairs={{0,4},{4,0},{8,12},{12,8},{1,5},{5,1},{9,13},{13,9},{2,6},{6,2},{1... | collective-permute-start | bytes 7864328 | tf_op jit(solution)/shard_map/ppermute | solution.py:304
  162.7 362.1 %all-gather.9.cloned.1.call-start = ((), (), s32[]{:S(2)}) async-start(), calls=%async_computation | async-start | bytes 6553600 | tf_op jit(solution)/shard_map/all_gather | solution.py:439
  209.0 124.9 %collective-permute-start.7 = (bf16[160,96,128]{2,1,0:T(8,128)(2,1)}, bf16[160,96,128]{2,1,0:T(8,128)(2,1)}, u32[]{:S(2)}, u32[]{:S(2)}) collective-permute-start(bf16[160,96,128]{2,1,0:T(8,128)(2,1)} %slice.49.refs_0_), channel_id=1, source_target_pairs={{0,4},{4,0},{8,12},{12,8},{1,5},{5,1},{9,13},{13,9},{2,6},{6,2},{1... | collective-permute-start | bytes 11796488 | tf_op jit(solution)/shard_map/ppermute | solution.py:304
  209.0 124.9 %collective-permute-start.8 = (bf16[160,96,128]{2,1,0:T(8,128)(2,1)}, bf16[160,96,128]{2,1,0:T(8,128)(2,1)}, u32[]{:S(2)}, u32[]{:S(2)}) collective-permute-start(bf16[160,96,128]{2,1,0:T(8,128)(2,1)} %collective-permute-done.4.refs_2_), channel_id=1, source_target_pairs={{0,4},{4,0},{8,12},{12,8},{1,5},{5,1},{9,13},{13,9},{2,6},{6,2},{1... | collective-permute-start | bytes 11796488 | tf_op jit(solution)/shard_map/ppermute | solution.py:304
  330.7 23.7 %collective-permute-start.5 = (bf16[2,160,32,128]{3,2,1,0:T(8,128)(2,1)}, bf16[2,160,32,128]{3,2,1,0:T(8,128)(2,1)}, u32[]{:S(2)}, u32[]{:S(2)}) collective-permute-start(bf16[2,160,32,128]{3,2,1,0:T(8,128)(2,1)} %get-tuple-element.122), channel_id=1, source_target_pairs={{0,4},{4,0},{8,12},{12,8},{1,5},{5,1},{9,13},{13,9},{2,6},{6,2},{1... | collective-permute-start | bytes 7864328 | tf_op jit(solution)/shard_map/ppermute | solution.py:304
  332.4 31.4 %collective-permute-start.6 = (bf16[1,160,32,128]{3,2,1,0:T(8,128)(2,1)}, bf16[1,160,32,128]{3,2,1,0:T(8,128)(2,1)}, u32[]{:S(2)}, u32[]{:S(2)}) collective-permute-start(bf16[1,160,32,128]{3,2,1,0:T(8,128)(2,1)} %get-tuple-element.180), channel_id=1, source_target_pairs={{0,8},{4,12},{8,0},{12,4},{1,9},{5,13},{9,1},{13,5},{2,10},{6,14},... | collective-permute-start | bytes 3932168 | tf_op jit(solution)/shard_map/ppermute | solution.py:304
  392.4 26.1 %collective-permute-start.9 = (bf16[2,160,32,128]{3,2,1,0:T(8,128)(2,1)}, bf16[2,160,32,128]{3,2,1,0:T(8,128)(2,1)}, u32[]{:S(2)}, u32[]{:S(2)}) collective-permute-start(bf16[2,160,32,128]{3,2,1,0:T(8,128)(2,1)} %get-tuple-element.135), channel_id=1, source_target_pairs={{0,4},{4,0},{8,12},{12,8},{1,5},{5,1},{9,13},{13,9},{2,6},{6,2},{1... | collective-permute-start | bytes 7864328 | tf_op jit(solution)/shard_map/ppermute | solution.py:304
  396.1 31.5 %collective-permute-start.10 = (bf16[1,160,32,128]{3,2,1,0:T(8,128)(2,1)}, bf16[1,160,32,128]{3,2,1,0:T(8,128)(2,1)}, u32[]{:S(2)}, u32[]{:S(2)}) collective-permute-start(bf16[1,160,32,128]{3,2,1,0:T(8,128)(2,1)} %get-tuple-element.182), channel_id=1, source_target_pairs={{0,8},{4,12},{8,0},{12,4},{1,9},{5,13},{9,1},{13,5},{2,10},{6,14},... | collective-permute-start | bytes 3932168 | tf_op jit(solution)/shard_map/ppermute | solution.py:304
  456.1 23.5 %collective-permute-start.11 = (bf16[2,160,32,128]{3,2,1,0:T(8,128)(2,1)}, bf16[2,160,32,128]{3,2,1,0:T(8,128)(2,1)}, u32[]{:S(2)}, u32[]{:S(2)}) collective-permute-start(bf16[2,160,32,128]{3,2,1,0:T(8,128)(2,1)} %get-tuple-element.145), channel_id=1, source_target_pairs={{0,4},{4,0},{8,12},{12,8},{1,5},{5,1},{9,13},{13,9},{2,6},{6,2},{1... | collective-permute-start | bytes 7864328 | tf_op jit(solution)/shard_map/ppermute | solution.py:304
  458.0 31.5 %collective-permute-start.12 = (bf16[1,160,32,128]{3,2,1,0:T(8,128)(2,1)}, bf16[1,160,32,128]{3,2,1,0:T(8,128)(2,1)}, u32[]{:S(2)}, u32[]{:S(2)}) collective-permute-start(bf16[1,160,32,128]{3,2,1,0:T(8,128)(2,1)} %get-tuple-element.184), channel_id=1, source_target_pairs={{0,8},{4,12},{8,0},{12,4},{1,9},{5,13},{9,1},{13,5},{2,10},{6,14},... | collective-permute-start | bytes 3932168 | tf_op jit(solution)/shard_map/ppermute | solution.py:304
  553.2 14.5 %collective-permute-start.13 = (bf16[2,160,32,128]{3,2,1,0:T(8,128)(2,1)}, bf16[2,160,32,128]{3,2,1,0:T(8,128)(2,1)}, u32[]{:S(2)}, u32[]{:S(2)}) collective-permute-start(bf16[2,160,32,128]{3,2,1,0:T(8,128)(2,1)} %get-tuple-element.155), channel_id=1, source_target_pairs={{0,4},{4,0},{8,12},{12,8},{1,5},{5,1},{9,13},{13,9},{2,6},{6,2},{1... | collective-permute-start | bytes 7864328 | tf_op jit(solution)/shard_map/ppermute | solution.py:304
  555.1 31.5 %collective-permute-start.14 = (bf16[1,160,32,128]{3,2,1,0:T(8,128)(2,1)}, bf16[1,160,32,128]{3,2,1,0:T(8,128)(2,1)}, u32[]{:S(2)}, u32[]{:S(2)}) collective-permute-start(bf16[1,160,32,128]{3,2,1,0:T(8,128)(2,1)} %get-tuple-element.186), channel_id=1, source_target_pairs={{0,8},{4,12},{8,0},{12,4},{1,9},{5,13},{9,1},{13,5},{2,10},{6,14},... | collective-permute-start | bytes 3932168 | tf_op jit(solution)/shard_map/ppermute | solution.py:304
  588.6 50.7 %collective-permute-start.15 = (bf16[1,160,32,128]{3,2,1,0:T(8,128)(2,1)}, bf16[1,160,32,128]{3,2,1,0:T(8,128)(2,1)}, u32[]{:S(2)}, u32[]{:S(2)}) collective-permute-start(bf16[1,160,32,128]{3,2,1,0:T(8,128)(2,1)} %get-tuple-element.187), channel_id=1, source_target_pairs={{0,8},{4,12},{8,0},{12,4},{1,9},{5,13},{9,1},{13,5},{2,10},{6,14},... | collective-permute-start | bytes 3932168 | tf_op jit(solution)/shard_map/ppermute | solution.py:304
  648.5 6.5 collective-permute-start.18
  655.0 6.7 collective-permute-start.19
  655.1 11.1 %collective-permute-start.20 = (f32[200,128]{1,0:T(8,128)S(1)}, f32[200,128]{1,0:T(8,128)S(1)}, u32[]{:S(2)}, u32[]{:S(2)}) collective-permute-start(f32[200,128]{1,0:T(8,128)S(1)} %fusion), channel_id=1, source_target_pairs={{0,2},{1,3},{2,0},{3,1},{4,6},{5,7},{6,4},{7,5},{8,10},{9,11},{10,... | collective-permute-start | bytes 307208 | tf_op jit(solution)/shard_map/ppermute | solution.py:304
  656.4 9.8 %collective-permute-start.21 = (f32[200,128]{1,0:T(8,128)S(1)}, f32[200,128]{1,0:T(8,128)S(1)}, u32[]{:S(2)}, u32[]{:S(2)}) collective-permute-start(f32[200,128]{1,0:T(8,128)S(1)} %fusion), channel_id=1, source_target_pairs={{0,3},{1,2},{2,1},{3,0},{4,7},{5,6},{6,5},{7,4},{8,11},{9,10},{10,... | collective-permute-start | bytes 307208 | tf_op jit(solution)/shard_map/ppermute | solution.py:304
  (30 other events, 188.4 us)
Sparse Core Ops, SparseCore 0:
  17.4 100.7 all-gather.12
  119.8 182.2 all-gather.10
  303.7 96.2 all-gather.14
  401.4 96.4 all-gather.8

commit v6 on v5

--- a/solution.py
+++ b/solution.py
@@ -393,10 +393,11 @@
             if q > 0:
                 slots, start = (b_early, off) if off < split else (b_late, off - split)
                 b_t = slots_to_channels(slots, r, start, size)
-                group, da, b_t = lax.optimization_barrier((group, da, b_t))
                 if pairs:
+                    group, da, b_t, db[-1][1] = lax.optimization_barrier((group, da, b_t, db[-1][1]))
                     pairs[-1] = da
                 else:
+                    group, da, b_t = lax.optimization_barrier((group, da, b_t))
                     terms[-1] = da
             dx_t = gathered_to_channels(group, r, at, size)
             part = jnp.einsum("cik,cij->ckj", a_t, dx_t, preferred_element_type=F32).astype(BF16)
@@ -413,6 +414,8 @@
             if q == 0:
                 da, half, *late = lax.optimization_barrier((da, half, *late))
                 b_late = core_slots(late, n)
+            elif pairs:
+                da, half = lax.optimization_barrier((da, half))
             else:
                 da, half, db[-1][1] = lax.optimization_barrier((da, half, db[-1][1]))
             db.append(list(reduce_chips(half, come, n)))
@@ -431,8 +434,6 @@
     even = n_row == n_col and n_row & (n_row - 1) == 0 and cols % 32 == 0 and rows % 16 == 0
     size = 32 if even else cols
     widths = [size] * (cols // size)
-    if len(widths) > 3:
-        widths[1:3] = [2 * size]
     groups, chain, off = [], [], 0
     for width in widths:
         dx, *chain = dx_chunk(pair, product, grad_out, weights, norms, off, width, chain)

time: 690 us -> 657 us (0.952)
  waiting for transfers between devices: 179 us -> 148 us
    all_gather x4 -> x5, waiting for transfers between devices: 111 us -> 81.8 us  [shards(): groups.append(lax.all_gather(dx, 'col', axis=0) if even else dx)]
    pallas_call x4 -> x5, Pallas kernels: 40.1 us -> 42.2 us  [dx_chunk(): pl.pallas_call(functools.partial(dx_kernel, step, bool(chain)), grid=(row...]
  transfers between devices with their start and end apart: 29 -> 30, of which waited for: 15 -> 15; matrix products, arithmetic and copies ran while one was open for 31% -> 31% of each run, Pallas kernels for 29% -> 31%
where the time goes in v6:
time: 657 us; the launch traced here: 649 us
  Pallas kernels  232 us (35%)
  waiting for transfers between devices  148 us (23%)
  matrix products  109 us (17%)
  local copies, waits for them, and re-layouts  84.6 us (13%)
  other arithmetic  40 us (6%)
  starting transfers between devices  20.3 us (3%)
  between operations  14.3 us (2%)
    all_gather x5, waiting for transfers between devices, shards(): groups.append(lax.all_gather(dx, 'col', axis=0) if even else dx)  81.8 us
    pallas_call x10, Pallas kernels, to_channels(): pl.pallas_call(functools.partial(to_channels_kernel, slots), grid_spec=pl...  81.2 us
    ppermute x25, waiting for transfers between devices, swap(): return lax.ppermute(v, axis, [(r, r ^ bit) for r in range(n)])  66.5 us
    dot_general x5, matrix products, triangles(): da = jnp.einsum('cij,ckj->cik', dx_t, b_t, preferred_element_type=F32)  54.7 us
    dot_general x5, matrix products, triangles(): jnp.einsum('cik,cij->ckj', a_t, dx_t, preferred_element_type=F32)  54.4 us
    pallas_call x5, Pallas kernels, final_chunk(): pl.pallas_call(functools.partial(final_kernel, step, bool(chain)), grid=(...  43.1 us
    pallas_call x5, Pallas kernels, dx_chunk(): pl.pallas_call(functools.partial(dx_kernel, step, bool(chain)), grid=(row...  42.2 us
    pallas_call x5, Pallas kernels, from_channels(): pl.pallas_call(functools.partial(from_channels_kernel, slots), grid=(lead...  41.9 us
  transfers between devices with their start and end apart: 30, of which 15 were waited for; matrix products, arithmetic and copies ran while one was open for 31% of the time, Pallas kernels for 31%

profile of v6, /device:TPU:0, one launch (start us, length us, event | category | flops | bytes accessed | tf_op | source)
XLA Modules:
  0.0 648.7 jit_solution(5588957648790410141)
XLA Ops:
  23.6 23.7 %projections.1 = (bf16[160,160,128]{2,1,0:T(8,128)(2,1)}, bf16[160,160,128]{2,1,0:T(8,128)(2,1)}, bf16[160,160,128]{2,1,0:T(8,128)(2,1)}, bf16[160,160,128]{2,1,...) custom-call(bf16[160,160,128]{2,1,0:T(8,128)(2,1)} %pair.21, ...), custom_call_target="tpu_custom_call" | custom-call | flops 3355443200 | bytes 52428800 | tf_op jit(solution)/shard_map/projections/pallas_call | solution.py:157
  93.6 24.6 %all-gather.15.cloned.1.call-done = bf16[640,32,128]{2,1,0:T(8,128)(2,1)} async-done(((bf16[160,32,128]{2,1,0:T(8,128)(2,1)}), bf16[640,32,128]{2,1,0:T(8,128)(2,1)}) %all-gather.15.cloned.1.call-update) | async-done | bytes 5242896 | tf_op jit(solution)/shard_map/all_gather | solution.py:440
  118.2 15.7 %copy.38 = bf16[128,160,160]{1,2,0:T(8,128)(2,1)} copy(bf16[128,160,160]{0,2,1:T(8,128)(2,1)} %bitcast.125) | data formatting | bytes 13107200 | tf_op jit(solution)/shard_map/optimization_barrier | solution.py:384
  143.4 9.3 %convolution_convert_fusion.9.x = bf16[128,160,128]{2,1,0:T(8,128)(2,1)} fusion(bf16[128,160,160]{1,2,0:T(8,128)(2,1)} %copy.38, bf16[128,160,128]{2,1,0:T(8,128)(2,1)S(1)} %to_channels.10), kind=kOutput, calls=%fused_computation.15 | convolution fusion | flops 841482240 | bytes 17039360 | tf_op jit(solution)/shard_map/cik,cij->ckj/dot_general | solution.py:403
  171.6 8.8 %to_channels.11 = bf16[128,160,128]{2,1,0:T(8,128)(2,1)} custom-call(s32[1]{0:T(128)} %bitcast.2.r, bf16[160,64,128]{2,1,0:T(8,128)(2,1)S(1)} %slice.48.refs_0_, bf16[160,64,128]{2,1,0:T(8,128)(2,1)} %collective-permute-done.1.refs_1_, bf16[160,64,128]{2,1,0:T(8,128)(2,1)} %collective-permute-done.refs_2_, bf16[160,64,128]{2,1,0:T(8,128)(2,1)} %collective-permute-done.2.refs_3_), custom_call_target="tpu_custom_call" | custom-call | flops 10485760 | bytes 10485760 | tf_op jit(solution)/shard_map/to_channels/pallas_call | solution.py:183
  184.4 10.9 %convolution_convert_fusion.4 = bf16[128,160,160]{2,1,0:T(8,128)(2,1)} fusion(bf16[128,160,128]{2,1,0:T(8,128)(2,1)} %copy-done, bf16[128,160,128]{2,1,0:T(8,128)(2,1)} %to_channels.11), kind=kOutput, calls=%fused_computation.5 | convolution fusion | flops 842137600 | bytes 17039360 | tf_op jit(solution)/shard_map/cij,ckj->cik/dot_general | solution.py:412
  195.3 15.9 %collective-permute-done.4.refs_2_ = bf16[160,96,128]{2,1,0:T(8,128)(2,1)} collective-permute-done((bf16[160,96,128]{2,1,0:T(8,128)(2,1)}, bf16[160,96,128]{2,1,0:T(8,128)(2,1)}, u32[]{:S(2)}, u32[]{:S(2)}) %collective-permute-start.4) | collective-permute-done | bytes 3932192 | tf_op jit(solution)/shard_map/ppermute | solution.py:304
  228.0 11.1 %convolution_convert_fusion.8.x = bf16[128,160,128]{2,1,0:T(8,128)(2,1)} fusion(bf16[128,160,160]{1,2,0:T(8,128)(2,1)} %copy.38, bf16[128,160,128]{2,1,0:T(8,128)(2,1)S(1)} %to_channels.13), kind=kOutput, calls=%fused_computation.14 | convolution fusion | flops 841482240 | bytes 17039360 | tf_op jit(solution)/shard_map/cik,cij->ckj/dot_general | solution.py:403
  252.4 10.9 %convolution_convert_fusion.3 = bf16[128,160,160]{2,1,0:T(8,128)(2,1)} fusion(bf16[128,160,128]{2,1,0:T(8,128)(2,1)} %copy-done.3, bf16[128,160,128]{2,1,0:T(8,128)(2,1)} %to_channels.12), kind=kOutput, calls=%fused_computation.4 | convolution fusion | flops 842137600 | bytes 17039360 | tf_op jit(solution)/shard_map/cij,ckj->cik/dot_general | solution.py:412
  268.0 14.1 %collective-permute-done.6 = bf16[1,160,32,128]{3,2,1,0:T(8,128)(2,1)} collective-permute-done((bf16[1,160,32,128]{3,2,1,0:T(8,128)(2,1)}, bf16[1,160,32,128]{3,2,1,0:T(8,128)(2,1)}, u32[]{:S(2)}, u32[]{:S(2)}) %collective-permute-start.6) | collective-permute-done | bytes 1310752 | tf_op jit(solution)/shard_map/ppermute | solution.py:304
  282.1 9.2 %to_channels.14 = bf16[128,160,128]{2,1,0:T(8,128)(2,1)} custom-call(s32[1]{0:T(128)} %bitcast.2.r, bf16[160,96,128]{2,1,0:T(8,128)(2,1)} %slice.49.refs_0_, bf16[160,96,128]{2,1,0:T(8,128)(2,1)} %collective-permute-done.7.refs_1_, bf16[160,96,128]{2,1,0:T(8,128)(2,1)} %collective-permute-done.4.refs_2_, bf16[160,96,128]{2,1,0:T(8,128)(2,1)} %collective-permute-done.8.refs_3_), custom_call_target="tpu_custom_call" | custom-call | flops 10485760 | bytes 10485760 | tf_op jit(solution)/shard_map/to_channels/pallas_call | solution.py:183
  291.3 23.0 %all-gather.17.cloned.1.call-done = bf16[640,32,128]{2,1,0:T(8,128)(2,1)} async-done(((bf16[160,32,128]{2,1,0:T(8,128)(2,1)}), bf16[640,32,128]{2,1,0:T(8,128)(2,1)}) %all-gather.17.cloned.1.call-update) | async-done | bytes 5242896 | tf_op jit(solution)/shard_map/all_gather | solution.py:440
  321.5 11.4 %convolution_convert_fusion.7.x = bf16[128,160,128]{2,1,0:T(8,128)(2,1)} fusion(bf16[128,160,160]{1,2,0:T(8,128)(2,1)} %copy.38, bf16[128,160,128]{2,1,0:T(8,128)(2,1)S(1)} %to_channels.15), kind=kOutput, calls=%fused_computation.13 | convolution fusion | flops 841482240 | bytes 17039360 | tf_op jit(solution)/shard_map/cik,cij->ckj/dot_general | solution.py:403
  348.0 9.0 %to_channels.16 = bf16[128,160,128]{2,1,0:T(8,128)(2,1)} custom-call(s32[1]{0:T(128)} %bitcast.2.r, bf16[160,96,128]{2,1,0:T(8,128)(2,1)} %slice.49.refs_0_, bf16[160,96,128]{2,1,0:T(8,128)(2,1)} %collective-permute-done.7.refs_1_, bf16[160,96,128]{2,1,0:T(8,128)(2,1)} %collective-permute-done.4.refs_2_, bf16[160,96,128]{2,1,0:T(8,128)(2,1)} %collective-permute-done.8.refs_3_), custom_call_target="tpu_custom_call" | custom-call | flops 10485760 | bytes 10485760 | tf_op jit(solution)/shard_map/to_channels/pallas_call | solution.py:183
  357.0 11.0 %convolution_convert_fusion.2 = bf16[128,160,160]{2,1,0:T(8,128)(2,1)} fusion(bf16[128,160,128]{2,1,0:T(8,128)(2,1)} %copy-done.1, bf16[128,160,128]{2,1,0:T(8,128)(2,1)} %to_channels.14), kind=kOutput, calls=%fused_computation.3 | convolution fusion | flops 842137600 | bytes 17039360 | tf_op jit(solution)/shard_map/cij,ckj->cik/dot_general | solution.py:412
  377.9 34.3 %all-gather.19.cloned.1.call-done = bf16[640,32,128]{2,1,0:T(8,128)(2,1)} async-done(((bf16[160,32,128]{2,1,0:T(8,128)(2,1)}), bf16[640,32,128]{2,1,0:T(8,128)(2,1)}) %all-gather.19.cloned.1.call-update) | async-done | bytes 5242896 | tf_op jit(solution)/shard_map/all_gather | solution.py:440
  419.4 11.4 %convolution_convert_fusion.6.x = bf16[128,160,128]{2,1,0:T(8,128)(2,1)} fusion(bf16[128,160,160]{1,2,0:T(8,128)(2,1)} %copy.38, bf16[128,160,128]{2,1,0:T(8,128)(2,1)S(1)} %to_channels.17), kind=kOutput, calls=%fused_computation.12 | convolution fusion | flops 841482240 | bytes 17039360 | tf_op jit(solution)/shard_map/cik,cij->ckj/dot_general | solution.py:403
  445.9 9.2 %to_channels.18 = bf16[128,160,128]{2,1,0:T(8,128)(2,1)} custom-call(s32[1]{0:T(128)} %bitcast.2.r, bf16[160,96,128]{2,1,0:T(8,128)(2,1)} %slice.49.refs_0_, bf16[160,96,128]{2,1,0:T(8,128)(2,1)} %collective-permute-done.7.refs_1_, bf16[160,96,128]{2,1,0:T(8,128)(2,1)} %collective-permute-done.4.refs_2_, bf16[160,96,128]{2,1,0:T(8,128)(2,1)} %collective-permute-done.8.refs_3_), custom_call_target="tpu_custom_call" | custom-call | flops 10485760 | bytes 10485760 | tf_op jit(solution)/shard_map/to_channels/pallas_call | solution.py:183
  455.1 11.0 %convolution_convert_fusion.1 = bf16[128,160,160]{2,1,0:T(8,128)(2,1)} fusion(bf16[128,160,128]{2,1,0:T(8,128)(2,1)} %copy-done.2, bf16[128,160,128]{2,1,0:T(8,128)(2,1)} %to_channels.16), kind=kOutput, calls=%fused_computation.2 | convolution fusion | flops 842137600 | bytes 17039360 | tf_op jit(solution)/shard_map/cij,ckj->cik/dot_general | solution.py:412
  479.3 19.1 %add_convert_fusion = bf16[128,160,160]{2,1,0:T(8,128)(2,1)} fusion(bf16[128,160,160]{2,1,0:T(8,128)(2,1)S(1)} %copy-done.21, bf16[128,160,160]{2,1,0:T(8,128)(2,1)} %convolution_convert_fusion.2, bf16[128,160,160]{2,1,0:T(8,128)(2,1)} %convolution_convert_fusion.3, bf16[128,160,160]{2,1,0:T(8,128)(2,1)} %convolution_convert_fusion.4), kind=kLoop, calls=%fused_computation | loop fusion | flops 26214400 | bytes 32768000 | tf_op jit(solution)/shard_map/convert_element_type | solution.py:373
  498.3 14.1 %copy.42 = bf16[128,160,160]{0,2,1:T(8,128)(2,1)} copy(bf16[128,160,160]{2,1,0:T(8,128)(2,1)} %add_convert_fusion) | data formatting | bytes 13107200 | tf_op jit(solution)/shard_map/layout_constraint | solution.py:374
  519.6 11.1 %convolution_convert_fusion.5.x = bf16[128,160,128]{2,1,0:T(8,128)(2,1)} fusion(bf16[128,160,160]{1,2,0:T(8,128)(2,1)} %copy.38, bf16[128,160,128]{2,1,0:T(8,128)(2,1)S(1)} %to_channels.19), kind=kOutput, calls=%fused_computation.11 | convolution fusion | flops 841482240 | bytes 17039360 | tf_op jit(solution)/shard_map/cik,cij->ckj/dot_general | solution.py:403
  540.9 11.0 %convolution_convert_fusion = bf16[128,160,160]{2,1,0:T(8,128)(2,1)} fusion(bf16[128,160,128]{2,1,0:T(8,128)(2,1)} %copy-done.4, bf16[128,160,128]{2,1,0:T(8,128)(2,1)} %to_channels.18), kind=kOutput, calls=%fused_computation.1 | convolution fusion | flops 842137600 | bytes 17039360 | tf_op jit(solution)/shard_map/cij,ckj->cik/dot_general | solution.py:412
  557.9 14.1 %copy.44 = bf16[128,160,160]{0,2,1:T(8,128)(2,1)} copy(bf16[128,160,160]{2,1,0:T(8,128)(2,1)} %convolution_convert_fusion) | data formatting | bytes 13107200 | tf_op jit(solution)/shard_map/layout_constraint | solution.py:374
  (154 shorter events, 290.6 us)
Async XLA Ops:
  7.2 111.0 %all-gather.15.cloned.1.call-start = ((), (), s32[]{:S(2)}) async-start(), calls=%async_computation.2 | async-start | bytes 6553600 | tf_op jit(solution)/shard_map/all_gather | solution.py:440
  17.3 203.3 %all-gather.13.cloned.1.call-start = ((), (), s32[]{:S(2)}) async-start(), calls=%async_computation.1 | async-start | bytes 6553600 | tf_op jit(solution)/shard_map/all_gather | solution.py:440
  55.8 258.5 %all-gather.17.cloned.1.call-start = ((), (), s32[]{:S(2)}) async-start(), calls=%async_computation.3 | async-start | bytes 6553600 | tf_op jit(solution)/shard_map/all_gather | solution.py:440
  64.3 347.9 %all-gather.19.cloned.1.call-start = ((), (), s32[]{:S(2)}) async-start(), calls=%async_computation.4 | async-start | bytes 6553600 | tf_op jit(solution)/shard_map/all_gather | solution.py:440
  67.0 95.5 %collective-permute-start = (bf16[160,64,128]{2,1,0:T(8,128)(2,1)S(1)}, bf16[160,64,128]{2,1,0:T(8,128)(2,1)}, u32[]{:S(2)}, u32[]{:S(2)}) collective-permute-start(bf16[160,64,128]{2,1,0:T(8,128)(2,1)S(1)} %slice.48.refs_0_), channel_id=1, source_target_pairs={{0,8},{4,12},{8,0},{12,4},{1,9},{5,13},{9,1},{13,5},{2,10},{6,14},... | collective-permute-start | bytes 7864328 | tf_op jit(solution)/shard_map/ppermute | solution.py:304
  74.7 136.5 %collective-permute-start.4 = (bf16[160,96,128]{2,1,0:T(8,128)(2,1)}, bf16[160,96,128]{2,1,0:T(8,128)(2,1)}, u32[]{:S(2)}, u32[]{:S(2)}) collective-permute-start(bf16[160,96,128]{2,1,0:T(8,128)(2,1)} %slice.49.refs_0_), channel_id=1, source_target_pairs={{0,8},{4,12},{8,0},{12,4},{1,9},{5,13},{9,1},{13,5},{2,10},{6,14},... | collective-permute-start | bytes 11796488 | tf_op jit(solution)/shard_map/ppermute | solution.py:304
  162.6 8.8 %collective-permute-start.1 = (bf16[160,64,128]{2,1,0:T(8,128)(2,1)S(1)}, bf16[160,64,128]{2,1,0:T(8,128)(2,1)}, u32[]{:S(2)}, u32[]{:S(2)}) collective-permute-start(bf16[160,64,128]{2,1,0:T(8,128)(2,1)S(1)} %slice.48.refs_0_), channel_id=1, source_target_pairs={{0,4},{4,0},{8,12},{12,8},{1,5},{5,1},{9,13},{13,9},{2,6},{6,2},{1... | collective-permute-start | bytes 7864328 | tf_op jit(solution)/shard_map/ppermute | solution.py:304
  162.6 9.0 %collective-permute-start.2 = (bf16[160,64,128]{2,1,0:T(8,128)(2,1)}, bf16[160,64,128]{2,1,0:T(8,128)(2,1)}, u32[]{:S(2)}, u32[]{:S(2)}) collective-permute-start(bf16[160,64,128]{2,1,0:T(8,128)(2,1)} %collective-permute-done.refs_2_), channel_id=1, source_target_pairs={{0,4},{4,0},{8,12},{12,8},{1,5},{5,1},{9,13},{13,9},{2,6},{6,2},{1... | collective-permute-start | bytes 7864328 | tf_op jit(solution)/shard_map/ppermute | solution.py:304
  163.1 17.3 %collective-permute-start.3 = (bf16[2,160,32,128]{3,2,1,0:T(8,128)(2,1)}, bf16[2,160,32,128]{3,2,1,0:T(8,128)(2,1)}, u32[]{:S(2)}, u32[]{:S(2)}) collective-permute-start(bf16[2,160,32,128]{3,2,1,0:T(8,128)(2,1)} %get-tuple-element.118), channel_id=1, source_target_pairs={{0,4},{4,0},{8,12},{12,8},{1,5},{5,1},{9,13},{13,9},{2,6},{6,2},{1... | collective-permute-start | bytes 7864328 | tf_op jit(solution)/shard_map/ppermute | solution.py:304
  163.1 349.3 %all-gather.11.cloned.1.call-start = ((), (), s32[]{:S(2)}) async-start(), calls=%async_computation | async-start | bytes 6553600 | tf_op jit(solution)/shard_map/all_gather | solution.py:440
  211.2 70.9 %collective-permute-start.7 = (bf16[160,96,128]{2,1,0:T(8,128)(2,1)}, bf16[160,96,128]{2,1,0:T(8,128)(2,1)}, u32[]{:S(2)}, u32[]{:S(2)}) collective-permute-start(bf16[160,96,128]{2,1,0:T(8,128)(2,1)} %slice.49.refs_0_), channel_id=1, source_target_pairs={{0,4},{4,0},{8,12},{12,8},{1,5},{5,1},{9,13},{13,9},{2,6},{6,2},{1... | collective-permute-start | bytes 11796488 | tf_op jit(solution)/shard_map/ppermute | solution.py:304
  211.2 70.9 %collective-permute-start.8 = (bf16[160,96,128]{2,1,0:T(8,128)(2,1)}, bf16[160,96,128]{2,1,0:T(8,128)(2,1)}, u32[]{:S(2)}, u32[]{:S(2)}) collective-permute-start(bf16[160,96,128]{2,1,0:T(8,128)(2,1)} %collective-permute-done.4.refs_2_), channel_id=1, source_target_pairs={{0,4},{4,0},{8,12},{12,8},{1,5},{5,1},{9,13},{13,9},{2,6},{6,2},{1... | collective-permute-start | bytes 11796488 | tf_op jit(solution)/shard_map/ppermute | solution.py:304
  249.1 14.3 %collective-permute-start.5 = (bf16[2,160,32,128]{3,2,1,0:T(8,128)(2,1)}, bf16[2,160,32,128]{3,2,1,0:T(8,128)(2,1)}, u32[]{:S(2)}, u32[]{:S(2)}) collective-permute-start(bf16[2,160,32,128]{3,2,1,0:T(8,128)(2,1)} %get-tuple-element.128), channel_id=1, source_target_pairs={{0,4},{4,0},{8,12},{12,8},{1,5},{5,1},{9,13},{13,9},{2,6},{6,2},{1... | collective-permute-start | bytes 7864328 | tf_op jit(solution)/shard_map/ppermute | solution.py:304
  250.6 31.5 %collective-permute-start.6 = (bf16[1,160,32,128]{3,2,1,0:T(8,128)(2,1)}, bf16[1,160,32,128]{3,2,1,0:T(8,128)(2,1)}, u32[]{:S(2)}, u32[]{:S(2)}) collective-permute-start(bf16[1,160,32,128]{3,2,1,0:T(8,128)(2,1)} %get-tuple-element.186), channel_id=1, source_target_pairs={{0,8},{4,12},{8,0},{12,4},{1,9},{5,13},{9,1},{13,5},{2,10},{6,14},... | collective-permute-start | bytes 3932168 | tf_op jit(solution)/shard_map/ppermute | solution.py:304
  342.7 25.2 %collective-permute-start.9 = (bf16[2,160,32,128]{3,2,1,0:T(8,128)(2,1)}, bf16[2,160,32,128]{3,2,1,0:T(8,128)(2,1)}, u32[]{:S(2)}, u32[]{:S(2)}) collective-permute-start(bf16[2,160,32,128]{3,2,1,0:T(8,128)(2,1)} %get-tuple-element.141), channel_id=1, source_target_pairs={{0,4},{4,0},{8,12},{12,8},{1,5},{5,1},{9,13},{13,9},{2,6},{6,2},{1... | collective-permute-start | bytes 7864328 | tf_op jit(solution)/shard_map/ppermute | solution.py:304
  346.4 31.4 %collective-permute-start.10 = (bf16[1,160,32,128]{3,2,1,0:T(8,128)(2,1)}, bf16[1,160,32,128]{3,2,1,0:T(8,128)(2,1)}, u32[]{:S(2)}, u32[]{:S(2)}) collective-permute-start(bf16[1,160,32,128]{3,2,1,0:T(8,128)(2,1)} %get-tuple-element.188), channel_id=1, source_target_pairs={{0,8},{4,12},{8,0},{12,4},{1,9},{5,13},{9,1},{13,5},{2,10},{6,14},... | collective-permute-start | bytes 3932168 | tf_op jit(solution)/shard_map/ppermute | solution.py:304
  440.6 25.5 %collective-permute-start.11 = (bf16[2,160,32,128]{3,2,1,0:T(8,128)(2,1)}, bf16[2,160,32,128]{3,2,1,0:T(8,128)(2,1)}, u32[]{:S(2)}, u32[]{:S(2)}) collective-permute-start(bf16[2,160,32,128]{3,2,1,0:T(8,128)(2,1)} %get-tuple-element.151), channel_id=1, source_target_pairs={{0,4},{4,0},{8,12},{12,8},{1,5},{5,1},{9,13},{13,9},{2,6},{6,2},{1... | collective-permute-start | bytes 7864328 | tf_op jit(solution)/shard_map/ppermute | solution.py:304
  444.3 31.4 %collective-permute-start.12 = (bf16[1,160,32,128]{3,2,1,0:T(8,128)(2,1)}, bf16[1,160,32,128]{3,2,1,0:T(8,128)(2,1)}, u32[]{:S(2)}, u32[]{:S(2)}) collective-permute-start(bf16[1,160,32,128]{3,2,1,0:T(8,128)(2,1)} %get-tuple-element.190), channel_id=1, source_target_pairs={{0,8},{4,12},{8,0},{12,4},{1,9},{5,13},{9,1},{13,5},{2,10},{6,14},... | collective-permute-start | bytes 3932168 | tf_op jit(solution)/shard_map/ppermute | solution.py:304
  477.7 34.7 %collective-permute-start.13 = (bf16[1,160,32,128]{3,2,1,0:T(8,128)(2,1)}, bf16[1,160,32,128]{3,2,1,0:T(8,128)(2,1)}, u32[]{:S(2)}, u32[]{:S(2)}) collective-permute-start(bf16[1,160,32,128]{3,2,1,0:T(8,128)(2,1)} %get-tuple-element.192), channel_id=1, source_target_pairs={{0,8},{4,12},{8,0},{12,4},{1,9},{5,13},{9,1},{13,5},{2,10},{6,14},... | collective-permute-start | bytes 3932168 | tf_op jit(solution)/shard_map/ppermute | solution.py:304
  540.9 11.0 %collective-permute-start.14 = (bf16[2,160,32,128]{3,2,1,0:T(8,128)(2,1)}, bf16[2,160,32,128]{3,2,1,0:T(8,128)(2,1)}, u32[]{:S(2)}, u32[]{:S(2)}) collective-permute-start(bf16[2,160,32,128]{3,2,1,0:T(8,128)(2,1)} %get-tuple-element.162), channel_id=1, source_target_pairs={{0,4},{4,0},{8,12},{12,8},{1,5},{5,1},{9,13},{13,9},{2,6},{6,2},{1... | collective-permute-start | bytes 7864328 | tf_op jit(solution)/shard_map/ppermute | solution.py:304
  557.0 49.6 %collective-permute-start.15 = (bf16[1,160,32,128]{3,2,1,0:T(8,128)(2,1)}, bf16[1,160,32,128]{3,2,1,0:T(8,128)(2,1)}, u32[]{:S(2)}, u32[]{:S(2)}) collective-permute-start(bf16[1,160,32,128]{3,2,1,0:T(8,128)(2,1)} %get-tuple-element.193), channel_id=1, source_target_pairs={{0,8},{4,12},{8,0},{12,4},{1,9},{5,13},{9,1},{13,5},{2,10},{6,14},... | collective-permute-start | bytes 3932168 | tf_op jit(solution)/shard_map/ppermute | solution.py:304
  622.2 7.0 %collective-permute-start.19 = (f32[200,128]{1,0:T(8,128)S(1)}, f32[200,128]{1,0:T(8,128)S(1)}, u32[]{:S(2)}, u32[]{:S(2)}) collective-permute-start(f32[200,128]{1,0:T(8,128)S(1)} %fusion), channel_id=1, source_target_pairs={{0,1},{1,0},{2,3},{3,2},{4,5},{5,4},{6,7},{7,6},{8,9},{9,8},{10,11... | collective-permute-start | bytes 307208 | tf_op jit(solution)/shard_map/ppermute | solution.py:304
  622.3 11.1 %collective-permute-start.20 = (f32[200,128]{1,0:T(8,128)S(1)}, f32[200,128]{1,0:T(8,128)S(1)}, u32[]{:S(2)}, u32[]{:S(2)}) collective-permute-start(f32[200,128]{1,0:T(8,128)S(1)} %fusion), channel_id=1, source_target_pairs={{0,2},{1,3},{2,0},{3,1},{4,6},{5,7},{6,4},{7,5},{8,10},{9,11},{10,... | collective-permute-start | bytes 307208 | tf_op jit(solution)/shard_map/ppermute | solution.py:304
  623.8 9.6 %collective-permute-start.21 = (f32[200,128]{1,0:T(8,128)S(1)}, f32[200,128]{1,0:T(8,128)S(1)}, u32[]{:S(2)}, u32[]{:S(2)}) collective-permute-start(f32[200,128]{1,0:T(8,128)S(1)} %fusion), channel_id=1, source_target_pairs={{0,3},{1,2},{2,1},{3,0},{4,7},{5,6},{6,5},{7,4},{8,11},{9,10},{10,... | collective-permute-start | bytes 307208 | tf_op jit(solution)/shard_map/ppermute | solution.py:304
  (31 other events, 186.1 us)
Sparse Core Ops, SparseCore 0:
  17.4 100.7 all-gather.14
  119.8 96.4 all-gather.12
  217.8 96.4 all-gather.16
  315.7 96.4 all-gather.18
  413.6 96.4 all-gather.10

commit v7 on v5

--- a/solution.py
+++ b/solution.py
@@ -374,10 +374,9 @@
     return jnp.transpose(with_layout_constraint(total, major), (1, 2, 0))
 
 
-def triangles(n, groups, size, a, b_swapped, acc):
+def triangles(n, groups, split, a, b_swapped, acc):
     r = lax.axis_index("row").astype(jnp.int32).reshape(1)
     cols = b_swapped.shape[1]
-    split = 2 * size if cols > 2 * size else cols
     early = chip_slots(b_swapped[:, :split], n)
     late = chip_slots(b_swapped[:, split:], n) if split < cols else []
     a_t = jnp.transpose(a, (2, 0, 1))
@@ -386,42 +385,45 @@
     major = Layout(major_to_minor=(0, 1, 2))
     da, b_t = None, None
     db, spans, terms, pairs = [], [], [], []
-    for group in groups:
-        for at in range(group.shape[2] // size):
-            q = len(spans)
-            off = q * size
-            if q > 0:
-                slots, start = (b_early, off) if off < split else (b_late, off - split)
-                b_t = slots_to_channels(slots, r, start, size)
+    off = 0
+    for q, group in enumerate(groups):
+        size = group.shape[2]
+        if q > 0:
+            slots, start = (b_early, off) if off < split else (b_late, off - split)
+            b_t = slots_to_channels(slots, r, start, size)
+            if pairs:
+                group, da, b_t, db[-1][1] = lax.optimization_barrier((group, da, b_t, db[-1][1]))
+                pairs[-1] = da
+            else:
                 group, da, b_t = lax.optimization_barrier((group, da, b_t))
-                if pairs:
-                    pairs[-1] = da
-                else:
-                    terms[-1] = da
-            dx_t = gathered_to_channels(group, r, at, size)
-            part = jnp.einsum("cik,cij->ckj", a_t, dx_t, preferred_element_type=F32).astype(BF16)
-            kept, sent = from_channels(part, n)
-            if q == 0:
-                dx_t, kept, sent, *early = lax.optimization_barrier((dx_t, kept, sent, *early))
-                b_early = core_slots(early, n)
-                b_t = slots_to_channels(b_early, r, off, size)
-            else:
-                dx_t, kept, sent = lax.optimization_barrier((dx_t, kept, sent))
-            half, come = reduce_cores(kept, sent, n)
-            da = jnp.einsum("cij,ckj->cik", dx_t, b_t, preferred_element_type=F32)
-            da = with_layout_constraint(da.astype(BF16), major)
-            if q == 0:
-                da, half, *late = lax.optimization_barrier((da, half, *late))
-                b_late = core_slots(late, n)
-            else:
-                da, half, db[-1][1] = lax.optimization_barrier((da, half, db[-1][1]))
-            db.append(list(reduce_chips(half, come, n)))
-            spans.append((off, size))
-            terms.append(da)
-            if off + 2 * size == cols:
-                da = to_pairs(terms, major)
-                terms = []
-                pairs.append(da)
+                terms[-1] = da
+        dx_t = gathered_to_channels(group, r, 0, size)
+        part = jnp.einsum("cik,cij->ckj", a_t, dx_t, preferred_element_type=F32).astype(BF16)
+        kept, sent = from_channels(part, n)
+        if q == 0:
+            dx_t, kept, sent, *early = lax.optimization_barrier((dx_t, kept, sent, *early))
+            b_early = core_slots(early, n)
+            b_t = slots_to_channels(b_early, r, off, size)
+        else:
+            dx_t, kept, sent = lax.optimization_barrier((dx_t, kept, sent))
+        half, come = reduce_cores(kept, sent, n)
+        da = jnp.einsum("cij,ckj->cik", dx_t, b_t, preferred_element_type=F32)
+        da = with_layout_constraint(da.astype(BF16), major)
+        if q == 0:
+            da, half, *late = lax.optimization_barrier((da, half, *late))
+            b_late = core_slots(late, n)
+        elif pairs:
+            da, half = lax.optimization_barrier((da, half))
+        else:
+            da, half, db[-1][1] = lax.optimization_barrier((da, half, db[-1][1]))
+        db.append(list(reduce_chips(half, come, n)))
+        spans.append((off, size))
+        terms.append(da)
+        off += size
+        if q == len(groups) - 2:
+            da = to_pairs(terms, major)
+            terms = []
+            pairs.append(da)
     pairs.append(to_pairs(terms, major))
     return pairs, db, spans, acc
 
@@ -429,10 +431,12 @@
 def shards(n_row, n_col, pair, product, mask, grad_out, weights, norms):
     rows, cols, c = pair.shape
     even = n_row == n_col and n_row & (n_row - 1) == 0 and cols % 32 == 0 and rows % 16 == 0
-    size = 32 if even else cols
-    widths = [size] * (cols // size)
-    if len(widths) > 3:
-        widths[1:3] = [2 * size]
+    if not even:
+        widths, split = [cols], cols
+    elif cols % 160 == 0:
+        widths, split = [3 * cols // 10] * 2 + [cols // 5] * 2, 3 * cols // 5
+    else:
+        widths, split = [32] * (cols // 32), min(64, cols)
     groups, chain, off = [], [], 0
     for width in widths:
         dx, *chain = dx_chunk(pair, product, grad_out, weights, norms, off, width, chain)
@@ -444,7 +448,7 @@
         off += width
     dol, acc = chain
     if even:
-        da, db, spans, acc = triangles(n_row, groups, size, a, b_swapped, acc)
+        da, db, spans, acc = triangles(n_row, groups, split, a, b_swapped, acc)
     else:
         da, db, spans = triangles_plain(n_row, n_col, groups[0], a, b_swapped)
     da = da if len(da) == 2 else [da[0], jnp.zeros_like(da[0])]

time: 690 us -> 656 us (0.951)
  matrix products: 110 us -> 90.6 us
  other arithmetic: 44.3 us -> 32.6 us
    ppermute x25 -> x23, waiting for transfers between devices: 68.4 us -> 82.9 us  [swap(): return lax.ppermute(v, axis, [(r, r ^ bit) for r in range(n)])]
    all_gather x4, waiting for transfers between devices: 111 us -> 96.7 us  [shards(): groups.append(lax.all_gather(dx, 'col', axis=0) if even else dx)]
    dot_general x5 -> x4, matrix products: 55.6 us -> 46.1 us  [triangles(): da = jnp.einsum('cij,ckj->cik', dx_t, b_t, preferred_element_type=F32)]
    dot_general x5 -> x4, matrix products: 53.9 us -> 44.5 us  [triangles(): jnp.einsum('cik,cij->ckj', a_t, dx_t, preferred_element_type=F32)]
    convert_element_type x5 -> x4, other arithmetic: 22.2 us -> 16.1 us  [reduce_cores(): return ((kept.astype(F32) + come.astype(F32)).astype(BF16), None)]
    pallas_call x10 -> x8, Pallas kernels: 81.6 us -> 87.2 us  [to_channels(): pl.pallas_call(functools.partial(to_channels_kernel, slots), grid_spec=pl...]
    pallas_call x5 -> x4, Pallas kernels: 41.9 us -> 38.1 us  [from_channels(): pl.pallas_call(functools.partial(from_channels_kernel, slots), grid=(lead...]
    pallas_call x5 -> x4, Pallas kernels: 43.1 us -> 40 us  [final_chunk(): pl.pallas_call(functools.partial(final_kernel, step, bool(chain)), grid=(...]
  transfers between devices with their start and end apart: 29 -> 27, of which waited for: 15 -> 14; matrix products, arithmetic and copies ran while one was open for 31% -> 27% of each run, Pallas kernels for 29% -> 30%
where the time goes in v7:
time: 656 us; the launch traced here: 648 us
  Pallas kernels  229 us (35%)
  waiting for transfers between devices  180 us (27%)
  matrix products  90.6 us (14%)
  local copies, waits for them, and re-layouts  82.1 us (13%)
  other arithmetic  32.6 us (5%)
  starting transfers between devices  20 us (3%)
  between operations  14.3 us (2%)
    all_gather x4, waiting for transfers between devices, shards(): groups.append(lax.all_gather(dx, 'col', axis=0) if even else dx)  96.7 us
    pallas_call x8, Pallas kernels, to_channels(): pl.pallas_call(functools.partial(to_channels_kernel, slots), grid_spec=pl...  87.2 us
    ppermute x23, waiting for transfers between devices, swap(): return lax.ppermute(v, axis, [(r, r ^ bit) for r in range(n)])  82.9 us
    dot_general x4, matrix products, triangles(): da = jnp.einsum('cij,ckj->cik', dx_t, b_t, preferred_element_type=F32)  46.1 us
    dot_general x4, matrix products, triangles(): jnp.einsum('cik,cij->ckj', a_t, dx_t, preferred_element_type=F32)  44.5 us
    pallas_call x4, Pallas kernels, dx_chunk(): pl.pallas_call(functools.partial(dx_kernel, step, bool(chain)), grid=(row...  40.2 us
    pallas_call x4, Pallas kernels, final_chunk(): pl.pallas_call(functools.partial(final_kernel, step, bool(chain)), grid=(...  40 us
    pallas_call x4, Pallas kernels, from_channels(): pl.pallas_call(functools.partial(from_channels_kernel, slots), grid=(lead...  38.1 us
  transfers between devices with their start and end apart: 27, of which 14 were waited for; matrix products, arithmetic and copies ran while one was open for 27% of the time, Pallas kernels for 30%

profile of v7, /device:TPU:0, one launch (start us, length us, event | category | flops | bytes accessed | tf_op | source)
XLA Modules:
  0.0 648.4 jit_solution(15180358802098094986)
XLA Ops:
  8.8 11.6 %dx_part.4 = (bf16[160,48,128]{2,1,0:T(8,128)(2,1)}, bf16[160,160,128]{2,1,0:T(8,128)(2,1)}, f32[800,128]{1,0:T(8,128)S(1)}) custom-call(bf16[160,160,128]{2,1,0:T(8,128)(2,1)} %pair.17, bf16[160,160,128]{2,1,0:T(8,128)(2,1)} %product.7, bf16[160,160,128]{2,1,0:T(8,128)(2,1)} %go.7, bf16[6,128,128]{2,1,0:T(8,128)(2,1)S(1)} %copy-done.4, f32[4,128]{1,0:T(4,128)S(1)} %copy-done.19), custom_call_target="tpu_custom_call" | custom-call | flops 1006632960 | bytes 9830400 | tf_op jit(solution)/shard_map/dx_part/pallas_call | solution.py:104
  26.8 23.7 %projections.1 = (bf16[160,160,128]{2,1,0:T(8,128)(2,1)}, bf16[160,160,128]{2,1,0:T(8,128)(2,1)}, bf16[160,160,128]{2,1,0:T(8,128)(2,1)}, bf16[160,160,128]{2,1,...) custom-call(bf16[160,160,128]{2,1,0:T(8,128)(2,1)} %pair.17, ...), custom_call_target="tpu_custom_call" | custom-call | flops 3355443200 | bytes 52428800 | tf_op jit(solution)/shard_map/projections/pallas_call | solution.py:157
  50.5 11.7 %dx_part.5 = (bf16[160,48,128]{2,1,0:T(8,128)(2,1)}, bf16[160,160,128]{2,1,0:T(8,128)(2,1)}, f32[800,128]{1,0:T(8,128)S(1)}) custom-call(bf16[160,160,128]{2,1,0:T(8,128)(2,1)} %pair.17, bf16[160,160,128]{2,1,0:T(8,128)(2,1)} %product.7, bf16[160,160,128]{2,1,0:T(8,128)(2,1)} %go.7, ...), custom_call_target="tpu_custom_call", output_to_operand_aliasing={{1}: (5, {})} | custom-call | flops 1006632960 | bytes 9830400 | tf_op jit(solution)/shard_map/dx_part/pallas_call | solution.py:104
  89.0 75.5 %all-gather.13.cloned.1.call-done = bf16[640,48,128]{2,1,0:T(8,128)(2,1)} async-done(((bf16[160,48,128]{2,1,0:T(8,128)(2,1)}), bf16[640,48,128]{2,1,0:T(8,128)(2,1)}) %all-gather.13.cloned.1.call-update) | async-done | bytes 7864336 | tf_op jit(solution)/shard_map/all_gather | solution.py:443
  164.4 15.9 %copy.33 = bf16[128,160,160]{1,2,0:T(8,128)(2,1)} copy(bf16[128,160,160]{0,2,1:T(8,128)(2,1)} %bitcast.108) | data formatting | bytes 13107200 | tf_op jit(solution)/shard_map/optimization_barrier | solution.py:383
  180.3 13.9 %to_channels.8 = bf16[128,160,192]{2,1,0:T(8,128)(2,1)} custom-call(s32[1]{0:T(128)} %bitcast.2.r, bf16[4,160,48,128]{3,2,1,0:T(8,128)(2,1)} %bitcast.92, bf16[4,160,48,128]{3,2,1,0:T(8,128)(2,1)} %bitcast.93, bf16[4,160,48,128]{3,2,1,0:T(8,128)(2,1)} %bitcast.94, bf16[4,160,48,128]{3,2,1,0:T(8,128)(2,1)} %bitcast.95), custom_call_target="tpu_custom_call" | custom-call | flops 15728640 | bytes 15728640 | tf_op jit(solution)/shard_map/to_channels/pallas_call | solution.py:183
  230.5 13.4 %to_channels.9 = bf16[128,160,192]{2,1,0:T(8,128)(2,1)} custom-call(s32[1]{0:T(128)} %bitcast.2.r, bf16[160,96,128]{2,1,0:T(8,128)(2,1)} %slice.42.refs_0_, bf16[160,96,128]{2,1,0:T(8,128)(2,1)} %collective-permute-done.1.refs_1_, bf16[160,96,128]{2,1,0:T(8,128)(2,1)} %collective-permute-done.refs_2_, bf16[160,96,128]{2,1,0:T(8,128)(2,1)} %collective-permute-done.2.refs_3_), custom_call_target="tpu_custom_call" | custom-call | flops 15728640 | bytes 15728640 | tf_op jit(solution)/shard_map/to_channels/pallas_call | solution.py:183
  249.0 12.1 %convolution_convert_fusion.4 = bf16[128,160,160]{2,1,0:T(8,128)(2,1)} fusion(bf16[128,160,192]{2,1,0:T(8,128)(2,1)} %to_channels.8, bf16[128,160,192]{2,1,0:T(8,128)(2,1)} %to_channels.9), kind=kOutput, calls=%fused_computation.7 | convolution fusion | flops 1261568000 | bytes 22282240 | tf_op jit(solution)/shard_map/cij,ckj->cik/dot_general | solution.py:410
  261.1 19.6 %collective-permute-done.4.refs_2_ = bf16[160,64,128]{2,1,0:T(8,128)(2,1)} collective-permute-done((bf16[160,64,128]{2,1,0:T(8,128)(2,1)S(1)}, bf16[160,64,128]{2,1,0:T(8,128)(2,1)}, u32[]{:S(2)}, u32[]{:S(2)}) %collective-permute-start.4) | collective-permute-done | bytes 2621472 | tf_op jit(solution)/shard_map/ppermute | solution.py:304
  280.7 13.2 %to_channels.10 = bf16[128,160,192]{2,1,0:T(8,128)(2,1)} custom-call(s32[1]{0:T(128)} %bitcast.2.r, bf16[160,96,128]{2,1,0:T(8,128)(2,1)} %slice.42.refs_0_, bf16[160,96,128]{2,1,0:T(8,128)(2,1)} %collective-permute-done.1.refs_1_, bf16[160,96,128]{2,1,0:T(8,128)(2,1)} %collective-permute-done.refs_2_, bf16[160,96,128]{2,1,0:T(8,128)(2,1)} %collective-permute-done.2.refs_3_), custom_call_target="tpu_custom_call" | custom-call | flops 15728640 | bytes 15728640 | tf_op jit(solution)/shard_map/to_channels/pallas_call | solution.py:183
  293.9 11.4 %all-gather.11.cloned.1.call-done = bf16[640,48,128]{2,1,0:T(8,128)(2,1)} async-done(((bf16[160,48,128]{2,1,0:T(8,128)(2,1)}), bf16[640,48,128]{2,1,0:T(8,128)(2,1)}) %all-gather.11.cloned.1.call-update) | async-done | bytes 7864336 | tf_op jit(solution)/shard_map/all_gather | solution.py:443
  305.3 13.5 %to_channels.11 = bf16[128,160,192]{2,1,0:T(8,128)(2,1)} custom-call(s32[1]{0:T(128)} %bitcast.2.r, bf16[4,160,48,128]{3,2,1,0:T(8,128)(2,1)} %bitcast.88, bf16[4,160,48,128]{3,2,1,0:T(8,128)(2,1)} %bitcast.89, bf16[4,160,48,128]{3,2,1,0:T(8,128)(2,1)} %bitcast.90, bf16[4,160,48,128]{3,2,1,0:T(8,128)(2,1)} %bitcast.91), custom_call_target="tpu_custom_call" | custom-call | flops 15728640 | bytes 15728640 | tf_op jit(solution)/shard_map/to_channels/pallas_call | solution.py:183
  318.8 11.2 %convolution_convert_fusion.3.x = bf16[128,160,192]{2,1,0:T(8,128)(2,1)} fusion(bf16[128,160,160]{1,2,0:T(8,128)(2,1)} %copy.33, bf16[128,160,192]{2,1,0:T(8,128)(2,1)} %to_channels.11), kind=kOutput, calls=%fused_computation.6 | convolution fusion | flops 1262223360 | bytes 22282240 | tf_op jit(solution)/shard_map/cik,cij->ckj/dot_general | solution.py:401
  349.3 12.1 %convolution_convert_fusion.2 = bf16[128,160,160]{2,1,0:T(8,128)(2,1)} fusion(bf16[128,160,192]{2,1,0:T(8,128)(2,1)} %to_channels.11, bf16[128,160,192]{2,1,0:T(8,128)(2,1)} %to_channels.10), kind=kOutput, calls=%fused_computation.5 | convolution fusion | flops 1261568000 | bytes 22282240 | tf_op jit(solution)/shard_map/cij,ckj->cik/dot_general | solution.py:410
  375.8 17.6 %collective-permute-done.6 = bf16[1,160,48,128]{3,2,1,0:T(8,128)(2,1)} collective-permute-done((bf16[1,160,48,128]{3,2,1,0:T(8,128)(2,1)}, bf16[1,160,48,128]{3,2,1,0:T(8,128)(2,1)}, u32[]{:S(2)}, u32[]{:S(2)}) %collective-permute-start.6) | collective-permute-done | bytes 1966112 | tf_op jit(solution)/shard_map/ppermute | solution.py:304
  410.6 11.4 %convolution_convert_fusion.7.x = bf16[128,160,128]{2,1,0:T(8,128)(2,1)} fusion(bf16[128,160,160]{1,2,0:T(8,128)(2,1)} %copy.33, bf16[128,160,128]{2,1,0:T(8,128)(2,1)S(1)} %to_channels.13), kind=kOutput, calls=%fused_computation.12 | convolution fusion | flops 841482240 | bytes 17039360 | tf_op jit(solution)/shard_map/cik,cij->ckj/dot_general | solution.py:401
  446.4 11.0 %convolution_convert_fusion.1 = bf16[128,160,160]{2,1,0:T(8,128)(2,1)} fusion(bf16[128,160,128]{2,1,0:T(8,128)(2,1)} %copy-done, bf16[128,160,128]{2,1,0:T(8,128)(2,1)} %to_channels.12), kind=kOutput, calls=%fused_computation.4 | convolution fusion | flops 842137600 | bytes 17039360 | tf_op jit(solution)/shard_map/cij,ckj->cik/dot_general | solution.py:410
  460.0 21.1 %collective-permute-done.10 = bf16[1,160,48,128]{3,2,1,0:T(8,128)(2,1)} collective-permute-done((bf16[1,160,48,128]{3,2,1,0:T(8,128)(2,1)}, bf16[1,160,48,128]{3,2,1,0:T(8,128)(2,1)}, u32[]{:S(2)}, u32[]{:S(2)}) %collective-permute-start.10) | collective-permute-done | bytes 1966112 | tf_op jit(solution)/shard_map/ppermute | solution.py:304
  484.1 15.6 %add_convert_fusion = bf16[128,160,160]{2,1,0:T(8,128)(2,1)} fusion(bf16[128,160,160]{2,1,0:T(8,128)(2,1)S(1)} %copy-done.23, bf16[128,160,160]{2,1,0:T(8,128)(2,1)} %convolution_convert_fusion.2, bf16[128,160,160]{2,1,0:T(8,128)(2,1)} %convolution_convert_fusion.4), kind=kLoop, calls=%fused_computation | loop fusion | flops 19660800 | bytes 26214400 | tf_op jit(solution)/shard_map/convert_element_type | solution.py:373
  499.7 14.1 %copy.36 = bf16[128,160,160]{0,2,1:T(8,128)(2,1)} copy(bf16[128,160,160]{2,1,0:T(8,128)(2,1)} %add_convert_fusion) | data formatting | bytes 13107200 | tf_op jit(solution)/shard_map/layout_constraint | solution.py:374
  521.7 11.1 %convolution_convert_fusion.6.x = bf16[128,160,128]{2,1,0:T(8,128)(2,1)} fusion(bf16[128,160,160]{1,2,0:T(8,128)(2,1)} %copy.33, bf16[128,160,128]{2,1,0:T(8,128)(2,1)S(1)} %to_channels.15), kind=kOutput, calls=%fused_computation.11 | convolution fusion | flops 841482240 | bytes 17039360 | tf_op jit(solution)/shard_map/cik,cij->ckj/dot_general | solution.py:401
  559.4 14.2 %copy.38 = bf16[128,160,160]{0,2,1:T(8,128)(2,1)} copy(bf16[128,160,160]{2,1,0:T(8,128)(2,1)} %convolution_convert_fusion) | data formatting | bytes 13107200 | tf_op jit(solution)/shard_map/layout_constraint | solution.py:374
  574.6 11.4 %final_part.4 = (bf16[160,160,128]{2,1,0:T(8,128)(2,1)}, f32[800,128]{1,0:T(8,128)S(1)}) custom-call(bf16[160,160,128]{2,1,0:T(8,128)(2,1)} %pair.17, bf16[160,160,128]{2,1,0:T(8,128)(2,1)} %bitcast.80, bf16[160,160,128]{2,1,0:T(8,128)(2,1)} %bitcast.84, bf16[160,48,128]{2,1,0:T(8,128)(2,1)S(1)} %copy-done.2, bf16[160,48,128]{2,1,0:T(8,128)(2,1)} %bitcast.8.db1, ...), custom_call_target="tpu_custom_call" | custom-call | flops 2516582400 | bytes 21626880 | tf_op jit(solution)/shard_map/final_part/pallas_call | solution.py:281
  586.1 11.6 %final_part.5 = (bf16[160,160,128]{2,1,0:T(8,128)(2,1)}, f32[800,128]{1,0:T(8,128)S(1)}) custom-call(bf16[160,160,128]{2,1,0:T(8,128)(2,1)} %pair.17, bf16[160,160,128]{2,1,0:T(8,128)(2,1)} %bitcast.81, bf16[160,160,128]{2,1,0:T(8,128)(2,1)} %bitcast.85, bf16[160,48,128]{2,1,0:T(8,128)(2,1)S(1)} %copy-done.3, ...), custom_call_target="tpu_custom_call", output_to_operand_aliasing={{0}: (13, {})} | custom-call | flops 2516582400 | bytes 21626880 | tf_op jit(solution)/shard_map/final_part/pallas_call | solution.py:281
  (140 shorter events, 236.1 us)
Async XLA Ops:
  7.2 157.2 %all-gather.13.cloned.1.call-start = ((), (), s32[]{:S(2)}) async-start(), calls=%async_computation.2 | async-start | bytes 9830400 | tf_op jit(solution)/shard_map/all_gather | solution.py:443
  20.5 284.8 %all-gather.11.cloned.1.call-start = ((), (), s32[]{:S(2)}) async-start(), calls=%async_computation.1 | async-start | bytes 9830400 | tf_op jit(solution)/shard_map/all_gather | solution.py:443
  62.3 340.9 %all-gather.15.cloned.1.call-start = ((), (), s32[]{:S(2)}) async-start(), calls=%async_computation.3 | async-start | bytes 6553600 | tf_op jit(solution)/shard_map/all_gather | solution.py:443
  67.4 150.4 %collective-permute-start = (bf16[160,96,128]{2,1,0:T(8,128)(2,1)}, bf16[160,96,128]{2,1,0:T(8,128)(2,1)}, u32[]{:S(2)}, u32[]{:S(2)}) collective-permute-start(bf16[160,96,128]{2,1,0:T(8,128)(2,1)} %slice.42.refs_0_), channel_id=1, source_target_pairs={{0,8},{4,12},{8,0},{12,4},{1,9},{5,13},{9,1},{13,5},{2,10},{6,14},... | collective-permute-start | bytes 11796488 | tf_op jit(solution)/shard_map/ppermute | solution.py:304
  217.8 7.1 %collective-permute-start.1 = (bf16[160,96,128]{2,1,0:T(8,128)(2,1)}, bf16[160,96,128]{2,1,0:T(8,128)(2,1)}, u32[]{:S(2)}, u32[]{:S(2)}) collective-permute-start(bf16[160,96,128]{2,1,0:T(8,128)(2,1)} %slice.42.refs_0_), channel_id=1, source_target_pairs={{0,4},{4,0},{8,12},{12,8},{1,5},{5,1},{9,13},{13,9},{2,6},{6,2},{1... | collective-permute-start | bytes 11796488 | tf_op jit(solution)/shard_map/ppermute | solution.py:304
  217.9 12.7 %collective-permute-start.2 = (bf16[160,96,128]{2,1,0:T(8,128)(2,1)}, bf16[160,96,128]{2,1,0:T(8,128)(2,1)}, u32[]{:S(2)}, u32[]{:S(2)}) collective-permute-start(bf16[160,96,128]{2,1,0:T(8,128)(2,1)} %collective-permute-done.refs_2_), channel_id=1, source_target_pairs={{0,4},{4,0},{8,12},{12,8},{1,5},{5,1},{9,13},{13,9},{2,6},{6,2},{1... | collective-permute-start | bytes 11796488 | tf_op jit(solution)/shard_map/ppermute | solution.py:304
  218.3 25.6 %collective-permute-start.3 = (bf16[2,160,48,128]{3,2,1,0:T(8,128)(2,1)}, bf16[2,160,48,128]{3,2,1,0:T(8,128)(2,1)}, u32[]{:S(2)}, u32[]{:S(2)}) collective-permute-start(bf16[2,160,48,128]{3,2,1,0:T(8,128)(2,1)} %get-tuple-element.100), channel_id=1, source_target_pairs={{0,4},{4,0},{8,12},{12,8},{1,5},{5,1},{9,13},{13,9},{2,6},{6,2},{1... | collective-permute-start | bytes 11796488 | tf_op jit(solution)/shard_map/ppermute | solution.py:304
  218.4 295.4 %all-gather.9.cloned.1.call-start = ((), (), s32[]{:S(2)}) async-start(), calls=%async_computation | async-start | bytes 6553600 | tf_op jit(solution)/shard_map/all_gather | solution.py:443
  221.3 59.4 %collective-permute-start.4 = (bf16[160,64,128]{2,1,0:T(8,128)(2,1)S(1)}, bf16[160,64,128]{2,1,0:T(8,128)(2,1)}, u32[]{:S(2)}, u32[]{:S(2)}) collective-permute-start(bf16[160,64,128]{2,1,0:T(8,128)(2,1)S(1)} %slice.43.refs_0_), channel_id=1, source_target_pairs={{0,8},{4,12},{8,0},{12,4},{1,9},{5,13},{9,1},{13,5},{2,10},{6,14},... | collective-permute-start | bytes 7864328 | tf_op jit(solution)/shard_map/ppermute | solution.py:304
  342.6 28.0 %collective-permute-start.5 = (bf16[2,160,48,128]{3,2,1,0:T(8,128)(2,1)}, bf16[2,160,48,128]{3,2,1,0:T(8,128)(2,1)}, u32[]{:S(2)}, u32[]{:S(2)}) collective-permute-start(bf16[2,160,48,128]{3,2,1,0:T(8,128)(2,1)} %get-tuple-element.110), channel_id=1, source_target_pairs={{0,4},{4,0},{8,12},{12,8},{1,5},{5,1},{9,13},{13,9},{2,6},{6,2},{1... | collective-permute-start | bytes 11796488 | tf_op jit(solution)/shard_map/ppermute | solution.py:304
  342.6 18.8 %collective-permute-start.7 = (bf16[160,64,128]{2,1,0:T(8,128)(2,1)S(1)}, bf16[160,64,128]{2,1,0:T(8,128)(2,1)}, u32[]{:S(2)}, u32[]{:S(2)}) collective-permute-start(bf16[160,64,128]{2,1,0:T(8,128)(2,1)S(1)} %slice.43.refs_0_), channel_id=1, source_target_pairs={{0,4},{4,0},{8,12},{12,8},{1,5},{5,1},{9,13},{13,9},{2,6},{6,2},{1... | collective-permute-start | bytes 7864328 | tf_op jit(solution)/shard_map/ppermute | solution.py:304
  343.1 18.4 %collective-permute-start.8 = (bf16[160,64,128]{2,1,0:T(8,128)(2,1)}, bf16[160,64,128]{2,1,0:T(8,128)(2,1)}, u32[]{:S(2)}, u32[]{:S(2)}) collective-permute-start(bf16[160,64,128]{2,1,0:T(8,128)(2,1)} %collective-permute-done.4.refs_2_), channel_id=1, source_target_pairs={{0,4},{4,0},{8,12},{12,8},{1,5},{5,1},{9,13},{13,9},{2,6},{6,2},{1... | collective-permute-start | bytes 7864328 | tf_op jit(solution)/shard_map/ppermute | solution.py:304
  347.9 45.5 %collective-permute-start.6 = (bf16[1,160,48,128]{3,2,1,0:T(8,128)(2,1)}, bf16[1,160,48,128]{3,2,1,0:T(8,128)(2,1)}, u32[]{:S(2)}, u32[]{:S(2)}) collective-permute-start(bf16[1,160,48,128]{3,2,1,0:T(8,128)(2,1)} %get-tuple-element.154), channel_id=1, source_target_pairs={{0,8},{4,12},{8,0},{12,4},{1,9},{5,13},{9,1},{13,5},{2,10},{6,14},... | collective-permute-start | bytes 5898248 | tf_op jit(solution)/shard_map/ppermute | solution.py:304
  430.3 27.1 %collective-permute-start.9 = (bf16[2,160,32,128]{3,2,1,0:T(8,128)(2,1)}, bf16[2,160,32,128]{3,2,1,0:T(8,128)(2,1)}, u32[]{:S(2)}, u32[]{:S(2)}) collective-permute-start(bf16[2,160,32,128]{3,2,1,0:T(8,128)(2,1)} %get-tuple-element.122), channel_id=1, source_target_pairs={{0,4},{4,0},{8,12},{12,8},{1,5},{5,1},{9,13},{13,9},{2,6},{6,2},{1... | collective-permute-start | bytes 7864328 | tf_op jit(solution)/shard_map/ppermute | solution.py:304
  436.0 45.1 %collective-permute-start.10 = (bf16[1,160,48,128]{3,2,1,0:T(8,128)(2,1)}, bf16[1,160,48,128]{3,2,1,0:T(8,128)(2,1)}, u32[]{:S(2)}, u32[]{:S(2)}) collective-permute-start(bf16[1,160,48,128]{3,2,1,0:T(8,128)(2,1)} %get-tuple-element.156), channel_id=1, source_target_pairs={{0,8},{4,12},{8,0},{12,4},{1,9},{5,13},{9,1},{13,5},{2,10},{6,14},... | collective-permute-start | bytes 5898248 | tf_op jit(solution)/shard_map/ppermute | solution.py:304
  482.6 31.2 %collective-permute-start.11 = (bf16[1,160,32,128]{3,2,1,0:T(8,128)(2,1)}, bf16[1,160,32,128]{3,2,1,0:T(8,128)(2,1)S(1)}, u32[]{:S(2)}, u32[]{:S(2)}) collective-permute-start(bf16[1,160,32,128]{3,2,1,0:T(8,128)(2,1)} %get-tuple-element.158), channel_id=1, source_target_pairs={{0,8},{4,12},{8,0},{12,4},{1,9},{5,13},{9,1},{13,5},{2,10},{6,14},... | collective-permute-start | bytes 3932168 | tf_op jit(solution)/shard_map/ppermute | solution.py:304
  542.5 10.8 %collective-permute-start.12 = (bf16[2,160,32,128]{3,2,1,0:T(8,128)(2,1)}, bf16[2,160,32,128]{3,2,1,0:T(8,128)(2,1)}, u32[]{:S(2)}, u32[]{:S(2)}) collective-permute-start(bf16[2,160,32,128]{3,2,1,0:T(8,128)(2,1)} %get-tuple-element.133), channel_id=1, source_target_pairs={{0,4},{4,0},{8,12},{12,8},{1,5},{5,1},{9,13},{13,9},{2,6},{6,2},{1... | collective-permute-start | bytes 7864328 | tf_op jit(solution)/shard_map/ppermute | solution.py:304
  558.5 47.6 %collective-permute-start.13 = (bf16[1,160,32,128]{3,2,1,0:T(8,128)(2,1)}, bf16[1,160,32,128]{3,2,1,0:T(8,128)(2,1)}, u32[]{:S(2)}, u32[]{:S(2)}) collective-permute-start(bf16[1,160,32,128]{3,2,1,0:T(8,128)(2,1)} %get-tuple-element.159), channel_id=1, source_target_pairs={{0,8},{4,12},{8,0},{12,4},{1,9},{5,13},{9,1},{13,5},{2,10},{6,14},... | collective-permute-start | bytes 3932168 | tf_op jit(solution)/shard_map/ppermute | solution.py:304
  615.0 5.6 collective-permute-start.15
  621.7 6.9 %collective-permute-start.17 = (f32[200,128]{1,0:T(8,128)S(1)}, f32[200,128]{1,0:T(8,128)S(1)}, u32[]{:S(2)}, u32[]{:S(2)}) collective-permute-start(f32[200,128]{1,0:T(8,128)S(1)} %fusion), channel_id=1, source_target_pairs={{0,1},{1,0},{2,3},{3,2},{4,5},{5,4},{6,7},{7,6},{8,9},{9,8},{10,11... | collective-permute-start | bytes 307208 | tf_op jit(solution)/shard_map/ppermute | solution.py:304
  621.8 11.1 %collective-permute-start.18 = (f32[200,128]{1,0:T(8,128)S(1)}, f32[200,128]{1,0:T(8,128)S(1)}, u32[]{:S(2)}, u32[]{:S(2)}) collective-permute-start(f32[200,128]{1,0:T(8,128)S(1)} %fusion), channel_id=1, source_target_pairs={{0,2},{1,3},{2,0},{3,1},{4,6},{5,7},{6,4},{7,5},{8,10},{9,11},{10,... | collective-permute-start | bytes 307208 | tf_op jit(solution)/shard_map/ppermute | solution.py:304
  623.5 9.5 %collective-permute-start.19 = (f32[200,128]{1,0:T(8,128)S(1)}, f32[200,128]{1,0:T(8,128)S(1)}, u32[]{:S(2)}, u32[]{:S(2)}) collective-permute-start(f32[200,128]{1,0:T(8,128)S(1)} %fusion), channel_id=1, source_target_pairs={{0,3},{1,2},{2,1},{3,0},{4,7},{5,6},{6,5},{7,4},{8,11},{9,10},{10,... | collective-permute-start | bytes 307208 | tf_op jit(solution)/shard_map/ppermute | solution.py:304
  633.1 5.7 collective-permute-start.21
  634.6 5.5 collective-permute-start.22
  (29 other events, 242.3 us)
Sparse Core Ops, SparseCore 0:
  20.6 143.7 all-gather.12
  166.0 139.2 all-gather.10
  306.9 96.2 all-gather.14
  404.6 96.4 all-gather.8
